TPU v7x, 32 devices: a whole 2x2x4 slice. The times are simulated.
32 devices in a mesh: dp: 4 (over y, x), ctx: 8 (over z, core).
Axes of the slice: x: 2, y: 2, z: 4, core: 2. Of those that a mesh axis runs over, the one named last changes fastest.
Arguments:
- inputs: bfloat16 [4, 8, 128, 4096], P('dp', 'ctx'), may hold values from -6 to 6
- queries: bfloat16 [4, 8, 128, 1024], P('dp', 'ctx'), may hold values from -6 to 6
- keys_values: bfloat16 [4, 8, 128, 256], P('dp', 'ctx'), may hold values from -6 to 6
- out_grad: bfloat16 [4, 8, 128, 1024], P('dp', 'ctx'), may hold values from -6 to 6
- lengths: int32 [4, 10], P('dp'), may hold values from 1 to 256, 1024 in all within a row
Outputs:
- grad_q: bfloat16 [4, 8, 128, 1024], P('dp', 'ctx')
- grad_kv: bfloat16 [4, 8, 128, 256], P('dp', 'ctx')
- grad_kv_weight: float32 [4096, 256], P('ctx')
All inputs are finite; a program needn't handle non-finite values.
Results may differ from a plain program's by a relative error of at most 0.0052.
Values may be sent and summed in bfloat16 or wider, within the bound.
No kernel may reach another device: no remote copies, remote signals or barrier semaphores. Data moves between devices by JAX's collectives and lax.ppermute only.
A program may use at most 64 MiB of HBM per device.

v0:
```python
import jax
import jax.numpy as jnp
from jax import lax
from jax.sharding import PartitionSpec as P

HD = 128
RESPONSES = 4


neg_fill = -1e30


def from_behind(x, axis, by):
    length = lax.axis_size(axis)
    return lax.ppermute(x, axis, [(i, (i + by) % length) for i in range(length)])


def piece_of(positions, piece_ends):
    return jnp.sum((positions[:, None] >= piece_ends[None, :]).astype(jnp.int32), axis=1)


def allowed_pairs(query_pos, key_pos, piece_ends):
    per_group = RESPONSES + 1
    query_piece = piece_of(query_pos, piece_ends)
    key_piece = piece_of(key_pos, piece_ends)
    same_group = (query_piece // per_group)[:, None] == (key_piece // per_group)[None, :]
    visible = (key_piece % per_group == 0)[None, :] | (query_piece[:, None] == key_piece[None, :])
    return (key_pos[None, :] <= query_pos[:, None]) & same_group & visible


def contract_rows(left_side, right_side):
    return lax.dot_general(
        left_side, right_side, (((0,), (0,)), ((), ())), preferred_element_type=jnp.float32
    )


def on_device(inputs, queries, keys_values, out_grad, lengths):
    stripe_count = lax.axis_size("ctx")
    my_stripe = lax.axis_index("ctx")
    local_count = queries.shape[2]
    q_width = queries.shape[3]
    head_count = q_width // HD
    row_total = local_count * head_count
    score_scale = HD ** (-0.5)
    x_local = inputs[0, 0]
    q_rows = queries[0, 0].reshape(row_total, HD)
    grad_rows = out_grad[0, 0].reshape(row_total, HD)
    kv_local = keys_values[0, 0]
    piece_ends = jnp.cumsum(lengths[0], dtype=jnp.int32)
    query_pos = jnp.arange(local_count, dtype=jnp.int32) * stripe_count + my_stripe

    def row_mask(key_pos):
        key_count = key_pos.shape[0]
        allowed = allowed_pairs(query_pos, key_pos, piece_ends)
        return jnp.broadcast_to(allowed[:, None, :], (local_count, head_count, key_count)).reshape(
            row_total, key_count
        )

    def gathered_pos(first_row, row_count):
        key_rows = first_row + jnp.arange(row_count, dtype=jnp.int32)
        return key_rows % local_count * stripe_count + key_rows // local_count

    def forward_block(carried, kv_block, key_pos):
        running_max, running_sum, weighted = carried
        allowed = row_mask(key_pos)
        scores = (
            jnp.dot(q_rows, kv_block[:, :HD].T, preferred_element_type=jnp.float32) * score_scale
        )
        prob_grad = jnp.dot(grad_rows, kv_block[:, HD:].T, preferred_element_type=jnp.float32)
        new_max = jnp.maximum(running_max, jnp.max(jnp.where(allowed, scores, neg_fill), axis=1))
        factor = jnp.exp(running_max - new_max)
        expo_terms = jnp.where(allowed, jnp.exp(scores - new_max[:, None]), 0.0)
        new_sum = running_sum * factor + jnp.sum(expo_terms, axis=1)
        new_weighted = weighted * factor + jnp.sum(expo_terms * prob_grad, axis=1)
        return (new_max, new_sum, new_weighted)

    init_state = (
        jnp.full((row_total,), neg_fill, jnp.float32),
        jnp.zeros((row_total,), jnp.float32),
        jnp.zeros((row_total,), jnp.float32),
    )
    carried = init_state
    kv_piece = lax.all_gather(kv_local, "ctx", axis=0, tiled=True)
    row_count = kv_piece.shape[0]
    sub_blocks = kv_piece.reshape(row_count // 512, 512, kv_piece.shape[1])

    def inner_step(state_now, sub_item):
        sub_block, sub_index = sub_item
        return (forward_block(state_now, sub_block, gathered_pos(sub_index * 512, 512)), None)

    carried, unused = lax.scan(
        inner_step, carried, (sub_blocks, jnp.arange(row_count // 512, dtype=jnp.int32))
    )
    running_max, running_sum, weighted = carried
    log_total = running_max + jnp.log(running_sum)
    row_delta = weighted / running_sum

    def backward_block(grad_q, kv_block, key_pos):
        allowed = row_mask(key_pos)
        scores = (
            jnp.dot(q_rows, kv_block[:, :HD].T, preferred_element_type=jnp.float32) * score_scale
        )
        soft_probs = jnp.where(allowed, jnp.exp(scores - log_total[:, None]), 0.0)
        prob_grad = jnp.dot(grad_rows, kv_block[:, HD:].T, preferred_element_type=jnp.float32)
        score_grad = soft_probs * (prob_grad - row_delta[:, None])
        low_probs = soft_probs.astype(jnp.bfloat16)
        low_score = score_grad.astype(jnp.bfloat16)
        grad_q = (
            grad_q
            + jnp.dot(low_score, kv_block[:, :HD], preferred_element_type=jnp.float32) * score_scale
        )
        key_term = contract_rows(low_score, q_rows) * score_scale
        value_term = contract_rows(low_probs, grad_rows)
        return (grad_q, jnp.concatenate([key_term, value_term], axis=1))

    zero_grad = jnp.zeros((row_total, HD), jnp.float32)

    def cycle_step(cycle_index, state_now):
        grad_q, kv_block, key_grads = state_now
        source = (my_stripe - cycle_index) % stripe_count
        key_pos = jnp.arange(local_count, dtype=jnp.int32) * stripe_count + source
        grad_q, key_term = backward_block(grad_q, kv_block, key_pos)
        kv_block = from_behind(kv_block, "ctx", 1)
        key_grads = from_behind(key_grads + key_term, "ctx", 1)
        return (grad_q, kv_block, key_grads)

    def cycle_pair(pair_index, state_now):
        return cycle_step(2 * pair_index + 1, cycle_step(2 * pair_index, state_now))

    start_state = (zero_grad, kv_local, jnp.zeros((local_count, 2 * HD), jnp.float32))
    grad_q, spent_kv, key_grads = lax.fori_loop(0, stripe_count // 2, cycle_pair, start_state)
    kv_grad_low = key_grads.astype(jnp.bfloat16)
    grad_q_out = grad_q.astype(jnp.bfloat16).reshape(1, 1, local_count, q_width)
    dp_count = lax.axis_size("dp")
    weight_shard = lax.psum_scatter(
        contract_rows(x_local, kv_grad_low), "ctx", scatter_dimension=0, tiled=True
    )
    weight_total = lax.psum(weight_shard, "dp")
    return (grad_q_out, kv_grad_low.reshape(1, 1, local_count, 2 * HD), weight_total / dp_count)


def solution(mesh):
    return jax.shard_map(
        on_device,
        mesh=mesh,
        in_specs=(
            P("dp", "ctx", None, None),
            P("dp", "ctx", None, None),
            P("dp", "ctx", None, None),
            P("dp", "ctx", None, None),
            P("dp", None),
        ),
        out_specs=(P("dp", "ctx", None, None), P("dp", "ctx", None, None), P("ctx", None)),
        check_vma=False,
    )
```

profile of v0, /device:TPU:0, one launch (start us, length us, event | category | flops | bytes accessed | tf_op | source)
XLA Modules:
  0.0 199.8 jit_solution(7566774253962633199)
XLA Ops:
  7.2 0.9 copy.50
  8.1 0.8 reduce-window.9
  9.0 1.1 reshape_squeeze.6
  10.0 1.1 reshape_squeeze.7
  11.1 16.6 %all-gather = bf16[1,1,1024,256]{3,2,1,0:T(8,128)(2,1)S(1)} all-gather(bf16[1,1,128,256]{3,2,1,0:T(8,128)(2,1)S(1)} %copy.50), channel_id=2, replica_groups=mesh['dp'=4,'ctx'=8] {'ctx'}, dimensions={2}, use_global_device_ids=true | all-gather | bytes 589824 | tf_op jit(solution)/shard_map/all_gather | solution.py:83
  27.7 9.2 %while.41 = (s32[]{:T(128)}, f32[1024]{0:T(1024)S(1)}, f32[1024]{0:T(1024)S(1)}, f32[1024]{0:T(1024)S(1)}, s32[2]{0:T(128)S(1)}, /*index=5*/s32[10]{0:T(128)S(1)...) while((s32[]{:T(128)}, f32[1024]{0:T(1024)S(1)}, ...), condition=%wide.region_7.8_spmd.clone, body=%wide.region_1.7_spmd.clone.sunk | while | flops 275166080 | bytes 10976516 | solution.py:91
  27.7 0.7 dynamic_slice.22
  29.8 0.6 copy.19
  30.4 0.5 fusion.111
  30.9 0.8 fusion.112
  31.7 0.6 fusion.113
  32.3 0.7 dynamic_slice.22
  34.4 0.6 copy.19
  35.0 0.5 fusion.111
  35.5 0.8 fusion.112
  36.3 0.6 fusion.113
  37.0 56.3 %while.42 = (s32[]{:T(128)}, f32[1024,128]{1,0:T(8,128)S(1)}, bf16[128,256]{1,0:T(8,128)(2,1)S(1)}, f32[128,256]{0,1:T(8,128)S(1)}, s32[]{:T(128)}, /*index=5*/s...) while((s32[]{:T(128)}, f32[1024,128]{1,0:T(8,128)S(1)}, ...), condition=%wide.region_12.13_spmd.clone.clone.clone, body=%wide.region_8.12_spmd.clone.clone.clone.sunk | while | flops 338411936 | bytes 11827317 | solution.py:131
  37.0 0.4 collective-permute-start
  37.7 0.3 fusion.139
  38.8 1.3 collective-permute-start.2
  40.3 2.2 %collective-permute-done = bf16[128,256]{1,0:T(8,128)(2,1)S(1)} collective-permute-done((bf16[128,256]{1,0:T(8,128)(2,1)S(1)}, bf16[128,256]{1,0:T(8,128)(2,1)S(1)}, u32[]{:S(2)}, u32[]{:S(2)}) %collective-permute-start) | collective-permute-done | bytes 65568 | tf_op jit(solution)/shard_map/while/body/eval_jaxpr/ppermute | solution.py:15
  42.5 0.3 fusion.142
  43.7 1.4 collective-permute-done.2
  45.4 3.3 %collective-permute-done.1 = bf16[128,256]{1,0:T(8,128)(2,1)S(1)} collective-permute-done((bf16[128,256]{1,0:T(8,128)(2,1)S(1)}, bf16[128,256]{1,0:T(8,128)(2,1)S(1)}, u32[]{:S(2)}, u32[]{:S(2)}) %collective-permute-start.1) | collective-permute-done | bytes 65568 | tf_op jit(solution)/shard_map/while/body/eval_jaxpr/ppermute | solution.py:15
  48.6 2.7 %collective-permute-done.3 = f32[128,256]{0,1:T(8,128)S(1)} collective-permute-done((f32[128,256]{0,1:T(8,128)S(1)}, f32[128,256]{0,1:T(8,128)S(1)}, u32[]{:S(2)}, u32[]{:S(2)}) %collective-permute-start.3) | collective-permute-done | bytes 131104 | tf_op jit(solution)/shard_map/while/body/eval_jaxpr/ppermute | solution.py:15
  51.6 0.3 fusion.139
  53.1 3.8 %collective-permute-done = bf16[128,256]{1,0:T(8,128)(2,1)S(1)} collective-permute-done((bf16[128,256]{1,0:T(8,128)(2,1)S(1)}, bf16[128,256]{1,0:T(8,128)(2,1)S(1)}, u32[]{:S(2)}, u32[]{:S(2)}) %collective-permute-start) | collective-permute-done | bytes 65568 | tf_op jit(solution)/shard_map/while/body/eval_jaxpr/ppermute | solution.py:15
  58.0 1.0 collective-permute-done.2
  59.3 3.6 %collective-permute-done.1 = bf16[128,256]{1,0:T(8,128)(2,1)S(1)} collective-permute-done((bf16[128,256]{1,0:T(8,128)(2,1)S(1)}, bf16[128,256]{1,0:T(8,128)(2,1)S(1)}, u32[]{:S(2)}, u32[]{:S(2)}) %collective-permute-start.1) | collective-permute-done | bytes 65568 | tf_op jit(solution)/shard_map/while/body/eval_jaxpr/ppermute | solution.py:15
  62.9 2.4 %collective-permute-done.3 = f32[128,256]{0,1:T(8,128)S(1)} collective-permute-done((f32[128,256]{0,1:T(8,128)S(1)}, f32[128,256]{0,1:T(8,128)S(1)}, u32[]{:S(2)}, u32[]{:S(2)}) %collective-permute-start.3) | collective-permute-done | bytes 131104 | tf_op jit(solution)/shard_map/while/body/eval_jaxpr/ppermute | solution.py:15
  65.6 0.3 fusion.139
  67.0 3.7 %collective-permute-done = bf16[128,256]{1,0:T(8,128)(2,1)S(1)} collective-permute-done((bf16[128,256]{1,0:T(8,128)(2,1)S(1)}, bf16[128,256]{1,0:T(8,128)(2,1)S(1)}, u32[]{:S(2)}, u32[]{:S(2)}) %collective-permute-start) | collective-permute-done | bytes 65568 | tf_op jit(solution)/shard_map/while/body/eval_jaxpr/ppermute | solution.py:15
  70.8 0.3 fusion.142
  72.0 1.0 collective-permute-done.2
  73.3 3.6 %collective-permute-done.1 = bf16[128,256]{1,0:T(8,128)(2,1)S(1)} collective-permute-done((bf16[128,256]{1,0:T(8,128)(2,1)S(1)}, bf16[128,256]{1,0:T(8,128)(2,1)S(1)}, u32[]{:S(2)}, u32[]{:S(2)}) %collective-permute-start.1) | collective-permute-done | bytes 65568 | tf_op jit(solution)/shard_map/while/body/eval_jaxpr/ppermute | solution.py:15
  76.9 2.3 %collective-permute-done.3 = f32[128,256]{0,1:T(8,128)S(1)} collective-permute-done((f32[128,256]{0,1:T(8,128)S(1)}, f32[128,256]{0,1:T(8,128)S(1)}, u32[]{:S(2)}, u32[]{:S(2)}) %collective-permute-start.3) | collective-permute-done | bytes 131104 | tf_op jit(solution)/shard_map/while/body/eval_jaxpr/ppermute | solution.py:15
  79.6 0.3 fusion.139
  81.0 3.7 %collective-permute-done = bf16[128,256]{1,0:T(8,128)(2,1)S(1)} collective-permute-done((bf16[128,256]{1,0:T(8,128)(2,1)S(1)}, bf16[128,256]{1,0:T(8,128)(2,1)S(1)}, u32[]{:S(2)}, u32[]{:S(2)}) %collective-permute-start) | collective-permute-done | bytes 65568 | tf_op jit(solution)/shard_map/while/body/eval_jaxpr/ppermute | solution.py:15
  84.7 0.3 fusion.142
  85.9 1.0 collective-permute-done.2
  87.2 3.6 %collective-permute-done.1 = bf16[128,256]{1,0:T(8,128)(2,1)S(1)} collective-permute-done((bf16[128,256]{1,0:T(8,128)(2,1)S(1)}, bf16[128,256]{1,0:T(8,128)(2,1)S(1)}, u32[]{:S(2)}, u32[]{:S(2)}) %collective-permute-start.1) | collective-permute-done | bytes 65568 | tf_op jit(solution)/shard_map/while/body/eval_jaxpr/ppermute | solution.py:15
  90.9 2.3 %collective-permute-done.3 = f32[128,256]{0,1:T(8,128)S(1)} collective-permute-done((f32[128,256]{0,1:T(8,128)S(1)}, f32[128,256]{0,1:T(8,128)S(1)}, u32[]{:S(2)}, u32[]{:S(2)}) %collective-permute-start.3) | collective-permute-done | bytes 131104 | tf_op jit(solution)/shard_map/while/body/eval_jaxpr/ppermute | solution.py:15
  93.3 2.7 %convolution_bitcast_fusion = f32[4096,256]{0,1:T(8,128)} fusion(bf16[1,1,128,4096]{3,2,1,0:T(8,128)(2,1)S(1)} %copy-done, bf16[128,256]{1,0:T(8,128)(2,1)S(1)} %copy.16), kind=kOutput, calls=%fused_computation.91 | convolution fusion | flops 268435456 | bytes 5308416 | tf_op jit(solution)/shard_map/dot_general | solution.py:32
  96.1 48.3 %reduce-scatter.2.cloned.1.call-done = f32[512,256]{0,1:T(8,128)} async-done(((f32[4096,256]{0,1:T(8,128)}), f32[512,256]{0,1:T(8,128)}) %reduce-scatter.2.cloned.1.call-update) | async-done | bytes 524304 | tf_op jit(solution)/shard_map/reduce_scatter | solution.py:135
  144.4 0.8 reshape.519
  145.2 45.7 %all-reduce.2.cloned.1.call-done = f32[512,256]{0,1:T(8,128)} async-done(((f32[512,256]{0,1:T(8,128)}), f32[512,256]{0,1:T(8,128)}) %all-reduce.2.cloned.1.call-update) | async-done | bytes 524304 | tf_op jit(solution)/shard_map/psum | solution.py:138
  190.9 1.1 broadcast_multiply_fusion
  192.0 1.0 copy.17
  (130 shorter events, 11.9 us)
Async XLA Ops:
  7.2 86.2 %copy-start = (bf16[1,1,128,4096]{3,2,1,0:T(8,128)(2,1)S(1)}, bf16[1,1,128,4096]{3,2,1,0:T(8,128)(2,1)}, u32[]{:S(2)}) copy-start(bf16[1,1,128,4096]{3,2,1,0:T(8,128)(2,1)} %param.9) | copy-start | bytes 3145732
  7.2 137.2 %reduce-scatter.2.cloned.1.call-start = ((), (), s32[]{:S(2)}) async-start(), calls=%async_computation.1 | async-start | bytes 4718592 | tf_op jit(solution)/shard_map/reduce_scatter | solution.py:135
  37.0 5.5 %collective-permute-start = (bf16[128,256]{1,0:T(8,128)(2,1)S(1)}, bf16[128,256]{1,0:T(8,128)(2,1)S(1)}, u32[]{:S(2)}, u32[]{:S(2)}) collective-permute-start(bf16[128,256]{1,0:T(8,128)(2,1)S(1)} %get-tuple-element.882), channel_id=1, source_target_pairs={{0,1},{1,2},{2,3},{3,4},{4,5},{5,6},{6,7},{7,0},{8,9},{9,10},{10,1... | collective-permute-start | bytes 196616 | tf_op jit(solution)/shard_map/while/body/eval_jaxpr/ppermute | solution.py:15
  38.8 6.2 %collective-permute-start.2 = (f32[128,256]{0,1:T(8,128)S(1)}, f32[128,256]{0,1:T(8,128)S(1)}, u32[]{:S(2)}, u32[]{:S(2)}) collective-permute-start(f32[128,256]{0,1:T(8,128)S(1)} %maximum_add_fusion.4), channel_id=1, source_target_pairs={{0,1},{1,2},{2,3},{3,4},{4,5},{5,6},{6,7},{7,0},{8,9},{9,10},{10,1... | collective-permute-start | bytes 393224 | tf_op jit(solution)/shard_map/while/body/eval_jaxpr/ppermute | solution.py:15
  43.1 5.5 %collective-permute-start.1 = (bf16[128,256]{1,0:T(8,128)(2,1)S(1)}, bf16[128,256]{1,0:T(8,128)(2,1)S(1)}, u32[]{:S(2)}, u32[]{:S(2)}) collective-permute-start(bf16[128,256]{1,0:T(8,128)(2,1)S(1)} %collective-permute-done), channel_id=1, source_target_pairs={{0,1},{1,2},{2,3},{3,4},{4,5},{5,6},{6,7},{7,0},{8,9},{9,10},{10,1... | collective-permute-start | bytes 196616 | tf_op jit(solution)/shard_map/while/body/eval_jaxpr/ppermute | solution.py:15
  45.1 6.2 %collective-permute-start.3 = (f32[128,256]{0,1:T(8,128)S(1)}, f32[128,256]{0,1:T(8,128)S(1)}, u32[]{:S(2)}, u32[]{:S(2)}) collective-permute-start(f32[128,256]{0,1:T(8,128)S(1)} %maximum_add_fusion.5), channel_id=1, source_target_pairs={{0,1},{1,2},{2,3},{3,4},{4,5},{5,6},{6,7},{7,0},{8,9},{9,10},{10,1... | collective-permute-start | bytes 393224 | tf_op jit(solution)/shard_map/while/body/eval_jaxpr/ppermute | solution.py:15
  51.3 5.5 %collective-permute-start = (bf16[128,256]{1,0:T(8,128)(2,1)S(1)}, bf16[128,256]{1,0:T(8,128)(2,1)S(1)}, u32[]{:S(2)}, u32[]{:S(2)}) collective-permute-start(bf16[128,256]{1,0:T(8,128)(2,1)S(1)} %get-tuple-element.882), channel_id=1, source_target_pairs={{0,1},{1,2},{2,3},{3,4},{4,5},{5,6},{6,7},{7,0},{8,9},{9,10},{10,1... | collective-permute-start | bytes 196616 | tf_op jit(solution)/shard_map/while/body/eval_jaxpr/ppermute | solution.py:15
  52.8 6.2 %collective-permute-start.2 = (f32[128,256]{0,1:T(8,128)S(1)}, f32[128,256]{0,1:T(8,128)S(1)}, u32[]{:S(2)}, u32[]{:S(2)}) collective-permute-start(f32[128,256]{0,1:T(8,128)S(1)} %maximum_add_fusion.4), channel_id=1, source_target_pairs={{0,1},{1,2},{2,3},{3,4},{4,5},{5,6},{6,7},{7,0},{8,9},{9,10},{10,1... | collective-permute-start | bytes 393224 | tf_op jit(solution)/shard_map/while/body/eval_jaxpr/ppermute | solution.py:15
  57.4 5.5 %collective-permute-start.1 = (bf16[128,256]{1,0:T(8,128)(2,1)S(1)}, bf16[128,256]{1,0:T(8,128)(2,1)S(1)}, u32[]{:S(2)}, u32[]{:S(2)}) collective-permute-start(bf16[128,256]{1,0:T(8,128)(2,1)S(1)} %collective-permute-done), channel_id=1, source_target_pairs={{0,1},{1,2},{2,3},{3,4},{4,5},{5,6},{6,7},{7,0},{8,9},{9,10},{10,1... | collective-permute-start | bytes 196616 | tf_op jit(solution)/shard_map/while/body/eval_jaxpr/ppermute | solution.py:15
  59.0 6.2 %collective-permute-start.3 = (f32[128,256]{0,1:T(8,128)S(1)}, f32[128,256]{0,1:T(8,128)S(1)}, u32[]{:S(2)}, u32[]{:S(2)}) collective-permute-start(f32[128,256]{0,1:T(8,128)S(1)} %maximum_add_fusion.5), channel_id=1, source_target_pairs={{0,1},{1,2},{2,3},{3,4},{4,5},{5,6},{6,7},{7,0},{8,9},{9,10},{10,1... | collective-permute-start | bytes 393224 | tf_op jit(solution)/shard_map/while/body/eval_jaxpr/ppermute | solution.py:15
  65.3 5.5 %collective-permute-start = (bf16[128,256]{1,0:T(8,128)(2,1)S(1)}, bf16[128,256]{1,0:T(8,128)(2,1)S(1)}, u32[]{:S(2)}, u32[]{:S(2)}) collective-permute-start(bf16[128,256]{1,0:T(8,128)(2,1)S(1)} %get-tuple-element.882), channel_id=1, source_target_pairs={{0,1},{1,2},{2,3},{3,4},{4,5},{5,6},{6,7},{7,0},{8,9},{9,10},{10,1... | collective-permute-start | bytes 196616 | tf_op jit(solution)/shard_map/while/body/eval_jaxpr/ppermute | solution.py:15
  66.7 6.2 %collective-permute-start.2 = (f32[128,256]{0,1:T(8,128)S(1)}, f32[128,256]{0,1:T(8,128)S(1)}, u32[]{:S(2)}, u32[]{:S(2)}) collective-permute-start(f32[128,256]{0,1:T(8,128)S(1)} %maximum_add_fusion.4), channel_id=1, source_target_pairs={{0,1},{1,2},{2,3},{3,4},{4,5},{5,6},{6,7},{7,0},{8,9},{9,10},{10,1... | collective-permute-start | bytes 393224 | tf_op jit(solution)/shard_map/while/body/eval_jaxpr/ppermute | solution.py:15
  71.4 5.5 %collective-permute-start.1 = (bf16[128,256]{1,0:T(8,128)(2,1)S(1)}, bf16[128,256]{1,0:T(8,128)(2,1)S(1)}, u32[]{:S(2)}, u32[]{:S(2)}) collective-permute-start(bf16[128,256]{1,0:T(8,128)(2,1)S(1)} %collective-permute-done), channel_id=1, source_target_pairs={{0,1},{1,2},{2,3},{3,4},{4,5},{5,6},{6,7},{7,0},{8,9},{9,10},{10,1... | collective-permute-start | bytes 196616 | tf_op jit(solution)/shard_map/while/body/eval_jaxpr/ppermute | solution.py:15
  73.0 6.2 %collective-permute-start.3 = (f32[128,256]{0,1:T(8,128)S(1)}, f32[128,256]{0,1:T(8,128)S(1)}, u32[]{:S(2)}, u32[]{:S(2)}) collective-permute-start(f32[128,256]{0,1:T(8,128)S(1)} %maximum_add_fusion.5), channel_id=1, source_target_pairs={{0,1},{1,2},{2,3},{3,4},{4,5},{5,6},{6,7},{7,0},{8,9},{9,10},{10,1... | collective-permute-start | bytes 393224 | tf_op jit(solution)/shard_map/while/body/eval_jaxpr/ppermute | solution.py:15
  79.2 5.5 %collective-permute-start = (bf16[128,256]{1,0:T(8,128)(2,1)S(1)}, bf16[128,256]{1,0:T(8,128)(2,1)S(1)}, u32[]{:S(2)}, u32[]{:S(2)}) collective-permute-start(bf16[128,256]{1,0:T(8,128)(2,1)S(1)} %get-tuple-element.882), channel_id=1, source_target_pairs={{0,1},{1,2},{2,3},{3,4},{4,5},{5,6},{6,7},{7,0},{8,9},{9,10},{10,1... | collective-permute-start | bytes 196616 | tf_op jit(solution)/shard_map/while/body/eval_jaxpr/ppermute | solution.py:15
  80.7 6.2 %collective-permute-start.2 = (f32[128,256]{0,1:T(8,128)S(1)}, f32[128,256]{0,1:T(8,128)S(1)}, u32[]{:S(2)}, u32[]{:S(2)}) collective-permute-start(f32[128,256]{0,1:T(8,128)S(1)} %maximum_add_fusion.4), channel_id=1, source_target_pairs={{0,1},{1,2},{2,3},{3,4},{4,5},{5,6},{6,7},{7,0},{8,9},{9,10},{10,1... | collective-permute-start | bytes 393224 | tf_op jit(solution)/shard_map/while/body/eval_jaxpr/ppermute | solution.py:15
  85.3 5.5 %collective-permute-start.1 = (bf16[128,256]{1,0:T(8,128)(2,1)S(1)}, bf16[128,256]{1,0:T(8,128)(2,1)S(1)}, u32[]{:S(2)}, u32[]{:S(2)}) collective-permute-start(bf16[128,256]{1,0:T(8,128)(2,1)S(1)} %collective-permute-done), channel_id=1, source_target_pairs={{0,1},{1,2},{2,3},{3,4},{4,5},{5,6},{6,7},{7,0},{8,9},{9,10},{10,1... | collective-permute-start | bytes 196616 | tf_op jit(solution)/shard_map/while/body/eval_jaxpr/ppermute | solution.py:15
  87.0 6.2 %collective-permute-start.3 = (f32[128,256]{0,1:T(8,128)S(1)}, f32[128,256]{0,1:T(8,128)S(1)}, u32[]{:S(2)}, u32[]{:S(2)}) collective-permute-start(f32[128,256]{0,1:T(8,128)S(1)} %maximum_add_fusion.5), channel_id=1, source_target_pairs={{0,1},{1,2},{2,3},{3,4},{4,5},{5,6},{6,7},{7,0},{8,9},{9,10},{10,1... | collective-permute-start | bytes 393224 | tf_op jit(solution)/shard_map/while/body/eval_jaxpr/ppermute | solution.py:15
  93.3 2.7 %copy-start.1 = (bf16[128,256]{1,0:T(8,128)(2,1)}, bf16[128,256]{1,0:T(8,128)(2,1)S(1)}, u32[]{:S(2)}) copy-start(bf16[128,256]{1,0:T(8,128)(2,1)S(1)} %copy.16) | copy-start | bytes 196612
  96.0 94.9 %all-reduce.2.cloned.1.call-start = ((), (), s32[]{:S(2)}) async-start(), calls=%async_computation.2 | async-start | bytes 1048576 | tf_op jit(solution)/shard_map/psum | solution.py:138
Sparse Core Ops, SparseCore 0:
  96.1 48.1 reduce-scatter.1
  147.4 43.4 all-reduce.1
where the time goes:
time: 200 us
  waiting for transfers between devices  136 us (68%)
  blocking collectives  16.6 us (8%)
  matrix products  15.7 us (8%)
  between operations  14.1 us (7%)
  local copies, waits for them, and re-layouts  8.09 us (4%)
  other arithmetic  5.1 us (3%)
  starting transfers between devices  2.4 us (1%)
  loops' own time  2.14 us (1%)
    reduce_scatter x1, waiting for transfers between devices, on_device(): lax.psum_scatter(contract_rows(x_local, kv_grad_low), 'ctx', scatter_dime...  48.3 us
    psum x1, waiting for transfers between devices, on_device(): weight_total = lax.psum(weight_shard, 'dp')  45.7 us
    ppermute x16, waiting for transfers between devices, from_behind(): lax.ppermute(x, axis, [(i, (i + by) % length) for i in range(length)])  41.7 us
    all_gather x1, blocking collectives, on_device(): kv_piece = lax.all_gather(kv_local, 'ctx', axis=0, tiled=True)  16.6 us
    dot_general x17, matrix products, contract_rows(): lax.dot_general(left_side, right_side, (((0,), (0,)), ((), ())), preferre...  7.14 us
  transfers between devices with their start and end apart: 18, of which 18 were waited for; matrix products, arithmetic and copies ran while one was open for 6% of the time, Pallas kernels for 0%

commit v1 on v0

v1 whole, which is shorter than its diff:
```python
import functools

import jax
import jax.numpy as jnp
from jax import lax
from jax.experimental import pallas as pl
from jax.experimental.pallas import tpu as pltpu
from jax.sharding import PartitionSpec as P

HD = 128
RESPONSES = 4
LOG2E = 1.4426950408889634
NEG = -1e30

NT = (((1,), (1,)), ((), ()))
TN = (((0,), (0,)), ((), ()))


def dot(a, b, dims=(((1,), (0,)), ((), ()))):
    return lax.dot_general(a, b, dims, preferred_element_type=jnp.float32)


def swap(x, axis, mask):
    size = lax.axis_size(axis)
    return lax.ppermute(x, axis, [(i, i ^ mask) for i in range(size)])


def attention_kernel(half, local, pieces, *refs):
    (len_ref, me_ref), kv_refs = refs[:2], refs[2 : 2 + half + 1]
    q_ref, do_ref = refs[3 + half : 5 + half]
    gq_ref, own_ref, sib_ref = refs[5 + half : 8 + half]
    k_all, v_all, bias, x_buf, dp_buf, p_buf, ds_buf = refs[8 + half :]
    stripes = 2 * half
    me = me_ref[0]
    heads = q_ref.shape[1] // HD
    per_group = RESPONSES + 1
    coef = HD**-0.5 * LOG2E

    for k in range(half):
        rows = slice(k * local, (k + 1) * local)
        k_all[rows, :] = kv_refs[k][:, :HD]
        v_all[rows, :] = kv_refs[k][:, HD:]
    k_all[half * local :, :] = kv_refs[half][:, :HD]
    v_all[half * local :, :] = kv_refs[half][:, HD:]

    q_pos = lax.broadcasted_iota(jnp.int32, (1, local), 1) * stripes + me
    own_start = jnp.zeros((1, local), jnp.int32)
    prompt_start = jnp.zeros((1, local), jnp.int32)
    prompt_end = jnp.zeros((1, local), jnp.int32)
    start = jnp.int32(0)
    for k in range(pieces):
        length = len_ref[0, k]
        inside = q_pos >= start
        own_start = jnp.where(inside, start, own_start)
        if k % per_group == 0:
            prompt_start = jnp.where(inside, start, prompt_start)
            prompt_end = jnp.where(inside, start + length, prompt_end)
        start = start + length
    prompt_end = jnp.minimum(prompt_end, q_pos + 1)
    row_pos = lax.broadcasted_iota(jnp.int32, (local, local), 0) * stripes
    for m in range(stripes):
        b, k = m // half, m % half
        k_pos = row_pos + (me ^ (2 * k + b))
        ok = ((k_pos >= own_start) & (k_pos <= q_pos)) | (
            (k_pos >= prompt_start) & (k_pos < prompt_end)
        )
        bias[m * local : (m + 1) * local, :] = jnp.where(ok, 0.0, NEG)

    def head_pair(hp, _):
        c0 = pl.multiple_of(hp * 2 * HD, 2 * HD)
        q2 = jnp.concatenate(
            [q_ref[:, pl.ds(c0, HD)], q_ref[:, pl.ds(c0 + HD, HD)]], axis=0
        )
        do2 = jnp.concatenate(
            [do_ref[:, pl.ds(c0, HD)], do_ref[:, pl.ds(c0 + HD, HD)]], axis=0
        )
        width = 2 * local
        top = jnp.full((8, width), NEG, jnp.float32)
        for m in range(stripes):
            rows = slice(m * local, (m + 1) * local)
            b = bias[rows, :]
            x = dot(k_all[rows, :], q2, NT) + jnp.concatenate([b, b], axis=1)
            x_buf[rows, :] = x
            top = jnp.maximum(top, jnp.max(x.reshape(local // 8, 8, width), axis=0))
        top = jnp.max(top, axis=0, keepdims=True) * coef
        total = jnp.zeros((8, width), jnp.float32)
        weighted = jnp.zeros((8, width), jnp.float32)
        for m in range(stripes):
            rows = slice(m * local, (m + 1) * local)
            e = jnp.exp2(x_buf[rows, :] * coef - top)
            d = dot(v_all[rows, :], do2, NT)
            total = total + jnp.sum(e.reshape(local // 8, 8, width), axis=0)
            weighted = weighted + jnp.sum((e * d).reshape(local // 8, 8, width), axis=0)
            x_buf[rows, :] = e
            dp_buf[rows, :] = d
        total = jnp.sum(total, axis=0, keepdims=True)
        weighted = jnp.sum(weighted, axis=0, keepdims=True)
        inv = 1.0 / total
        delta = weighted * inv
        for m in range(stripes):
            rows = slice(m * local, (m + 1) * local)
            p = x_buf[rows, :] * inv
            ds = p * (dp_buf[rows, :] - delta)
            p_buf[rows, pl.ds(c0, 2 * HD)] = p.astype(jnp.bfloat16)
            ds_buf[rows, pl.ds(c0, 2 * HD)] = ds.astype(jnp.bfloat16)
        gq = dot(ds_buf[:, pl.ds(c0, 2 * HD)], k_all[...], TN) * HD**-0.5
        gq = gq.astype(jnp.bfloat16)
        gq_ref[:, pl.ds(c0, HD)] = gq[:local]
        gq_ref[:, pl.ds(c0 + HD, HD)] = gq[local:]
        return 0

    lax.fori_loop(0, heads // 2, head_pair, 0)

    q_rows = jnp.concatenate([q_ref[:, h * HD : (h + 1) * HD] for h in range(heads)], axis=0)
    do_rows = jnp.concatenate([do_ref[:, h * HD : (h + 1) * HD] for h in range(heads)], axis=0)
    half_rows = half * local
    sib_ref[:, :HD] = (dot(ds_buf[half_rows:, :], q_rows) * HD**-0.5).astype(sib_ref.dtype)
    sib_ref[:, HD:] = dot(p_buf[half_rows:, :], do_rows).astype(sib_ref.dtype)
    own_ref[:, :HD] = dot(ds_buf[:half_rows, :], q_rows) * HD**-0.5
    own_ref[:, HD:] = dot(p_buf[:half_rows, :], do_rows)


def attention(lengths, me, kv_blocks, q, do):
    half = len(kv_blocks) - 1
    local, width = q.shape
    keys = 2 * half * local
    heads = width // HD
    vm = pl.BlockSpec(memory_space=pltpu.VMEM)
    sm = pl.BlockSpec(memory_space=pltpu.SMEM)
    return pl.pallas_call(
        functools.partial(attention_kernel, half, local, lengths.shape[1]),
        out_shape=(
            jax.ShapeDtypeStruct((local, width), jnp.bfloat16),
            jax.ShapeDtypeStruct((half * local, 2 * HD), jnp.float32),
            jax.ShapeDtypeStruct((half * local, 2 * HD), jnp.bfloat16),
        ),
        in_specs=[sm, sm] + [vm] * (half + 3),
        out_specs=(vm, vm, vm),
        scratch_shapes=[
            pltpu.VMEM((keys, HD), jnp.bfloat16),
            pltpu.VMEM((keys, HD), jnp.bfloat16),
            pltpu.VMEM((keys, local), jnp.float32),
            pltpu.VMEM((keys, 2 * local), jnp.float32),
            pltpu.VMEM((keys, 2 * local), jnp.float32),
            pltpu.VMEM((keys, heads * local), jnp.bfloat16),
            pltpu.VMEM((keys, heads * local), jnp.bfloat16),
        ],
        compiler_params=pltpu.CompilerParams(vmem_limit_bytes=56 * 1024 * 1024),
    )(lengths, me, *kv_blocks, q, do)


def on_device(inputs, queries, keys_values, out_grad, lengths):
    stripes = lax.axis_size("ctx")
    rows = lax.axis_size("dp")
    half = stripes // 2
    me = lax.axis_index("ctx")
    row = lax.axis_index("dp")
    x = inputs[0, 0]
    q = queries[0, 0]
    do = out_grad[0, 0]
    kv = keys_values[0, 0]
    local, features = x.shape
    part = features // (stripes * rows)

    kv_own = [kv] + [swap(kv, "ctx", 2 * k) for k in range(1, half)]
    kv_sib = swap(jnp.concatenate(kv_own, axis=0), "ctx", 1)

    xb = x.reshape(local, stripes, rows, part)
    x_slabs = []
    for k in range(rows):
        slab = lax.dynamic_index_in_dim(xb, row ^ k, 2, keepdims=False)
        slab = slab.reshape(local, stripes * part)
        x_slabs.append(slab if k == 0 else swap(slab, "dp", k))

    gq, part_own, part_sib = attention(
        lengths, me.reshape(1).astype(jnp.int32), kv_own + [kv_sib], q, do
    )

    chip = part_own + swap(part_sib, "ctx", 1).astype(jnp.float32)
    chip = chip.reshape(half, local, 2 * HD)
    terms = [swap(chip[k].astype(jnp.bfloat16), "ctx", 2 * k) for k in range(1, half)]
    gkv = chip[0] + sum(t.astype(jnp.float32) for t in terms)
    gkv = gkv.astype(jnp.bfloat16)

    g_rows = [gkv] + [swap(gkv, "dp", k) for k in range(1, rows)]
    x_all = jnp.concatenate(x_slabs, axis=0)
    g_all = jnp.concatenate(g_rows, axis=0)
    w = dot(x_all, g_all, TN) * (1.0 / rows)
    w = w.reshape(half, 2, part, 2 * HD)
    core = me % 2
    w_own = lax.dynamic_index_in_dim(w, core, 1, keepdims=False)
    w_sib = lax.dynamic_index_in_dim(w, 1 - core, 1, keepdims=False)
    w_chip = w_own + swap(w_sib.astype(jnp.bfloat16), "ctx", 1).astype(jnp.float32)
    z = me // 2
    w_mine = lax.dynamic_index_in_dim(w_chip, z, 0, keepdims=False)
    for k in range(1, half):
        block = lax.dynamic_index_in_dim(w_chip, z ^ k, 0, keepdims=False)
        w_mine = w_mine + swap(block.astype(jnp.bfloat16), "ctx", 2 * k).astype(jnp.float32)

    low = w_mine.astype(jnp.bfloat16)
    stacked = jnp.stack([low] + [swap(low, "dp", k) for k in range(1, rows)])
    order = jnp.arange(rows) ^ row
    w_out = stacked[order].reshape(rows * part, 2 * HD).astype(jnp.float32)
    return (
        gq.reshape(1, 1, local, -1),
        gkv.reshape(1, 1, local, 2 * HD),
        w_out,
    )


def solution(mesh):
    spec = P("dp", "ctx", None, None)
    return jax.shard_map(
        on_device,
        mesh=mesh,
        in_specs=(spec, spec, spec, spec, P("dp", None)),
        out_specs=(spec, spec, P("ctx", None)),
        check_vma=False,
    )
```

time: 200 us -> 68 us (0.34)
  waiting for transfers between devices: 136 us -> 27 us
  starting transfers between devices: 2.4 us -> 26.7 us
  blocking collectives: 16.6 us -> 0 us
  matrix products: 15.7 us -> 0.43 us
  between operations: 14.1 us -> 0.84 us
  Pallas kernels: 0 us -> 8.78 us
  local copies, waits for them, and re-layouts: 8.09 us -> 2.1 us
  other arithmetic: 5.1 us -> 1.95 us
  loops' own time: 2.14 us -> 0 us
    reduce_scatter x1 -> x0, waiting for transfers between devices: 48.3 us -> none  [on_device(): lax.psum_scatter(contract_rows(x_local, kv_grad_low), 'ctx', scatter_dime...]
    psum x1 -> x0, waiting for transfers between devices: 45.7 us -> none  [on_device(): weight_total = lax.psum(weight_shard, 'dp')]
    ppermute x16 -> x21, starting transfers between devices: 2.33 us -> 26.7 us  [swap(): return lax.ppermute(x, axis, [(i, i ^ mask) for i in range(size)])]
    all_gather x1 -> x0, blocking collectives: 16.6 us -> none  [on_device(): kv_piece = lax.all_gather(kv_local, 'ctx', axis=0, tiled=True)]
    dot_general x45 -> x1, matrix products: 15.7 us -> 0.43 us  [dot(): return lax.dot_general(a, b, dims, preferred_element_type=jnp.float32)]
    ppermute x16 -> x21, waiting for transfers between devices: 41.7 us -> 27 us  [swap(): return lax.ppermute(x, axis, [(i, i ^ mask) for i in range(size)])]
    pallas_call x0 -> x1, Pallas kernels: none -> 8.78 us  [attention(): pl.pallas_call(functools.partial(attention_kernel, half, local, lengths.s...]
    reshape x5 -> x0, local copies, waits for them, and re-layouts: 2.53 us -> none  [the longest x4 1.71 us: row_mask(): jnp.broadcast_to(allowed[:, None, :], (local_count, head_count, key_count))]
  transfers between devices with their start and end apart: 18 -> 21, of which waited for: 18 -> 17; matrix products, arithmetic and copies ran while one was open for 6% -> 1% of each run, Pallas kernels for 0% -> 0%
where the time goes in v1:
time: 68 us; the launch traced here: 67.8 us
  waiting for transfers between devices  27 us (40%)
  starting transfers between devices  26.7 us (39%)
  Pallas kernels  8.78 us (13%)
  local copies, waits for them, and re-layouts  2.1 us (3%)
  other arithmetic  1.95 us (3%)
  between operations  0.84 us (1%)
    ppermute x21, waiting for transfers between devices, swap(): return lax.ppermute(x, axis, [(i, i ^ mask) for i in range(size)])  27 us
    ppermute x21, starting transfers between devices, swap(): return lax.ppermute(x, axis, [(i, i ^ mask) for i in range(size)])  26.7 us
    pallas_call x1, Pallas kernels, attention(): pl.pallas_call(functools.partial(attention_kernel, half, local, lengths.s...  8.78 us
    unnamed x15, local copies, waits for them, and re-layouts  1.36 us
  transfers between devices with their start and end apart: 21, of which 17 were waited for; matrix products, arithmetic and copies ran while one was open for 1% of the time, Pallas kernels for 0%

profile of v1, /device:TPU:0, one launch (start us, length us, event | category | flops | bytes accessed | tf_op | source)
XLA Modules:
  0.0 67.8 jit_solution(2263097985879087816)
XLA Ops:
  0.6 3.1 %collective-permute-start = (bf16[128,256]{1,0:T(8,128)(2,1)}, bf16[128,256]{1,0:T(8,128)(2,1)S(1)}, u32[]{:S(2)}, u32[]{:S(2)}) collective-permute-start(bf16[128,256]{1,0:T(8,128)(2,1)} %bitcast.48), channel_id=1, source_target_pairs={{0,2},{1,3},{2,0},{3,1},{4,6},{5,7},{6,4},{7,5},{8,10},{9,11},{10,... | collective-permute-start | bytes 196616 | tf_op jit(solution)/shard_map/ppermute | solution.py:25
  3.7 2.6 %collective-permute-start.1 = (bf16[128,256]{1,0:T(8,128)(2,1)}, bf16[128,256]{1,0:T(8,128)(2,1)S(1)}, u32[]{:S(2)}, u32[]{:S(2)}) collective-permute-start(bf16[128,256]{1,0:T(8,128)(2,1)} %bitcast.49), channel_id=1, source_target_pairs={{0,4},{1,5},{2,6},{3,7},{4,0},{5,1},{6,2},{7,3},{8,12},{9,13},{10,... | collective-permute-start | bytes 196616 | tf_op jit(solution)/shard_map/ppermute | solution.py:25
  6.3 0.0 collective-permute-start.2
  6.3 4.9 %collective-permute-done.1.refs_4_ = bf16[128,256]{1,0:T(8,128)(2,1)S(1)} collective-permute-done((bf16[128,256]{1,0:T(8,128)(2,1)}, bf16[128,256]{1,0:T(8,128)(2,1)S(1)}, u32[]{:S(2)}, u32[]{:S(2)}) %collective-permute-start.1) | collective-permute-done | bytes 65568 | tf_op jit(solution)/shard_map/ppermute | solution.py:25
  11.2 1.4 %collective-permute-done.2.refs_5_ = bf16[128,256]{1,0:T(8,128)(2,1)S(1)} collective-permute-done((bf16[128,256]{1,0:T(8,128)(2,1)}, bf16[128,256]{1,0:T(8,128)(2,1)S(1)}, u32[]{:S(2)}, u32[]{:S(2)}) %collective-permute-start.2) | collective-permute-done | bytes 65568 | tf_op jit(solution)/shard_map/ppermute | solution.py:25
  12.6 0.9 %pad_maximum_fusion = bf16[512,256]{1,0:T(8,128)(2,1)S(1)} fusion(bf16[128,256]{1,0:T(8,128)(2,1)S(1)} %collective-permute-done.2.refs_5_, bf16[128,256]{1,0:T(8,128)(2,1)S(1)} %collective-permute-done.1.refs_4_, bf16[128,256]{1,0:T(8,128)(2,1)S(1)} %collective-permute-done.refs_3_, bf16[128,256]{1,0:T(8,128)(2,1)} %bitcast.51), kind=kLoop, calls=%fused_computation.13 | loop fusion | flops 1048576 | bytes 524288 | tf_op jit(solution)/shard_map/concatenate | solution.py:166
  13.5 0.1 collective-permute-start.3
  13.6 1.5 %collective-permute-done.3.refs_6_ = bf16[512,256]{1,0:T(8,128)(2,1)S(1)} collective-permute-done((bf16[512,256]{1,0:T(8,128)(2,1)S(1)}, bf16[512,256]{1,0:T(8,128)(2,1)S(1)}, u32[]{:S(2)}, u32[]{:S(2)}) %collective-permute-start.3) | collective-permute-done | bytes 262176 | tf_op jit(solution)/shard_map/ppermute | solution.py:25
  15.1 0.7 %copy-done.2 = bf16[512,256]{1,0:T(8,128)(2,1)} copy-done((bf16[512,256]{1,0:T(8,128)(2,1)}, bf16[512,256]{1,0:T(8,128)(2,1)S(1)}, u32[]{:S(2)}) %copy-start.2) | copy-done | bytes 262168
  15.8 8.8 %shard_map.76 = (bf16[128,1024]{1,0:T(8,128)(2,1)}, f32[512,256]{1,0:T(8,128)}, bf16[512,256]{1,0:T(8,128)(2,1)}) custom-call(s32[1,10]{1,0:T(1,128)} %refs_0_.1, s32[1]{0:T(128)} %bitcast.refs_1_, bf16[128,256]{1,0:T(8,128)(2,1)} %bitcast.52, bf16[128,256]{1,0:T(8,128)(2,1)} %copy-done.3, bf16[128,256]{1,0:T(8,128)(2,1)} %copy-done.4, ...), custom_call_target="tpu_custom_call" | custom-call | tf_op jit(solution)/shard_map/pallas_call | solution.py:130
  24.6 0.1 collective-permute-start.4
  24.7 0.7 copy.8
  25.4 0.9 %collective-permute-done.4 = bf16[512,256]{1,0:T(8,128)(2,1)S(1)} collective-permute-done((bf16[512,256]{1,0:T(8,128)(2,1)}, bf16[512,256]{1,0:T(8,128)(2,1)S(1)}, u32[]{:S(2)}, u32[]{:S(2)}) %collective-permute-start.4) | collective-permute-done | bytes 262176 | tf_op jit(solution)/shard_map/ppermute | solution.py:25
  26.3 0.1 fusion.24
  26.4 1.8 %collective-permute-start.7 = (bf16[128,256]{1,0:T(8,128)(2,1)S(1)}, bf16[128,256]{1,0:T(8,128)(2,1)S(1)}, u32[]{:S(2)}, u32[]{:S(2)}) collective-permute-start(bf16[128,256]{1,0:T(8,128)(2,1)S(1)} %get-tuple-element.19), channel_id=1, source_target_pairs={{0,6},{1,7},{2,4},{3,5},{4,2},{5,3},{6,0},{7,1},{8,14},{9,15},{10,... | collective-permute-start | bytes 196616 | tf_op jit(solution)/shard_map/ppermute | solution.py:25
  28.3 0.0 collective-permute-start.6
  28.3 2.6 %collective-permute-start.5 = (bf16[128,256]{1,0:T(8,128)(2,1)S(1)}, bf16[128,256]{1,0:T(8,128)(2,1)S(1)}, u32[]{:S(2)}, u32[]{:S(2)}) collective-permute-start(bf16[128,256]{1,0:T(8,128)(2,1)S(1)} %get-tuple-element.18), channel_id=1, source_target_pairs={{0,2},{1,3},{2,0},{3,1},{4,6},{5,7},{6,4},{7,5},{8,10},{9,11},{10,... | collective-permute-start | bytes 196616 | tf_op jit(solution)/shard_map/ppermute | solution.py:25
  30.9 0.1 constant_dynamic-slice_fusion.3
  31.0 2.5 %collective-permute-start.10 = (bf16[128,1024]{0,1:T(8,128)(2,1)S(1)}, bf16[128,1024]{0,1:T(8,128)(2,1)S(1)}, u32[]{:S(2)}, u32[]{:S(2)}) collective-permute-start(bf16[128,1024]{0,1:T(8,128)(2,1)S(1)} %bitcast.47), channel_id=1, source_target_pairs={{0,24},{8,16},{16,8},{24,0},{1,25},{9,17},{17,9},{25,1},{2,26},{10... | collective-permute-start | bytes 786440 | tf_op jit(solution)/shard_map/ppermute | solution.py:25
  33.5 0.5 collective-permute-start.9
  34.0 0.7 %collective-permute-start.8 = (bf16[128,1024]{0,1:T(8,128)(2,1)S(1)}, bf16[128,1024]{0,1:T(8,128)(2,1)S(1)}, u32[]{:S(2)}, u32[]{:S(2)}) collective-permute-start(bf16[128,1024]{0,1:T(8,128)(2,1)S(1)} %bitcast.45), channel_id=1, source_target_pairs={{0,8},{8,0},{16,24},{24,16},{1,9},{9,1},{17,25},{25,17},{2,10},{10... | collective-permute-start | bytes 786440 | tf_op jit(solution)/shard_map/ppermute | solution.py:25
  34.7 0.5 collective-permute-done.6
  35.3 0.0 copy-start.6
  35.3 2.5 %collective-permute-start.13 = (bf16[128,256]{1,0:T(8,128)(2,1)S(1)}, bf16[128,256]{1,0:T(8,128)(2,1)S(1)}, u32[]{:S(2)}, u32[]{:S(2)}) collective-permute-start(bf16[128,256]{1,0:T(8,128)(2,1)S(1)} %fusion.15), channel_id=1, source_target_pairs={{0,24},{8,16},{16,8},{24,0},{1,25},{9,17},{17,9},{25,1},{2,26},{10... | collective-permute-start | bytes 196616 | tf_op jit(solution)/shard_map/ppermute | solution.py:25
  37.8 0.5 collective-permute-start.12
  38.3 2.9 %collective-permute-done.10 = bf16[128,1024]{0,1:T(8,128)(2,1)S(1)} collective-permute-done((bf16[128,1024]{0,1:T(8,128)(2,1)S(1)}, bf16[128,1024]{0,1:T(8,128)(2,1)S(1)}, u32[]{:S(2)}, u32[]{:S(2)}) %collective-permute-start.10) | collective-permute-done | bytes 262176 | tf_op jit(solution)/shard_map/ppermute | solution.py:25
  41.2 1.5 %collective-permute-start.11 = (bf16[128,256]{1,0:T(8,128)(2,1)S(1)}, bf16[128,256]{1,0:T(8,128)(2,1)S(1)}, u32[]{:S(2)}, u32[]{:S(2)}) collective-permute-start(bf16[128,256]{1,0:T(8,128)(2,1)S(1)} %fusion.15), channel_id=1, source_target_pairs={{0,8},{8,0},{16,24},{24,16},{1,9},{9,1},{17,25},{25,17},{2,10},{10... | collective-permute-start | bytes 196616 | tf_op jit(solution)/shard_map/ppermute | solution.py:25
  42.7 3.1 %collective-permute-done.9 = bf16[128,1024]{0,1:T(8,128)(2,1)S(1)} collective-permute-done((bf16[128,1024]{0,1:T(8,128)(2,1)S(1)}, bf16[128,1024]{0,1:T(8,128)(2,1)S(1)}, u32[]{:S(2)}, u32[]{:S(2)}) %collective-permute-start.9) | collective-permute-done | bytes 262176 | tf_op jit(solution)/shard_map/ppermute | solution.py:25
  45.9 0.7 %collective-permute-done.8 = bf16[128,1024]{0,1:T(8,128)(2,1)S(1)} collective-permute-done((bf16[128,1024]{0,1:T(8,128)(2,1)S(1)}, bf16[128,1024]{0,1:T(8,128)(2,1)S(1)}, u32[]{:S(2)}, u32[]{:S(2)}) %collective-permute-start.8) | collective-permute-done | bytes 262176 | tf_op jit(solution)/shard_map/ppermute | solution.py:25
  46.6 0.8 %collective-permute-done.13 = bf16[128,256]{1,0:T(8,128)(2,1)S(1)} collective-permute-done((bf16[128,256]{1,0:T(8,128)(2,1)S(1)}, bf16[128,256]{1,0:T(8,128)(2,1)S(1)}, u32[]{:S(2)}, u32[]{:S(2)}) %collective-permute-start.13) | collective-permute-done | bytes 65568 | tf_op jit(solution)/shard_map/ppermute | solution.py:25
  47.3 0.6 collective-permute-done.12
  47.9 0.1 collective-permute-done.11
  48.0 0.4 convolution_multiply_fusion
  48.5 0.1 collective-permute-start.14
  48.6 1.5 %collective-permute-done.14 = bf16[4,128,256]{2,1,0:T(8,128)(2,1)S(1)} collective-permute-done((bf16[4,128,256]{2,1,0:T(8,128)(2,1)S(1)}, bf16[4,128,256]{2,1,0:T(8,128)(2,1)S(1)}, u32[]{:S(2)}, u32[]{:S(2)}) %collective-permute-start.14) | collective-permute-done | bytes 262176 | tf_op jit(solution)/shard_map/ppermute | solution.py:25
  50.1 0.1 bitcast_add_fusion
  50.2 1.9 %collective-permute-start.17 = (bf16[128,256]{1,0:T(8,128)(2,1)S(1)}, bf16[128,256]{1,0:T(8,128)(2,1)S(1)}, u32[]{:S(2)}, u32[]{:S(2)}) collective-permute-start(bf16[128,256]{1,0:T(8,128)(2,1)S(1)} %get-tuple-element.16), channel_id=1, source_target_pairs={{0,6},{1,7},{2,4},{3,5},{4,2},{5,3},{6,0},{7,1},{8,14},{9,15},{10,... | collective-permute-start | bytes 196616 | tf_op jit(solution)/shard_map/ppermute | solution.py:25
  52.0 2.6 %collective-permute-start.15 = (bf16[128,256]{1,0:T(8,128)(2,1)S(1)}, bf16[128,256]{1,0:T(8,128)(2,1)S(1)}, u32[]{:S(2)}, u32[]{:S(2)}) collective-permute-start(bf16[128,256]{1,0:T(8,128)(2,1)S(1)} %get-tuple-element.15), channel_id=1, source_target_pairs={{0,2},{1,3},{2,0},{3,1},{4,6},{5,7},{6,4},{7,5},{8,10},{9,11},{10,... | collective-permute-start | bytes 196616 | tf_op jit(solution)/shard_map/ppermute | solution.py:25
  54.6 2.3 %collective-permute-done.17 = bf16[128,256]{1,0:T(8,128)(2,1)S(1)} collective-permute-done((bf16[128,256]{1,0:T(8,128)(2,1)S(1)}, bf16[128,256]{1,0:T(8,128)(2,1)S(1)}, u32[]{:S(2)}, u32[]{:S(2)}) %collective-permute-start.17) | collective-permute-done | bytes 65568 | tf_op jit(solution)/shard_map/ppermute | solution.py:25
  57.0 2.0 %collective-permute-done.16 = bf16[128,256]{1,0:T(8,128)(2,1)S(1)} collective-permute-done((bf16[128,256]{1,0:T(8,128)(2,1)S(1)}, bf16[128,256]{1,0:T(8,128)(2,1)S(1)}, u32[]{:S(2)}, u32[]{:S(2)}) %collective-permute-start.16) | collective-permute-done | bytes 65568 | tf_op jit(solution)/shard_map/ppermute | solution.py:25
  59.0 1.8 %collective-permute-start.20 = (bf16[128,256]{1,0:T(8,128)(2,1)S(1)}, bf16[128,256]{1,0:T(8,128)(2,1)S(1)}, u32[]{:S(2)}, u32[]{:S(2)}) collective-permute-start(bf16[128,256]{1,0:T(8,128)(2,1)S(1)} %fusion.18), channel_id=1, source_target_pairs={{0,24},{8,16},{16,8},{24,0},{1,25},{9,17},{17,9},{25,1},{2,26},{10... | collective-permute-start | bytes 196616 | tf_op jit(solution)/shard_map/ppermute | solution.py:25
  60.8 1.3 %collective-permute-start.19 = (bf16[128,256]{1,0:T(8,128)(2,1)S(1)}, bf16[128,256]{1,0:T(8,128)(2,1)S(1)}, u32[]{:S(2)}, u32[]{:S(2)}) collective-permute-start(bf16[128,256]{1,0:T(8,128)(2,1)S(1)} %fusion.18), channel_id=1, source_target_pairs={{0,16},{8,24},{16,0},{24,8},{1,17},{9,25},{17,1},{25,9},{2,18},{10... | collective-permute-start | bytes 196616 | tf_op jit(solution)/shard_map/ppermute | solution.py:25
  62.0 0.5 collective-permute-start.18
  62.6 1.7 %collective-permute-done.20 = bf16[128,256]{1,0:T(8,128)(2,1)S(1)} collective-permute-done((bf16[128,256]{1,0:T(8,128)(2,1)S(1)}, bf16[128,256]{1,0:T(8,128)(2,1)S(1)}, u32[]{:S(2)}, u32[]{:S(2)}) %collective-permute-start.20) | collective-permute-done | bytes 65568 | tf_op jit(solution)/shard_map/ppermute | solution.py:25
  64.3 1.1 %collective-permute-done.19 = bf16[128,256]{1,0:T(8,128)(2,1)S(1)} collective-permute-done((bf16[128,256]{1,0:T(8,128)(2,1)S(1)}, bf16[128,256]{1,0:T(8,128)(2,1)S(1)}, u32[]{:S(2)}, u32[]{:S(2)}) %collective-permute-start.19) | collective-permute-done | bytes 65568 | tf_op jit(solution)/shard_map/ppermute | solution.py:25
  65.4 0.9 %collective-permute-done.18 = bf16[128,256]{1,0:T(8,128)(2,1)S(1)} collective-permute-done((bf16[128,256]{1,0:T(8,128)(2,1)S(1)}, bf16[128,256]{1,0:T(8,128)(2,1)S(1)}, u32[]{:S(2)}, u32[]{:S(2)}) %collective-permute-start.18) | collective-permute-done | bytes 65568 | tf_op jit(solution)/shard_map/ppermute | solution.py:25
  66.3 0.6 gather_fusion
  66.9 0.8 %bitcast_convert_fusion = f32[512,256]{1,0:T(8,128)} fusion(bf16[4,128,256]{2,1,0:T(8,128)(2,1)S(1)} %gather_fusion), kind=kLoop, calls=%fused_computation.22 | loop fusion | flops 131072 | bytes 786432 | tf_op jit(solution)/shard_map/convert_element_type | solution.py:203
  (25 shorter events, 0.2 us)
Async XLA Ops:
  0.6 24.1 %copy-start = (bf16[1,1,128,4096]{3,2,1,0:T(8,128)(2,1)S(1)}, bf16[1,1,128,4096]{3,2,1,0:T(8,128)(2,1)}, u32[]{:S(2)}) copy-start(bf16[1,1,128,4096]{3,2,1,0:T(8,128)(2,1)} %param.5) | copy-start | bytes 3145732
  0.6 5.7 %collective-permute-start = (bf16[128,256]{1,0:T(8,128)(2,1)}, bf16[128,256]{1,0:T(8,128)(2,1)S(1)}, u32[]{:S(2)}, u32[]{:S(2)}) collective-permute-start(bf16[128,256]{1,0:T(8,128)(2,1)} %bitcast.48), channel_id=1, source_target_pairs={{0,2},{1,3},{2,0},{3,1},{4,6},{5,7},{6,4},{7,5},{8,10},{9,11},{10,... | collective-permute-start | bytes 196616 | tf_op jit(solution)/shard_map/ppermute | solution.py:25
  3.7 7.5 %collective-permute-start.1 = (bf16[128,256]{1,0:T(8,128)(2,1)}, bf16[128,256]{1,0:T(8,128)(2,1)S(1)}, u32[]{:S(2)}, u32[]{:S(2)}) collective-permute-start(bf16[128,256]{1,0:T(8,128)(2,1)} %bitcast.49), channel_id=1, source_target_pairs={{0,4},{1,5},{2,6},{3,7},{4,0},{5,1},{6,2},{7,3},{8,12},{9,13},{10,... | collective-permute-start | bytes 196616 | tf_op jit(solution)/shard_map/ppermute | solution.py:25
  6.3 6.3 %collective-permute-start.2 = (bf16[128,256]{1,0:T(8,128)(2,1)}, bf16[128,256]{1,0:T(8,128)(2,1)S(1)}, u32[]{:S(2)}, u32[]{:S(2)}) collective-permute-start(bf16[128,256]{1,0:T(8,128)(2,1)} %bitcast.50), channel_id=1, source_target_pairs={{0,6},{1,7},{2,4},{3,5},{4,2},{5,3},{6,0},{7,1},{8,14},{9,15},{10,... | collective-permute-start | bytes 196616 | tf_op jit(solution)/shard_map/ppermute | solution.py:25
  6.3 8.8 %copy-start.3 = (bf16[128,256]{1,0:T(8,128)(2,1)}, bf16[128,256]{1,0:T(8,128)(2,1)S(1)}, u32[]{:S(2)}) copy-start(bf16[128,256]{1,0:T(8,128)(2,1)S(1)} %collective-permute-done.refs_3_) | copy-start | bytes 196612
  11.2 3.9 %copy-start.4 = (bf16[128,256]{1,0:T(8,128)(2,1)}, bf16[128,256]{1,0:T(8,128)(2,1)S(1)}, u32[]{:S(2)}) copy-start(bf16[128,256]{1,0:T(8,128)(2,1)S(1)} %collective-permute-done.1.refs_4_) | copy-start | bytes 196612
  12.6 2.5 %copy-start.5 = (bf16[128,256]{1,0:T(8,128)(2,1)}, bf16[128,256]{1,0:T(8,128)(2,1)S(1)}, u32[]{:S(2)}) copy-start(bf16[128,256]{1,0:T(8,128)(2,1)S(1)} %collective-permute-done.2.refs_5_) | copy-start | bytes 196612
  13.5 1.6 %collective-permute-start.3 = (bf16[512,256]{1,0:T(8,128)(2,1)S(1)}, bf16[512,256]{1,0:T(8,128)(2,1)S(1)}, u32[]{:S(2)}, u32[]{:S(2)}) collective-permute-start(bf16[512,256]{1,0:T(8,128)(2,1)S(1)} %pad_maximum_fusion), channel_id=1, source_target_pairs={{0,1},{1,0},{2,3},{3,2},{4,5},{5,4},{6,7},{7,6},{8,9},{9,8},{10,11... | collective-permute-start | bytes 786440 | tf_op jit(solution)/shard_map/ppermute | solution.py:25
  15.1 0.7 %copy-start.2 = (bf16[512,256]{1,0:T(8,128)(2,1)}, bf16[512,256]{1,0:T(8,128)(2,1)S(1)}, u32[]{:S(2)}) copy-start(bf16[512,256]{1,0:T(8,128)(2,1)S(1)} %collective-permute-done.3.refs_6_) | copy-start | bytes 786436
  24.6 1.7 %collective-permute-start.4 = (bf16[512,256]{1,0:T(8,128)(2,1)}, bf16[512,256]{1,0:T(8,128)(2,1)S(1)}, u32[]{:S(2)}, u32[]{:S(2)}) collective-permute-start(bf16[512,256]{1,0:T(8,128)(2,1)} %get-tuple-element.8), channel_id=1, source_target_pairs={{0,1},{1,0},{2,3},{3,2},{4,5},{5,4},{6,7},{7,6},{8,9},{9,8},{10,11... | collective-permute-start | bytes 786440 | tf_op jit(solution)/shard_map/ppermute | solution.py:25
  24.7 1.6 %copy-start.1 = (f32[512,256]{1,0:T(8,128)S(1)}, f32[512,256]{1,0:T(8,128)}, u32[]{:S(2)}) copy-start(f32[512,256]{1,0:T(8,128)} %get-tuple-element.7) | copy-start | bytes 1572868
  26.4 7.6 %collective-permute-start.7 = (bf16[128,256]{1,0:T(8,128)(2,1)S(1)}, bf16[128,256]{1,0:T(8,128)(2,1)S(1)}, u32[]{:S(2)}, u32[]{:S(2)}) collective-permute-start(bf16[128,256]{1,0:T(8,128)(2,1)S(1)} %get-tuple-element.19), channel_id=1, source_target_pairs={{0,6},{1,7},{2,4},{3,5},{4,2},{5,3},{6,0},{7,1},{8,14},{9,15},{10,... | collective-permute-start | bytes 196616 | tf_op jit(solution)/shard_map/ppermute | solution.py:25
  28.3 7.0 %collective-permute-start.6 = (bf16[128,256]{1,0:T(8,128)(2,1)S(1)}, bf16[128,256]{1,0:T(8,128)(2,1)S(1)}, u32[]{:S(2)}, u32[]{:S(2)}) collective-permute-start(bf16[128,256]{1,0:T(8,128)(2,1)S(1)} %get-tuple-element.20), channel_id=1, source_target_pairs={{0,4},{1,5},{2,6},{3,7},{4,0},{5,1},{6,2},{7,3},{8,12},{9,13},{10,... | collective-permute-start | bytes 196616 | tf_op jit(solution)/shard_map/ppermute | solution.py:25
  28.3 7.0 %collective-permute-start.5 = (bf16[128,256]{1,0:T(8,128)(2,1)S(1)}, bf16[128,256]{1,0:T(8,128)(2,1)S(1)}, u32[]{:S(2)}, u32[]{:S(2)}) collective-permute-start(bf16[128,256]{1,0:T(8,128)(2,1)S(1)} %get-tuple-element.18), channel_id=1, source_target_pairs={{0,2},{1,3},{2,0},{3,1},{4,6},{5,7},{6,4},{7,5},{8,10},{9,11},{10,... | collective-permute-start | bytes 196616 | tf_op jit(solution)/shard_map/ppermute | solution.py:25
  31.0 10.3 %collective-permute-start.10 = (bf16[128,1024]{0,1:T(8,128)(2,1)S(1)}, bf16[128,1024]{0,1:T(8,128)(2,1)S(1)}, u32[]{:S(2)}, u32[]{:S(2)}) collective-permute-start(bf16[128,1024]{0,1:T(8,128)(2,1)S(1)} %bitcast.47), channel_id=1, source_target_pairs={{0,24},{8,16},{16,8},{24,0},{1,25},{9,17},{17,9},{25,1},{2,26},{10... | collective-permute-start | bytes 786440 | tf_op jit(solution)/shard_map/ppermute | solution.py:25
  33.5 12.4 %collective-permute-start.9 = (bf16[128,1024]{0,1:T(8,128)(2,1)S(1)}, bf16[128,1024]{0,1:T(8,128)(2,1)S(1)}, u32[]{:S(2)}, u32[]{:S(2)}) collective-permute-start(bf16[128,1024]{0,1:T(8,128)(2,1)S(1)} %bitcast.46), channel_id=1, source_target_pairs={{0,16},{8,24},{16,0},{24,8},{1,17},{9,25},{17,1},{25,9},{2,18},{10... | collective-permute-start | bytes 786440 | tf_op jit(solution)/shard_map/ppermute | solution.py:25
  34.0 12.6 %collective-permute-start.8 = (bf16[128,1024]{0,1:T(8,128)(2,1)S(1)}, bf16[128,1024]{0,1:T(8,128)(2,1)S(1)}, u32[]{:S(2)}, u32[]{:S(2)}) collective-permute-start(bf16[128,1024]{0,1:T(8,128)(2,1)S(1)} %bitcast.45), channel_id=1, source_target_pairs={{0,8},{8,0},{16,24},{24,16},{1,9},{9,1},{17,25},{25,17},{2,10},{10... | collective-permute-start | bytes 786440 | tf_op jit(solution)/shard_map/ppermute | solution.py:25
  35.3 13.2 %copy-start.6 = (bf16[128,256]{1,0:T(8,128)(2,1)}, bf16[128,256]{1,0:T(8,128)(2,1)S(1)}, u32[]{:S(2)}) copy-start(bf16[128,256]{1,0:T(8,128)(2,1)S(1)} %fusion.15) | copy-start | bytes 196612
  35.3 12.0 %collective-permute-start.13 = (bf16[128,256]{1,0:T(8,128)(2,1)S(1)}, bf16[128,256]{1,0:T(8,128)(2,1)S(1)}, u32[]{:S(2)}, u32[]{:S(2)}) collective-permute-start(bf16[128,256]{1,0:T(8,128)(2,1)S(1)} %fusion.15), channel_id=1, source_target_pairs={{0,24},{8,16},{16,8},{24,0},{1,25},{9,17},{17,9},{25,1},{2,26},{10... | collective-permute-start | bytes 196616 | tf_op jit(solution)/shard_map/ppermute | solution.py:25
  37.8 10.1 %collective-permute-start.12 = (bf16[128,256]{1,0:T(8,128)(2,1)S(1)}, bf16[128,256]{1,0:T(8,128)(2,1)S(1)}, u32[]{:S(2)}, u32[]{:S(2)}) collective-permute-start(bf16[128,256]{1,0:T(8,128)(2,1)S(1)} %fusion.15), channel_id=1, source_target_pairs={{0,16},{8,24},{16,0},{24,8},{1,17},{9,25},{17,1},{25,9},{2,18},{10... | collective-permute-start | bytes 196616 | tf_op jit(solution)/shard_map/ppermute | solution.py:25
  41.2 6.7 %collective-permute-start.11 = (bf16[128,256]{1,0:T(8,128)(2,1)S(1)}, bf16[128,256]{1,0:T(8,128)(2,1)S(1)}, u32[]{:S(2)}, u32[]{:S(2)}) collective-permute-start(bf16[128,256]{1,0:T(8,128)(2,1)S(1)} %fusion.15), channel_id=1, source_target_pairs={{0,8},{8,0},{16,24},{24,16},{1,9},{9,1},{17,25},{25,17},{2,10},{10... | collective-permute-start | bytes 196616 | tf_op jit(solution)/shard_map/ppermute | solution.py:25
  48.5 1.6 %collective-permute-start.14 = (bf16[4,128,256]{2,1,0:T(8,128)(2,1)S(1)}, bf16[4,128,256]{2,1,0:T(8,128)(2,1)S(1)}, u32[]{:S(2)}, u32[]{:S(2)}) collective-permute-start(bf16[4,128,256]{2,1,0:T(8,128)(2,1)S(1)} %fusion.7), channel_id=1, source_target_pairs={{0,1},{1,0},{2,3},{3,2},{4,5},{5,4},{6,7},{7,6},{8,9},{9,8},{10,11... | collective-permute-start | bytes 786440 | tf_op jit(solution)/shard_map/ppermute | solution.py:25
  50.2 6.8 %collective-permute-start.17 = (bf16[128,256]{1,0:T(8,128)(2,1)S(1)}, bf16[128,256]{1,0:T(8,128)(2,1)S(1)}, u32[]{:S(2)}, u32[]{:S(2)}) collective-permute-start(bf16[128,256]{1,0:T(8,128)(2,1)S(1)} %get-tuple-element.16), channel_id=1, source_target_pairs={{0,6},{1,7},{2,4},{3,5},{4,2},{5,3},{6,0},{7,1},{8,14},{9,15},{10,... | collective-permute-start | bytes 196616 | tf_op jit(solution)/shard_map/ppermute | solution.py:25
  52.0 7.0 %collective-permute-start.16 = (bf16[128,256]{1,0:T(8,128)(2,1)S(1)}, bf16[128,256]{1,0:T(8,128)(2,1)S(1)}, u32[]{:S(2)}, u32[]{:S(2)}) collective-permute-start(bf16[128,256]{1,0:T(8,128)(2,1)S(1)} %get-tuple-element.17), channel_id=1, source_target_pairs={{0,4},{1,5},{2,6},{3,7},{4,0},{5,1},{6,2},{7,3},{8,12},{9,13},{10,... | collective-permute-start | bytes 196616 | tf_op jit(solution)/shard_map/ppermute | solution.py:25
  52.0 7.0 %collective-permute-start.15 = (bf16[128,256]{1,0:T(8,128)(2,1)S(1)}, bf16[128,256]{1,0:T(8,128)(2,1)S(1)}, u32[]{:S(2)}, u32[]{:S(2)}) collective-permute-start(bf16[128,256]{1,0:T(8,128)(2,1)S(1)} %get-tuple-element.15), channel_id=1, source_target_pairs={{0,2},{1,3},{2,0},{3,1},{4,6},{5,7},{6,4},{7,5},{8,10},{9,11},{10,... | collective-permute-start | bytes 196616 | tf_op jit(solution)/shard_map/ppermute | solution.py:25
  59.0 5.3 %collective-permute-start.20 = (bf16[128,256]{1,0:T(8,128)(2,1)S(1)}, bf16[128,256]{1,0:T(8,128)(2,1)S(1)}, u32[]{:S(2)}, u32[]{:S(2)}) collective-permute-start(bf16[128,256]{1,0:T(8,128)(2,1)S(1)} %fusion.18), channel_id=1, source_target_pairs={{0,24},{8,16},{16,8},{24,0},{1,25},{9,17},{17,9},{25,1},{2,26},{10... | collective-permute-start | bytes 196616 | tf_op jit(solution)/shard_map/ppermute | solution.py:25
  60.8 4.6 %collective-permute-start.19 = (bf16[128,256]{1,0:T(8,128)(2,1)S(1)}, bf16[128,256]{1,0:T(8,128)(2,1)S(1)}, u32[]{:S(2)}, u32[]{:S(2)}) collective-permute-start(bf16[128,256]{1,0:T(8,128)(2,1)S(1)} %fusion.18), channel_id=1, source_target_pairs={{0,16},{8,24},{16,0},{24,8},{1,17},{9,25},{17,1},{25,9},{2,18},{10... | collective-permute-start | bytes 196616 | tf_op jit(solution)/shard_map/ppermute | solution.py:25
  62.0 4.3 %collective-permute-start.18 = (bf16[128,256]{1,0:T(8,128)(2,1)S(1)}, bf16[128,256]{1,0:T(8,128)(2,1)S(1)}, u32[]{:S(2)}, u32[]{:S(2)}) collective-permute-start(bf16[128,256]{1,0:T(8,128)(2,1)S(1)} %fusion.18), channel_id=1, source_target_pairs={{0,8},{8,0},{16,24},{24,16},{1,9},{9,1},{17,25},{25,17},{2,10},{10... | collective-permute-start | bytes 196616 | tf_op jit(solution)/shard_map/ppermute | solution.py:25

commit v2 on v1

--- a/solution.py
+++ b/solution.py
@@ -26,22 +26,19 @@
 
 
 def attention_kernel(half, local, pieces, *refs):
-    (len_ref, me_ref), kv_refs = refs[:2], refs[2 : 2 + half + 1]
-    q_ref, do_ref = refs[3 + half : 5 + half]
-    gq_ref, own_ref, sib_ref = refs[5 + half : 8 + half]
-    k_all, v_all, bias, x_buf, dp_buf, p_buf, ds_buf = refs[8 + half :]
     stripes = 2 * half
+    (len_ref, me_ref), kv_refs = refs[:2], refs[2 : 2 + stripes]
+    q_ref, do_ref, gq_ref, own_ref, sib_ref = refs[2 + stripes : 7 + stripes]
+    k_all, v_all, bias, x_bufs, dp_bufs, p_buf, ds_buf = refs[7 + stripes :]
     me = me_ref[0]
     heads = q_ref.shape[1] // HD
     per_group = RESPONSES + 1
     coef = HD**-0.5 * LOG2E
 
-    for k in range(half):
+    for k in range(stripes):
         rows = slice(k * local, (k + 1) * local)
         k_all[rows, :] = kv_refs[k][:, :HD]
         v_all[rows, :] = kv_refs[k][:, HD:]
-    k_all[half * local :, :] = kv_refs[half][:, :HD]
-    v_all[half * local :, :] = kv_refs[half][:, HD:]
 
     q_pos = lax.broadcasted_iota(jnp.int32, (1, local), 1) * stripes + me
     own_start = jnp.zeros((1, local), jnp.int32)
@@ -67,7 +64,9 @@
         bias[m * local : (m + 1) * local, :] = jnp.where(ok, 0.0, NEG)
 
     def head_pair(hp, _):
-        c0 = pl.multiple_of(hp * 2 * HD, 2 * HD)
+        c0 = hp * 2 * HD
+        x_buf = x_bufs.at[hp]
+        dp_buf = dp_bufs.at[hp]
         q2 = jnp.concatenate(
             [q_ref[:, pl.ds(c0, HD)], q_ref[:, pl.ds(c0 + HD, HD)]], axis=0
         )
@@ -103,14 +102,14 @@
             ds = p * (dp_buf[rows, :] - delta)
             p_buf[rows, pl.ds(c0, 2 * HD)] = p.astype(jnp.bfloat16)
             ds_buf[rows, pl.ds(c0, 2 * HD)] = ds.astype(jnp.bfloat16)
-        gq = dot(ds_buf[:, pl.ds(c0, 2 * HD)], k_all[...], TN) * HD**-0.5
-        gq = gq.astype(jnp.bfloat16)
-        gq_ref[:, pl.ds(c0, HD)] = gq[:local]
-        gq_ref[:, pl.ds(c0 + HD, HD)] = gq[local:]
         return 0
 
-    lax.fori_loop(0, heads // 2, head_pair, 0)
-
+    for hp in range(heads // 2):
+        head_pair(hp, 0)
+
+    gq = (dot(k_all[...].T, ds_buf[...]).T * HD**-0.5).astype(jnp.bfloat16)
+    for h in range(heads):
+        gq_ref[:, h * HD : (h + 1) * HD] = gq[h * local : (h + 1) * local]
     q_rows = jnp.concatenate([q_ref[:, h * HD : (h + 1) * HD] for h in range(heads)], axis=0)
     do_rows = jnp.concatenate([do_ref[:, h * HD : (h + 1) * HD] for h in range(heads)], axis=0)
     half_rows = half * local
@@ -121,7 +120,7 @@
 
 
 def attention(lengths, me, kv_blocks, q, do):
-    half = len(kv_blocks) - 1
+    half = len(kv_blocks) // 2
     local, width = q.shape
     keys = 2 * half * local
     heads = width // HD
@@ -134,18 +133,19 @@
             jax.ShapeDtypeStruct((half * local, 2 * HD), jnp.float32),
             jax.ShapeDtypeStruct((half * local, 2 * HD), jnp.bfloat16),
         ),
-        in_specs=[sm, sm] + [vm] * (half + 3),
+        in_specs=[sm, sm] + [vm] * (2 * half + 2),
         out_specs=(vm, vm, vm),
         scratch_shapes=[
             pltpu.VMEM((keys, HD), jnp.bfloat16),
             pltpu.VMEM((keys, HD), jnp.bfloat16),
             pltpu.VMEM((keys, local), jnp.float32),
-            pltpu.VMEM((keys, 2 * local), jnp.float32),
-            pltpu.VMEM((keys, 2 * local), jnp.float32),
+            pltpu.VMEM((heads // 2, keys, 2 * local), jnp.float32),
+            pltpu.VMEM((heads // 2, keys, 2 * local), jnp.float32),
             pltpu.VMEM((keys, heads * local), jnp.bfloat16),
             pltpu.VMEM((keys, heads * local), jnp.bfloat16),
         ],
-        compiler_params=pltpu.CompilerParams(vmem_limit_bytes=56 * 1024 * 1024),
+        cost_estimate=pl.CostEstimate(flops=1000000000, bytes_accessed=0, transcendentals=0),
+        compiler_params=pltpu.CompilerParams(vmem_limit_bytes=keys * 24 * 1024),
     )(lengths, me, *kv_blocks, q, do)
 
 
@@ -163,7 +163,7 @@
     part = features // (stripes * rows)
 
     kv_own = [kv] + [swap(kv, "ctx", 2 * k) for k in range(1, half)]
-    kv_sib = swap(jnp.concatenate(kv_own, axis=0), "ctx", 1)
+    kv_sib = [swap(block, "ctx", 1) for block in kv_own]
 
     xb = x.reshape(local, stripes, rows, part)
     x_slabs = []
@@ -173,8 +173,10 @@
         x_slabs.append(slab if k == 0 else swap(slab, "dp", k))
 
     gq, part_own, part_sib = attention(
-        lengths, me.reshape(1).astype(jnp.int32), kv_own + [kv_sib], q, do
+        lengths, me.reshape(1).astype(jnp.int32), kv_own + kv_sib, q, do
     )
+
+    part_sib, x_slabs = lax.optimization_barrier((part_sib, x_slabs))
 
     chip = part_own + swap(part_sib, "ctx", 1).astype(jnp.float32)
     chip = chip.reshape(half, local, 2 * HD)
@@ -198,9 +200,13 @@
         w_mine = w_mine + swap(block.astype(jnp.bfloat16), "ctx", 2 * k).astype(jnp.float32)
 
     low = w_mine.astype(jnp.bfloat16)
-    stacked = jnp.stack([low] + [swap(low, "dp", k) for k in range(1, rows)])
-    order = jnp.arange(rows) ^ row
-    w_out = stacked[order].reshape(rows * part, 2 * HD).astype(jnp.float32)
+    blocks = [low] + [swap(low, "dp", k) for k in range(1, rows)]
+    bit = 1
+    while bit < rows:
+        flip = (row & bit) != 0
+        blocks = [jnp.where(flip, blocks[j ^ bit], blocks[j]) for j in range(rows)]
+        bit *= 2
+    w_out = jnp.concatenate([b.astype(jnp.float32) for b in blocks], axis=0)
     return (
         gq.reshape(1, 1, local, -1),
         gkv.reshape(1, 1, local, 2 * HD),

time: 68 us -> 61.6 us (0.906)
  Pallas kernels: 8.78 us -> 5.29 us
  starting transfers between devices: 26.7 us -> 25.7 us
  other arithmetic: 1.95 us -> 1.06 us
  waiting for transfers between devices: 27 us -> 26.3 us
    pallas_call x1, Pallas kernels: 8.78 us -> 5.29 us  [attention(): pl.pallas_call(functools.partial(attention_kernel, half, local, lengths.s...]
    ppermute x21 -> x24, starting transfers between devices: 26.7 us -> 25.7 us  [swap(): return lax.ppermute(x, axis, [(i, i ^ mask) for i in range(size)])]
    convert_element_type x1 -> x0, other arithmetic: 0.85 us -> none  [on_device(): w_out = stacked[order].reshape(rows * part, 2 * HD).astype(jnp.float32)]
    ppermute x21 -> x24, waiting for transfers between devices: 27 us -> 26.3 us  [swap(): return lax.ppermute(x, axis, [(i, i ^ mask) for i in range(size)])]
    unnamed x15 -> x11, local copies, waits for them, and re-layouts: 1.36 us -> 1.68 us
  transfers between devices with their start and end apart: 21 -> 24, of which waited for: 17 -> 18; matrix products, arithmetic and copies ran while one was open for 1% -> 3% of each run, Pallas kernels for 0% -> 9%
where the time goes in v2:
time: 61.6 us; the launch traced here: 61.5 us
  waiting for transfers between devices  26.3 us (43%)
  starting transfers between devices  25.7 us (42%)
  Pallas kernels  5.29 us (9%)
  local copies, waits for them, and re-layouts  1.86 us (3%)
  other arithmetic  1.06 us (2%)
  between operations  0.84 us (1%)
    ppermute x24, waiting for transfers between devices, swap(): return lax.ppermute(x, axis, [(i, i ^ mask) for i in range(size)])  26.3 us
    ppermute x24, starting transfers between devices, swap(): return lax.ppermute(x, axis, [(i, i ^ mask) for i in range(size)])  25.7 us
    pallas_call x1, Pallas kernels, attention(): pl.pallas_call(functools.partial(attention_kernel, half, local, lengths.s...  5.29 us
    unnamed x11, local copies, waits for them, and re-layouts  1.68 us
  transfers between devices with their start and end apart: 24, of which 18 were waited for; matrix products, arithmetic and copies ran while one was open for 3% of the time, Pallas kernels for 9%

profile of v2, /device:TPU:0, one launch (start us, length us, event | category | flops | bytes accessed | tf_op | source)
XLA Modules:
  0.0 61.5 jit_solution(13428418592771052155)
XLA Ops:
  0.6 3.1 %collective-permute-start = (bf16[128,256]{1,0:T(8,128)(2,1)}, bf16[128,256]{1,0:T(8,128)(2,1)S(1)}, u32[]{:S(2)}, u32[]{:S(2)}) collective-permute-start(bf16[128,256]{1,0:T(8,128)(2,1)} %bitcast.36), channel_id=1, source_target_pairs={{0,2},{1,3},{2,0},{3,1},{4,6},{5,7},{6,4},{7,5},{8,10},{9,11},{10,... | collective-permute-start | bytes 196616 | tf_op jit(solution)/shard_map/ppermute | solution.py:25
  3.7 2.6 %collective-permute-start.1 = (bf16[128,256]{1,0:T(8,128)(2,1)}, bf16[128,256]{1,0:T(8,128)(2,1)S(1)}, u32[]{:S(2)}, u32[]{:S(2)}) collective-permute-start(bf16[128,256]{1,0:T(8,128)(2,1)} %bitcast.37), channel_id=1, source_target_pairs={{0,4},{1,5},{2,6},{3,7},{4,0},{5,1},{6,2},{7,3},{8,12},{9,13},{10,... | collective-permute-start | bytes 196616 | tf_op jit(solution)/shard_map/ppermute | solution.py:25
  6.3 1.6 %copy.10 = bf16[1,1,128,4096]{2,3,1,0:T(8,128)(2,1)S(1)} copy(bf16[1,1,128,4096]{3,2,1,0:T(8,128)(2,1)} %param.5) | data formatting | bytes 2097152 | tf_op args[0]
  8.0 0.0 copy-start
  8.0 0.0 copy-start.1
  8.0 0.1 constant_dynamic-slice_fusion
  8.1 1.8 %collective-permute-start.7 = (bf16[128,1024]{0,1:T(8,128)(2,1)S(1)}, bf16[128,1024]{0,1:T(8,128)(2,1)S(1)}, u32[]{:S(2)}, u32[]{:S(2)}) collective-permute-start(bf16[128,1024]{0,1:T(8,128)(2,1)S(1)} %bitcast.47), channel_id=1, source_target_pairs={{0,8},{8,0},{16,24},{24,16},{1,9},{9,1},{17,25},{25,17},{2,10},{10... | collective-permute-start | bytes 786440 | tf_op jit(solution)/shard_map/ppermute | solution.py:25
  9.9 1.5 %collective-permute-start.8 = (bf16[128,1024]{0,1:T(8,128)(2,1)S(1)}, bf16[128,1024]{0,1:T(8,128)(2,1)S(1)}, u32[]{:S(2)}, u32[]{:S(2)}) collective-permute-start(bf16[128,1024]{0,1:T(8,128)(2,1)S(1)} %bitcast.46), channel_id=1, source_target_pairs={{0,16},{8,24},{16,0},{24,8},{1,17},{9,25},{17,1},{25,9},{2,18},{10... | collective-permute-start | bytes 786440 | tf_op jit(solution)/shard_map/ppermute | solution.py:25
  11.4 0.3 collective-permute-start.9
  11.7 0.9 %collective-permute-done.2.refs_5_ = bf16[128,256]{1,0:T(8,128)(2,1)S(1)} collective-permute-done((bf16[128,256]{1,0:T(8,128)(2,1)}, bf16[128,256]{1,0:T(8,128)(2,1)S(1)}, u32[]{:S(2)}, u32[]{:S(2)}) %collective-permute-start.2) | collective-permute-done | bytes 65568 | tf_op jit(solution)/shard_map/ppermute | solution.py:25
  12.6 0.3 collective-permute-done.3.refs_6_
  13.0 0.2 collective-permute-start.5
  13.1 0.7 %collective-permute-done.4.refs_7_ = bf16[128,256]{1,0:T(8,128)(2,1)S(1)} collective-permute-done((bf16[128,256]{1,0:T(8,128)(2,1)S(1)}, bf16[128,256]{1,0:T(8,128)(2,1)S(1)}, u32[]{:S(2)}, u32[]{:S(2)}) %collective-permute-start.4) | collective-permute-done | bytes 65568 | tf_op jit(solution)/shard_map/ppermute | solution.py:25
  13.9 0.2 collective-permute-start.6
  14.0 0.2 collective-permute-done.5.refs_8_
  14.2 0.9 %collective-permute-done.6.refs_9_ = bf16[128,256]{1,0:T(8,128)(2,1)S(1)} collective-permute-done((bf16[128,256]{1,0:T(8,128)(2,1)S(1)}, bf16[128,256]{1,0:T(8,128)(2,1)S(1)}, u32[]{:S(2)}, u32[]{:S(2)}) %collective-permute-start.6) | collective-permute-done | bytes 65568 | tf_op jit(solution)/shard_map/ppermute | solution.py:25
  15.1 5.3 %shard_map.76 = (bf16[128,1024]{1,0:T(8,128)(2,1)}, f32[512,256]{1,0:T(8,128)S(1)}, bf16[512,256]{1,0:T(8,128)(2,1)S(1)}) custom-call(s32[1,10]{1,0:T(1,128)S(1)} %copy-done.3, s32[1]{0:T(128)} %bitcast.refs_1_, bf16[128,256]{1,0:T(8,128)(2,1)S(1)} %bitcast.40, bf16[128,256]{1,0:T(8,128)(2,1)S(1)} %collective-permute-done.refs_3_, ...), custom_call_target="tpu_custom_call" | custom-call | flops 1000000000 | tf_op jit(solution)/shard_map/pallas_call | solution.py:129
  20.4 2.1 %collective-permute-done.8 = bf16[128,1024]{0,1:T(8,128)(2,1)S(1)} collective-permute-done((bf16[128,1024]{0,1:T(8,128)(2,1)S(1)}, bf16[128,1024]{0,1:T(8,128)(2,1)S(1)}, u32[]{:S(2)}, u32[]{:S(2)}) %collective-permute-start.8) | collective-permute-done | bytes 262176 | tf_op jit(solution)/shard_map/ppermute | solution.py:25
  22.5 1.5 %collective-permute-done.10 = bf16[512,256]{1,0:T(8,128)(2,1)S(1)} collective-permute-done((bf16[512,256]{1,0:T(8,128)(2,1)S(1)}, bf16[512,256]{1,0:T(8,128)(2,1)S(1)}, u32[]{:S(2)}, u32[]{:S(2)}) %collective-permute-start.10) | collective-permute-done | bytes 262176 | tf_op jit(solution)/shard_map/ppermute | solution.py:25
  24.1 0.1 fusion.23
  24.2 0.7 %collective-permute-start.11 = (bf16[128,256]{1,0:T(8,128)(2,1)S(1)}, bf16[128,256]{1,0:T(8,128)(2,1)S(1)}, u32[]{:S(2)}, u32[]{:S(2)}) collective-permute-start(bf16[128,256]{1,0:T(8,128)(2,1)S(1)} %get-tuple-element.32), channel_id=1, source_target_pairs={{0,2},{1,3},{2,0},{3,1},{4,6},{5,7},{6,4},{7,5},{8,10},{9,11},{10,... | collective-permute-start | bytes 196616 | tf_op jit(solution)/shard_map/ppermute | solution.py:25
  24.8 3.5 %collective-permute-start.12 = (bf16[128,256]{1,0:T(8,128)(2,1)S(1)}, bf16[128,256]{1,0:T(8,128)(2,1)S(1)}, u32[]{:S(2)}, u32[]{:S(2)}) collective-permute-start(bf16[128,256]{1,0:T(8,128)(2,1)S(1)} %get-tuple-element.34), channel_id=1, source_target_pairs={{0,4},{1,5},{2,6},{3,7},{4,0},{5,1},{6,2},{7,3},{8,12},{9,13},{10,... | collective-permute-start | bytes 196616 | tf_op jit(solution)/shard_map/ppermute | solution.py:25
  28.3 0.3 collective-permute-start.13
  28.6 3.8 %collective-permute-done.12 = bf16[128,256]{1,0:T(8,128)(2,1)S(1)} collective-permute-done((bf16[128,256]{1,0:T(8,128)(2,1)S(1)}, bf16[128,256]{1,0:T(8,128)(2,1)S(1)}, u32[]{:S(2)}, u32[]{:S(2)}) %collective-permute-start.12) | collective-permute-done | bytes 65568 | tf_op jit(solution)/shard_map/ppermute | solution.py:25
  32.4 2.1 %collective-permute-done.13 = bf16[128,256]{1,0:T(8,128)(2,1)S(1)} collective-permute-done((bf16[128,256]{1,0:T(8,128)(2,1)S(1)}, bf16[128,256]{1,0:T(8,128)(2,1)S(1)}, u32[]{:S(2)}, u32[]{:S(2)}) %collective-permute-start.13) | collective-permute-done | bytes 65568 | tf_op jit(solution)/shard_map/ppermute | solution.py:25
  34.5 0.0 copy-start.4
  34.6 1.3 %collective-permute-start.14 = (bf16[128,256]{1,0:T(8,128)(2,1)S(1)}, bf16[128,256]{1,0:T(8,128)(2,1)S(1)}, u32[]{:S(2)}, u32[]{:S(2)}) collective-permute-start(bf16[128,256]{1,0:T(8,128)(2,1)S(1)} %fusion.15), channel_id=1, source_target_pairs={{0,8},{8,0},{16,24},{24,16},{1,9},{9,1},{17,25},{25,17},{2,10},{10... | collective-permute-start | bytes 196616 | tf_op jit(solution)/shard_map/ppermute | solution.py:25
  35.9 0.8 %collective-permute-start.15 = (bf16[128,256]{1,0:T(8,128)(2,1)S(1)}, bf16[128,256]{1,0:T(8,128)(2,1)S(1)}, u32[]{:S(2)}, u32[]{:S(2)}) collective-permute-start(bf16[128,256]{1,0:T(8,128)(2,1)S(1)} %fusion.15), channel_id=1, source_target_pairs={{0,16},{8,24},{16,0},{24,8},{1,17},{9,25},{17,1},{25,9},{2,18},{10... | collective-permute-start | bytes 196616 | tf_op jit(solution)/shard_map/ppermute | solution.py:25
  36.7 1.4 %collective-permute-start.16 = (bf16[128,256]{1,0:T(8,128)(2,1)S(1)}, bf16[128,256]{1,0:T(8,128)(2,1)S(1)}, u32[]{:S(2)}, u32[]{:S(2)}) collective-permute-start(bf16[128,256]{1,0:T(8,128)(2,1)S(1)} %fusion.15), channel_id=1, source_target_pairs={{0,24},{8,16},{16,8},{24,0},{1,25},{9,17},{17,9},{25,1},{2,26},{10... | collective-permute-start | bytes 196616 | tf_op jit(solution)/shard_map/ppermute | solution.py:25
  38.1 1.1 %collective-permute-done.14 = bf16[128,256]{1,0:T(8,128)(2,1)S(1)} collective-permute-done((bf16[128,256]{1,0:T(8,128)(2,1)S(1)}, bf16[128,256]{1,0:T(8,128)(2,1)S(1)}, u32[]{:S(2)}, u32[]{:S(2)}) %collective-permute-start.14) | collective-permute-done | bytes 65568 | tf_op jit(solution)/shard_map/ppermute | solution.py:25
  39.2 0.9 %collective-permute-done.15 = bf16[128,256]{1,0:T(8,128)(2,1)S(1)} collective-permute-done((bf16[128,256]{1,0:T(8,128)(2,1)S(1)}, bf16[128,256]{1,0:T(8,128)(2,1)S(1)}, u32[]{:S(2)}, u32[]{:S(2)}) %collective-permute-start.15) | collective-permute-done | bytes 65568 | tf_op jit(solution)/shard_map/ppermute | solution.py:25
  40.1 1.7 %collective-permute-done.16 = bf16[128,256]{1,0:T(8,128)(2,1)S(1)} collective-permute-done((bf16[128,256]{1,0:T(8,128)(2,1)S(1)}, bf16[128,256]{1,0:T(8,128)(2,1)S(1)}, u32[]{:S(2)}, u32[]{:S(2)}) %collective-permute-start.16) | collective-permute-done | bytes 65568 | tf_op jit(solution)/shard_map/ppermute | solution.py:25
  41.8 0.4 convolution_multiply_fusion
  42.3 0.1 collective-permute-start.17
  42.5 1.5 %collective-permute-done.17 = bf16[4,128,256]{2,1,0:T(8,128)(2,1)S(1)} collective-permute-done((bf16[4,128,256]{2,1,0:T(8,128)(2,1)S(1)}, bf16[4,128,256]{2,1,0:T(8,128)(2,1)S(1)}, u32[]{:S(2)}, u32[]{:S(2)}) %collective-permute-start.17) | collective-permute-done | bytes 262176 | tf_op jit(solution)/shard_map/ppermute | solution.py:25
  43.9 0.1 bitcast_add_fusion
  44.0 0.8 %collective-permute-start.18 = (bf16[128,256]{1,0:T(8,128)(2,1)S(1)}, bf16[128,256]{1,0:T(8,128)(2,1)S(1)}, u32[]{:S(2)}, u32[]{:S(2)}) collective-permute-start(bf16[128,256]{1,0:T(8,128)(2,1)S(1)} %get-tuple-element.25), channel_id=1, source_target_pairs={{0,2},{1,3},{2,0},{3,1},{4,6},{5,7},{6,4},{7,5},{8,10},{9,11},{10,... | collective-permute-start | bytes 196616 | tf_op jit(solution)/shard_map/ppermute | solution.py:25
  44.9 1.7 %collective-permute-start.19 = (bf16[128,256]{1,0:T(8,128)(2,1)S(1)}, bf16[128,256]{1,0:T(8,128)(2,1)S(1)}, u32[]{:S(2)}, u32[]{:S(2)}) collective-permute-start(bf16[128,256]{1,0:T(8,128)(2,1)S(1)} %get-tuple-element.27), channel_id=1, source_target_pairs={{0,4},{1,5},{2,6},{3,7},{4,0},{5,1},{6,2},{7,3},{8,12},{9,13},{10,... | collective-permute-start | bytes 196616 | tf_op jit(solution)/shard_map/ppermute | solution.py:25
  46.6 1.9 %collective-permute-start.20 = (bf16[128,256]{1,0:T(8,128)(2,1)S(1)}, bf16[128,256]{1,0:T(8,128)(2,1)S(1)}, u32[]{:S(2)}, u32[]{:S(2)}) collective-permute-start(bf16[128,256]{1,0:T(8,128)(2,1)S(1)} %get-tuple-element.26), channel_id=1, source_target_pairs={{0,6},{1,7},{2,4},{3,5},{4,2},{5,3},{6,0},{7,1},{8,14},{9,15},{10,... | collective-permute-start | bytes 196616 | tf_op jit(solution)/shard_map/ppermute | solution.py:25
  48.5 0.6 collective-permute-done.18
  49.1 4.2 %collective-permute-done.19 = bf16[128,256]{1,0:T(8,128)(2,1)S(1)} collective-permute-done((bf16[128,256]{1,0:T(8,128)(2,1)S(1)}, bf16[128,256]{1,0:T(8,128)(2,1)S(1)}, u32[]{:S(2)}, u32[]{:S(2)}) %collective-permute-start.19) | collective-permute-done | bytes 65568 | tf_op jit(solution)/shard_map/ppermute | solution.py:25
  53.3 1.5 %collective-permute-start.21 = (bf16[128,256]{1,0:T(8,128)(2,1)S(1)}, bf16[128,256]{1,0:T(8,128)(2,1)S(1)}, u32[]{:S(2)}, u32[]{:S(2)}) collective-permute-start(bf16[128,256]{1,0:T(8,128)(2,1)S(1)} %fusion.18), channel_id=1, source_target_pairs={{0,24},{8,16},{16,8},{24,0},{1,25},{9,17},{17,9},{25,1},{2,26},{10... | collective-permute-start | bytes 196616 | tf_op jit(solution)/shard_map/ppermute | solution.py:25
  54.8 1.5 %collective-permute-start.22 = (bf16[128,256]{1,0:T(8,128)(2,1)S(1)}, bf16[128,256]{1,0:T(8,128)(2,1)S(1)}, u32[]{:S(2)}, u32[]{:S(2)}) collective-permute-start(bf16[128,256]{1,0:T(8,128)(2,1)S(1)} %fusion.18), channel_id=1, source_target_pairs={{0,16},{8,24},{16,0},{24,8},{1,17},{9,25},{17,1},{25,9},{2,18},{10... | collective-permute-start | bytes 196616 | tf_op jit(solution)/shard_map/ppermute | solution.py:25
  56.3 0.5 collective-permute-start.23
  56.9 1.7 %collective-permute-done.21 = bf16[128,256]{1,0:T(8,128)(2,1)S(1)} collective-permute-done((bf16[128,256]{1,0:T(8,128)(2,1)S(1)}, bf16[128,256]{1,0:T(8,128)(2,1)S(1)}, u32[]{:S(2)}, u32[]{:S(2)}) %collective-permute-start.21) | collective-permute-done | bytes 65568 | tf_op jit(solution)/shard_map/ppermute | solution.py:25
  58.6 0.7 %collective-permute-done.22 = bf16[128,256]{1,0:T(8,128)(2,1)S(1)} collective-permute-done((bf16[128,256]{1,0:T(8,128)(2,1)S(1)}, bf16[128,256]{1,0:T(8,128)(2,1)S(1)}, u32[]{:S(2)}, u32[]{:S(2)}) %collective-permute-start.22) | collective-permute-done | bytes 65568 | tf_op jit(solution)/shard_map/ppermute | solution.py:25
  59.2 1.4 %collective-permute-done.23 = bf16[128,256]{1,0:T(8,128)(2,1)S(1)} collective-permute-done((bf16[128,256]{1,0:T(8,128)(2,1)S(1)}, bf16[128,256]{1,0:T(8,128)(2,1)S(1)}, u32[]{:S(2)}, u32[]{:S(2)}) %collective-permute-start.23) | collective-permute-done | bytes 65568 | tf_op jit(solution)/shard_map/ppermute | solution.py:25
  60.6 0.8 %maximum_convert_fusion = f32[512,256]{1,0:T(8,128)} fusion(bf16[128,256]{1,0:T(8,128)(2,1)S(1)} %get-tuple-element.31, bf16[128,256]{1,0:T(8,128)(2,1)S(1)} %get-tuple-element.30, bf16[128,256]{1,0:T(8,128)(2,1)S(1)} %get-tuple-element.29, bf16[128,256]{1,0:T(8,128)(2,1)S(1)} %get-tuple-element.28), kind=kLoop, calls=%fused_computation.19 | loop fusion | flops 1048576 | bytes 786432 | tf_op jit(solution)/shard_map/concatenate | solution.py:209
  (23 shorter events, 0.2 us)
Async XLA Ops:
  0.6 10.8 %collective-permute-start = (bf16[128,256]{1,0:T(8,128)(2,1)}, bf16[128,256]{1,0:T(8,128)(2,1)S(1)}, u32[]{:S(2)}, u32[]{:S(2)}) collective-permute-start(bf16[128,256]{1,0:T(8,128)(2,1)} %bitcast.36), channel_id=1, source_target_pairs={{0,2},{1,3},{2,0},{3,1},{4,6},{5,7},{6,4},{7,5},{8,10},{9,11},{10,... | collective-permute-start | bytes 196616 | tf_op jit(solution)/shard_map/ppermute | solution.py:25
  3.7 8.0 %collective-permute-start.1 = (bf16[128,256]{1,0:T(8,128)(2,1)}, bf16[128,256]{1,0:T(8,128)(2,1)S(1)}, u32[]{:S(2)}, u32[]{:S(2)}) collective-permute-start(bf16[128,256]{1,0:T(8,128)(2,1)} %bitcast.37), channel_id=1, source_target_pairs={{0,4},{1,5},{2,6},{3,7},{4,0},{5,1},{6,2},{7,3},{8,12},{9,13},{10,... | collective-permute-start | bytes 196616 | tf_op jit(solution)/shard_map/ppermute | solution.py:25
  6.3 6.3 %collective-permute-start.2 = (bf16[128,256]{1,0:T(8,128)(2,1)}, bf16[128,256]{1,0:T(8,128)(2,1)S(1)}, u32[]{:S(2)}, u32[]{:S(2)}) collective-permute-start(bf16[128,256]{1,0:T(8,128)(2,1)} %bitcast.38), channel_id=1, source_target_pairs={{0,6},{1,7},{2,4},{3,5},{4,2},{5,3},{6,0},{7,1},{8,14},{9,15},{10,... | collective-permute-start | bytes 196616 | tf_op jit(solution)/shard_map/ppermute | solution.py:25
  8.0 3.7 %copy-start.2 = (bf16[1,1,128,256]{3,2,1,0:T(8,128)(2,1)S(1)}, bf16[1,1,128,256]{3,2,1,0:T(8,128)(2,1)}, u32[]{:S(2)}) copy-start(bf16[1,1,128,256]{3,2,1,0:T(8,128)(2,1)} %param.7) | copy-start | bytes 196612
  8.0 7.1 %copy-start = (bf16[1,1,128,1024]{3,2,1,0:T(8,128)(2,1)S(1)}, bf16[1,1,128,1024]{3,2,1,0:T(8,128)(2,1)}, u32[]{:S(2)}) copy-start(bf16[1,1,128,1024]{3,2,1,0:T(8,128)(2,1)} %param.6) | copy-start | bytes 786436
  8.0 7.1 %copy-start.1 = (bf16[1,1,128,1024]{3,2,1,0:T(8,128)(2,1)S(1)}, bf16[1,1,128,1024]{3,2,1,0:T(8,128)(2,1)}, u32[]{:S(2)}) copy-start(bf16[1,1,128,1024]{3,2,1,0:T(8,128)(2,1)} %param.8) | copy-start | bytes 786436
  8.0 7.1 %copy-start.3 = (s32[1,10]{1,0:T(1,128)S(1)}, s32[1,10]{1,0:T(1,128)}, u32[]{:S(2)}) copy-start(s32[1,10]{1,0:T(1,128)} %refs_0_.1) | copy-start | bytes 124
  8.1 12.3 %collective-permute-start.7 = (bf16[128,1024]{0,1:T(8,128)(2,1)S(1)}, bf16[128,1024]{0,1:T(8,128)(2,1)S(1)}, u32[]{:S(2)}, u32[]{:S(2)}) collective-permute-start(bf16[128,1024]{0,1:T(8,128)(2,1)S(1)} %bitcast.47), channel_id=1, source_target_pairs={{0,8},{8,0},{16,24},{24,16},{1,9},{9,1},{17,25},{25,17},{2,10},{10... | collective-permute-start | bytes 786440 | tf_op jit(solution)/shard_map/ppermute | solution.py:25
  9.9 12.6 %collective-permute-start.8 = (bf16[128,1024]{0,1:T(8,128)(2,1)S(1)}, bf16[128,1024]{0,1:T(8,128)(2,1)S(1)}, u32[]{:S(2)}, u32[]{:S(2)}) collective-permute-start(bf16[128,1024]{0,1:T(8,128)(2,1)S(1)} %bitcast.46), channel_id=1, source_target_pairs={{0,16},{8,24},{16,0},{24,8},{1,17},{9,25},{17,1},{25,9},{2,18},{10... | collective-permute-start | bytes 786440 | tf_op jit(solution)/shard_map/ppermute | solution.py:25
  11.4 11.1 %collective-permute-start.9 = (bf16[128,1024]{0,1:T(8,128)(2,1)S(1)}, bf16[128,1024]{0,1:T(8,128)(2,1)S(1)}, u32[]{:S(2)}, u32[]{:S(2)}) collective-permute-start(bf16[128,1024]{0,1:T(8,128)(2,1)S(1)} %bitcast.45), channel_id=1, source_target_pairs={{0,24},{8,16},{16,8},{24,0},{1,25},{9,17},{17,9},{25,1},{2,26},{10... | collective-permute-start | bytes 786440 | tf_op jit(solution)/shard_map/ppermute | solution.py:25
  11.7 1.3 %collective-permute-start.3 = (bf16[128,256]{1,0:T(8,128)(2,1)S(1)}, bf16[128,256]{1,0:T(8,128)(2,1)S(1)}, u32[]{:S(2)}, u32[]{:S(2)}) collective-permute-start(bf16[128,256]{1,0:T(8,128)(2,1)S(1)} %bitcast.39), channel_id=1, source_target_pairs={{0,1},{1,0},{2,3},{3,2},{4,5},{5,4},{6,7},{7,6},{8,9},{9,8},{10,11... | collective-permute-start | bytes 196616 | tf_op jit(solution)/shard_map/ppermute | solution.py:25
  12.6 1.3 %collective-permute-start.4 = (bf16[128,256]{1,0:T(8,128)(2,1)S(1)}, bf16[128,256]{1,0:T(8,128)(2,1)S(1)}, u32[]{:S(2)}, u32[]{:S(2)}) collective-permute-start(bf16[128,256]{1,0:T(8,128)(2,1)S(1)} %collective-permute-done.refs_3_), channel_id=1, source_target_pairs={{0,1},{1,0},{2,3},{3,2},{4,5},{5,4},{6,7},{7,6},{8,9},{9,8},{10,11... | collective-permute-start | bytes 196616 | tf_op jit(solution)/shard_map/ppermute | solution.py:25
  13.0 1.3 %collective-permute-start.5 = (bf16[128,256]{1,0:T(8,128)(2,1)S(1)}, bf16[128,256]{1,0:T(8,128)(2,1)S(1)}, u32[]{:S(2)}, u32[]{:S(2)}) collective-permute-start(bf16[128,256]{1,0:T(8,128)(2,1)S(1)} %collective-permute-done.1.refs_4_), channel_id=1, source_target_pairs={{0,1},{1,0},{2,3},{3,2},{4,5},{5,4},{6,7},{7,6},{8,9},{9,8},{10,11... | collective-permute-start | bytes 196616 | tf_op jit(solution)/shard_map/ppermute | solution.py:25
  13.9 1.3 %collective-permute-start.6 = (bf16[128,256]{1,0:T(8,128)(2,1)S(1)}, bf16[128,256]{1,0:T(8,128)(2,1)S(1)}, u32[]{:S(2)}, u32[]{:S(2)}) collective-permute-start(bf16[128,256]{1,0:T(8,128)(2,1)S(1)} %collective-permute-done.2.refs_5_), channel_id=1, source_target_pairs={{0,1},{1,0},{2,3},{3,2},{4,5},{5,4},{6,7},{7,6},{8,9},{9,8},{10,11... | collective-permute-start | bytes 196616 | tf_op jit(solution)/shard_map/ppermute | solution.py:25
  22.5 1.5 %collective-permute-start.10 = (bf16[512,256]{1,0:T(8,128)(2,1)S(1)}, bf16[512,256]{1,0:T(8,128)(2,1)S(1)}, u32[]{:S(2)}, u32[]{:S(2)}) collective-permute-start(bf16[512,256]{1,0:T(8,128)(2,1)S(1)} %get-tuple-element.14), channel_id=1, source_target_pairs={{0,1},{1,0},{2,3},{3,2},{4,5},{5,4},{6,7},{7,6},{8,9},{9,8},{10,11... | collective-permute-start | bytes 786440 | tf_op jit(solution)/shard_map/ppermute | solution.py:25
  24.2 4.5 %collective-permute-start.11 = (bf16[128,256]{1,0:T(8,128)(2,1)S(1)}, bf16[128,256]{1,0:T(8,128)(2,1)S(1)}, u32[]{:S(2)}, u32[]{:S(2)}) collective-permute-start(bf16[128,256]{1,0:T(8,128)(2,1)S(1)} %get-tuple-element.32), channel_id=1, source_target_pairs={{0,2},{1,3},{2,0},{3,1},{4,6},{5,7},{6,4},{7,5},{8,10},{9,11},{10,... | collective-permute-start | bytes 196616 | tf_op jit(solution)/shard_map/ppermute | solution.py:25
  24.8 7.5 %collective-permute-start.12 = (bf16[128,256]{1,0:T(8,128)(2,1)S(1)}, bf16[128,256]{1,0:T(8,128)(2,1)S(1)}, u32[]{:S(2)}, u32[]{:S(2)}) collective-permute-start(bf16[128,256]{1,0:T(8,128)(2,1)S(1)} %get-tuple-element.34), channel_id=1, source_target_pairs={{0,4},{1,5},{2,6},{3,7},{4,0},{5,1},{6,2},{7,3},{8,12},{9,13},{10,... | collective-permute-start | bytes 196616 | tf_op jit(solution)/shard_map/ppermute | solution.py:25
  28.3 6.2 %collective-permute-start.13 = (bf16[128,256]{1,0:T(8,128)(2,1)S(1)}, bf16[128,256]{1,0:T(8,128)(2,1)S(1)}, u32[]{:S(2)}, u32[]{:S(2)}) collective-permute-start(bf16[128,256]{1,0:T(8,128)(2,1)S(1)} %get-tuple-element.33), channel_id=1, source_target_pairs={{0,6},{1,7},{2,4},{3,5},{4,2},{5,3},{6,0},{7,1},{8,14},{9,15},{10,... | collective-permute-start | bytes 196616 | tf_op jit(solution)/shard_map/ppermute | solution.py:25
  34.5 7.7 %copy-start.4 = (bf16[128,256]{1,0:T(8,128)(2,1)}, bf16[128,256]{1,0:T(8,128)(2,1)S(1)}, u32[]{:S(2)}) copy-start(bf16[128,256]{1,0:T(8,128)(2,1)S(1)} %fusion.15) | copy-start | bytes 196612
  34.6 4.6 %collective-permute-start.14 = (bf16[128,256]{1,0:T(8,128)(2,1)S(1)}, bf16[128,256]{1,0:T(8,128)(2,1)S(1)}, u32[]{:S(2)}, u32[]{:S(2)}) collective-permute-start(bf16[128,256]{1,0:T(8,128)(2,1)S(1)} %fusion.15), channel_id=1, source_target_pairs={{0,8},{8,0},{16,24},{24,16},{1,9},{9,1},{17,25},{25,17},{2,10},{10... | collective-permute-start | bytes 196616 | tf_op jit(solution)/shard_map/ppermute | solution.py:25
  35.9 4.3 %collective-permute-start.15 = (bf16[128,256]{1,0:T(8,128)(2,1)S(1)}, bf16[128,256]{1,0:T(8,128)(2,1)S(1)}, u32[]{:S(2)}, u32[]{:S(2)}) collective-permute-start(bf16[128,256]{1,0:T(8,128)(2,1)S(1)} %fusion.15), channel_id=1, source_target_pairs={{0,16},{8,24},{16,0},{24,8},{1,17},{9,25},{17,1},{25,9},{2,18},{10... | collective-permute-start | bytes 196616 | tf_op jit(solution)/shard_map/ppermute | solution.py:25
  36.7 5.2 %collective-permute-start.16 = (bf16[128,256]{1,0:T(8,128)(2,1)S(1)}, bf16[128,256]{1,0:T(8,128)(2,1)S(1)}, u32[]{:S(2)}, u32[]{:S(2)}) collective-permute-start(bf16[128,256]{1,0:T(8,128)(2,1)S(1)} %fusion.15), channel_id=1, source_target_pairs={{0,24},{8,16},{16,8},{24,0},{1,25},{9,17},{17,9},{25,1},{2,26},{10... | collective-permute-start | bytes 196616 | tf_op jit(solution)/shard_map/ppermute | solution.py:25
  42.3 1.6 %collective-permute-start.17 = (bf16[4,128,256]{2,1,0:T(8,128)(2,1)S(1)}, bf16[4,128,256]{2,1,0:T(8,128)(2,1)S(1)}, u32[]{:S(2)}, u32[]{:S(2)}) collective-permute-start(bf16[4,128,256]{2,1,0:T(8,128)(2,1)S(1)} %fusion.7), channel_id=1, source_target_pairs={{0,1},{1,0},{2,3},{3,2},{4,5},{5,4},{6,7},{7,6},{8,9},{9,8},{10,11... | collective-permute-start | bytes 786440 | tf_op jit(solution)/shard_map/ppermute | solution.py:25
  44.0 5.0 %collective-permute-start.18 = (bf16[128,256]{1,0:T(8,128)(2,1)S(1)}, bf16[128,256]{1,0:T(8,128)(2,1)S(1)}, u32[]{:S(2)}, u32[]{:S(2)}) collective-permute-start(bf16[128,256]{1,0:T(8,128)(2,1)S(1)} %get-tuple-element.25), channel_id=1, source_target_pairs={{0,2},{1,3},{2,0},{3,1},{4,6},{5,7},{6,4},{7,5},{8,10},{9,11},{10,... | collective-permute-start | bytes 196616 | tf_op jit(solution)/shard_map/ppermute | solution.py:25
  44.9 8.4 %collective-permute-start.19 = (bf16[128,256]{1,0:T(8,128)(2,1)S(1)}, bf16[128,256]{1,0:T(8,128)(2,1)S(1)}, u32[]{:S(2)}, u32[]{:S(2)}) collective-permute-start(bf16[128,256]{1,0:T(8,128)(2,1)S(1)} %get-tuple-element.27), channel_id=1, source_target_pairs={{0,4},{1,5},{2,6},{3,7},{4,0},{5,1},{6,2},{7,3},{8,12},{9,13},{10,... | collective-permute-start | bytes 196616 | tf_op jit(solution)/shard_map/ppermute | solution.py:25
  46.6 6.7 %collective-permute-start.20 = (bf16[128,256]{1,0:T(8,128)(2,1)S(1)}, bf16[128,256]{1,0:T(8,128)(2,1)S(1)}, u32[]{:S(2)}, u32[]{:S(2)}) collective-permute-start(bf16[128,256]{1,0:T(8,128)(2,1)S(1)} %get-tuple-element.26), channel_id=1, source_target_pairs={{0,6},{1,7},{2,4},{3,5},{4,2},{5,3},{6,0},{7,1},{8,14},{9,15},{10,... | collective-permute-start | bytes 196616 | tf_op jit(solution)/shard_map/ppermute | solution.py:25
  53.3 5.2 %collective-permute-start.21 = (bf16[128,256]{1,0:T(8,128)(2,1)S(1)}, bf16[128,256]{1,0:T(8,128)(2,1)S(1)}, u32[]{:S(2)}, u32[]{:S(2)}) collective-permute-start(bf16[128,256]{1,0:T(8,128)(2,1)S(1)} %fusion.18), channel_id=1, source_target_pairs={{0,24},{8,16},{16,8},{24,0},{1,25},{9,17},{17,9},{25,1},{2,26},{10... | collective-permute-start | bytes 196616 | tf_op jit(solution)/shard_map/ppermute | solution.py:25
  54.8 4.4 %collective-permute-start.22 = (bf16[128,256]{1,0:T(8,128)(2,1)S(1)}, bf16[128,256]{1,0:T(8,128)(2,1)S(1)}, u32[]{:S(2)}, u32[]{:S(2)}) collective-permute-start(bf16[128,256]{1,0:T(8,128)(2,1)S(1)} %fusion.18), channel_id=1, source_target_pairs={{0,16},{8,24},{16,0},{24,8},{1,17},{9,25},{17,1},{25,9},{2,18},{10... | collective-permute-start | bytes 196616 | tf_op jit(solution)/shard_map/ppermute | solution.py:25
  56.3 4.3 %collective-permute-start.23 = (bf16[128,256]{1,0:T(8,128)(2,1)S(1)}, bf16[128,256]{1,0:T(8,128)(2,1)S(1)}, u32[]{:S(2)}, u32[]{:S(2)}) collective-permute-start(bf16[128,256]{1,0:T(8,128)(2,1)S(1)} %fusion.18), channel_id=1, source_target_pairs={{0,8},{8,0},{16,24},{24,16},{1,9},{9,1},{17,25},{25,17},{2,10},{10... | collective-permute-start | bytes 196616 | tf_op jit(solution)/shard_map/ppermute | solution.py:25

commit v3 on v2

v3 whole, which is shorter than its diff:
```python
import functools

import jax
import jax.numpy as jnp
from jax import lax
from jax.experimental import pallas as pl
from jax.experimental.pallas import tpu as pltpu
from jax.sharding import PartitionSpec as P

HD = 128
RESPONSES = 4
LOG2E = 1.4426950408889634
NEG = -1e30
SCALE = HD**-0.5

NT = (((1,), (1,)), ((), ()))
TN = (((0,), (0,)), ((), ()))


def dot(a, b, dims=(((1,), (0,)), ((), ()))):
    return lax.dot_general(a, b, dims, preferred_element_type=jnp.float32)


def swap(x, axis, mask):
    size = lax.axis_size(axis)
    return lax.ppermute(x, axis, [(i, i ^ mask) for i in range(size)])


def fold(x):
    return x.reshape(x.shape[0] // 8, 8, x.shape[1])


def scores_kernel(half, local, pieces, *refs):
    (len_ref, me_ref), kv_refs = refs[:2], refs[2 : 2 + half]
    q_refs, do_refs = refs[2 + half : 4 + half], refs[4 + half : 6 + half]
    e_ref, d_ref, stat_ref, q_rows, do_rows, bias = refs[6 + half :]
    stripes = 2 * half
    me = me_ref[0]
    heads = q_refs[0].shape[1] // HD
    per_group = RESPONSES + 1
    coef = SCALE * LOG2E
    width = 2 * local

    row_pos = lax.broadcasted_iota(jnp.int32, (local, local), 0) * stripes
    for b in range(2):
        q_pos = lax.broadcasted_iota(jnp.int32, (1, local), 1) * stripes + (me ^ b)
        own_start = jnp.zeros((1, local), jnp.int32)
        prompt_start = jnp.zeros((1, local), jnp.int32)
        prompt_end = jnp.zeros((1, local), jnp.int32)
        start = jnp.int32(0)
        for k in range(pieces):
            length = len_ref[0, k]
            inside = q_pos >= start
            own_start = jnp.where(inside, start, own_start)
            if k % per_group == 0:
                prompt_start = jnp.where(inside, start, prompt_start)
                prompt_end = jnp.where(inside, start + length, prompt_end)
            start = start + length
        prompt_end = jnp.minimum(prompt_end, q_pos + 1)
        for k in range(half):
            k_pos = row_pos + (me ^ (2 * k))
            ok = ((k_pos >= own_start) & (k_pos <= q_pos)) | (
                (k_pos >= prompt_start) & (k_pos < prompt_end)
            )
            bias[b, k * local : (k + 1) * local, :] = jnp.where(ok, 0.0, NEG)

    for b in range(2):
        for pair in range(heads // 2):
            c = pair * 2 * HD
            cols = slice((b * heads + 2 * pair) * local, (b * heads + 2 * pair + 2) * local)
            q2 = jnp.concatenate(
                [q_refs[b][:, c : c + HD], q_refs[b][:, c + HD : c + 2 * HD]], axis=0
            )
            do2 = jnp.concatenate(
                [do_refs[b][:, c : c + HD], do_refs[b][:, c + HD : c + 2 * HD]], axis=0
            )
            q_rows[cols, :] = q2
            do_rows[cols, :] = do2
            top = jnp.full((8, width), NEG, jnp.float32)
            for k in range(half):
                rows = slice(k * local, (k + 1) * local)
                add = bias[b, rows, :]
                x = dot(kv_refs[k][:, :HD], q2, NT) + jnp.concatenate([add, add], axis=1)
                e_ref[rows, cols] = x
                top = jnp.maximum(top, jnp.max(fold(x), axis=0))
            top = jnp.max(top, axis=0, keepdims=True) * coef
            total = jnp.zeros((8, width), jnp.float32)
            weighted = jnp.zeros((8, width), jnp.float32)
            for k in range(half):
                rows = slice(k * local, (k + 1) * local)
                e = jnp.exp2(e_ref[rows, cols] * coef - top)
                d = dot(kv_refs[k][:, HD:], do2, NT)
                total = total + jnp.sum(fold(e), axis=0)
                weighted = weighted + jnp.sum(fold(e * d), axis=0)
                e_ref[rows, cols] = e
                d_ref[rows, cols] = d
            stat_ref[0:1, cols] = top
            stat_ref[1:2, cols] = jnp.sum(total, axis=0, keepdims=True)
            stat_ref[2:3, cols] = jnp.sum(weighted, axis=0, keepdims=True)
    stat_ref[3:8, :] = jnp.zeros((5, stat_ref.shape[1]), jnp.float32)


def gradients_kernel(half, local, *refs):
    e_ref, d_ref, mine_ref, other_ref, q_rows, do_rows = refs[:6]
    kv_refs = refs[6 : 6 + half]
    gq_ref, gq_other_ref, own_ref = refs[6 + half : 9 + half]
    part_refs = refs[9 + half : 8 + 2 * half]
    k_t, p_buf, ds_buf = refs[8 + 2 * half :]
    columns = e_ref.shape[1]
    heads = columns // (2 * local)
    side = columns // 2
    width = 2 * local

    for k in range(half):
        k_t[:, k * local : (k + 1) * local] = kv_refs[k][:, :HD].T
    for c in range(0, columns, width):
        cols = slice(c, c + width)
        across = slice((c + side) % columns, (c + side) % columns + width)
        top = jnp.maximum(mine_ref[0:1, cols], other_ref[0:1, across])
        factor = jnp.exp2(mine_ref[0:1, cols] - top)
        factor_other = jnp.exp2(other_ref[0:1, across] - top)
        total = mine_ref[1:2, cols] * factor + other_ref[1:2, across] * factor_other
        weighted = mine_ref[2:3, cols] * factor + other_ref[2:3, across] * factor_other
        inv = 1.0 / total
        delta = weighted * inv
        factor = factor * inv
        for k in range(half):
            rows = slice(k * local, (k + 1) * local)
            p = e_ref[rows, cols] * factor
            ds = p * (d_ref[rows, cols] - delta)
            p_buf[rows, cols] = p.astype(jnp.bfloat16)
            ds_buf[rows, cols] = ds.astype(jnp.bfloat16)

    gk = dot(ds_buf[...], q_rows[...]) * SCALE
    gv = dot(p_buf[...], do_rows[...])
    own_ref[:, :HD] = gk[:local]
    own_ref[:, HD:] = gv[:local]
    for k in range(1, half):
        rows = slice(k * local, (k + 1) * local)
        part_refs[k - 1][:, :HD] = gk[rows].astype(jnp.bfloat16)
        part_refs[k - 1][:, HD:] = gv[rows].astype(jnp.bfloat16)
    gq = dot(k_t[...], ds_buf[...]) * SCALE
    for h in range(heads):
        cols = slice(h * HD, (h + 1) * HD)
        gq_ref[:, cols] = gq[:, h * local : (h + 1) * local].T
        gq_other_ref[:, cols] = gq[:, side + h * local : side + (h + 1) * local].T


def attention(lengths, me, kv, q, do, q_other, do_other):
    half = len(kv)
    local, width = q.shape
    keys = half * local
    heads = width // HD
    columns = 2 * heads * local
    vm = pl.BlockSpec(memory_space=pltpu.VMEM)
    sm = pl.BlockSpec(memory_space=pltpu.SMEM)
    bf16, f32 = jnp.bfloat16, jnp.float32
    e, d, stat, q_rows, do_rows = pl.pallas_call(
        functools.partial(scores_kernel, half, local, lengths.shape[1]),
        out_shape=(
            jax.ShapeDtypeStruct((keys, columns), f32),
            jax.ShapeDtypeStruct((keys, columns), f32),
            jax.ShapeDtypeStruct((8, columns), f32),
            jax.ShapeDtypeStruct((columns, HD), bf16),
            jax.ShapeDtypeStruct((columns, HD), bf16),
        ),
        in_specs=[sm, sm] + [vm] * (half + 4),
        out_specs=(vm,) * 5,
        scratch_shapes=[pltpu.VMEM((2, keys, local), f32)],
        cost_estimate=pl.CostEstimate(flops=COST1, bytes_accessed=0, transcendentals=0),
        compiler_params=pltpu.CompilerParams(vmem_limit_bytes=keys * 44 * 1024),
    )(lengths, me, *kv, q, q_other, do, do_other)
    stat_other = swap(stat, "ctx", 1)
    return pl.pallas_call(
        functools.partial(gradients_kernel, half, local),
        out_shape=(
            jax.ShapeDtypeStruct((local, width), f32),
            jax.ShapeDtypeStruct((local, width), f32),
            jax.ShapeDtypeStruct((local, 2 * HD), f32),
        )
        + (jax.ShapeDtypeStruct((local, 2 * HD), bf16),) * (half - 1),
        in_specs=[vm] * (half + 6),
        out_specs=(vm,) * (half + 2),
        scratch_shapes=[
            pltpu.VMEM((HD, keys), bf16),
            pltpu.VMEM((keys, columns), bf16),
            pltpu.VMEM((keys, columns), bf16),
        ],
        cost_estimate=pl.CostEstimate(flops=COST2, bytes_accessed=0, transcendentals=0),
        compiler_params=pltpu.CompilerParams(vmem_limit_bytes=keys * 44 * 1024),
    )(e, d, stat, stat_other, q_rows, do_rows, *kv)


COST1 = 1_000_000_000
COST2 = 1_000_000_000


def on_device(inputs, queries, keys_values, out_grad, lengths):
    stripes = lax.axis_size("ctx")
    rows = lax.axis_size("dp")
    half = stripes // 2
    me = lax.axis_index("ctx")
    row = lax.axis_index("dp")
    x = inputs[0, 0]
    q = queries[0, 0]
    do = out_grad[0, 0]
    kv = keys_values[0, 0]
    local, features = x.shape
    part = features // (stripes * rows)

    kv_own = [kv] + [swap(kv, "ctx", 2 * k) for k in range(1, half)]
    q_other = swap(q, "ctx", 1)
    do_other = swap(do, "ctx", 1)

    x, q_other, do_other = lax.optimization_barrier((x, q_other, do_other))
    xb = x.reshape(local, stripes, rows, part)
    x_slabs = []
    for k in range(rows):
        slab = lax.dynamic_index_in_dim(xb, row ^ k, 2, keepdims=False)
        slab = slab.reshape(local, stripes * part)
        x_slabs.append(slab if k == 0 else swap(slab, "dp", k))

    gq, gq_other, own, *parts = attention(
        lengths, me.reshape(1).astype(jnp.int32), kv_own, q, do, q_other, do_other
    )
    parts, early = lax.optimization_barrier((parts, [x_slabs[k] for k in (3,)]))
    for k, slab in zip((3,), early):
        x_slabs[k] = slab

    terms = [swap(parts[k - 1], "ctx", 2 * k) for k in range(1, half)]
    gkv = own + sum(t.astype(jnp.float32) for t in terms)
    gkv = gkv.astype(jnp.bfloat16)
    gq = (gq + swap(gq_other, "ctx", 1)).astype(jnp.bfloat16)

    g_rows = [gkv] + [swap(gkv, "dp", k) for k in range(1, rows)]
    x_all = jnp.concatenate(x_slabs, axis=0)
    g_all = jnp.concatenate(g_rows, axis=0)
    w = dot(x_all, g_all, TN) * (1.0 / rows)
    w = w.reshape(half, 2, part, 2 * HD)
    core = me % 2
    w_own = lax.dynamic_index_in_dim(w, core, 1, keepdims=False)
    w_sib = lax.dynamic_index_in_dim(w, 1 - core, 1, keepdims=False)
    w_chip = w_own + swap(w_sib.astype(jnp.bfloat16), "ctx", 1).astype(jnp.float32)
    z = me // 2
    w_mine = lax.dynamic_index_in_dim(w_chip, z, 0, keepdims=False)
    for k in range(1, half):
        block = lax.dynamic_index_in_dim(w_chip, z ^ k, 0, keepdims=False)
        w_mine = w_mine + swap(block.astype(jnp.bfloat16), "ctx", 2 * k).astype(jnp.float32)

    low = w_mine.astype(jnp.bfloat16)
    low, gq = lax.optimization_barrier((low, gq))
    blocks = [low] + [swap(low, "dp", k) for k in range(1, rows)]
    bit = 1
    while bit < rows:
        flip = (row & bit) != 0
        blocks = [jnp.where(flip, blocks[j ^ bit], blocks[j]) for j in range(rows)]
        bit *= 2
    w_out = jnp.concatenate([b.astype(jnp.float32) for b in blocks], axis=0)
    return (
        gq.reshape(1, 1, local, -1),
        gkv.reshape(1, 1, local, 2 * HD),
        w_out,
    )


def solution(mesh):
    spec = P("dp", "ctx", None, None)
    return jax.shard_map(
        on_device,
        mesh=mesh,
        in_specs=(spec, spec, spec, spec, P("dp", None)),
        out_specs=(spec, spec, P("ctx", None)),
        check_vma=False,
    )
```

time: 61.6 us -> 56.4 us (0.916)
  waiting for transfers between devices: 26.3 us -> 18.1 us
  starting transfers between devices: 25.7 us -> 27.7 us
  matrix products: 0.44 us -> 1.31 us
  other arithmetic: 1.06 us -> 1.73 us
    ppermute x24 -> x23, waiting for transfers between devices: 26.3 us -> 18.1 us  [swap(): return lax.ppermute(x, axis, [(i, i ^ mask) for i in range(size)])]
    ppermute x24 -> x23, starting transfers between devices: 25.7 us -> 27.7 us  [swap(): return lax.ppermute(x, axis, [(i, i ^ mask) for i in range(size)])]
    dot_general x1, matrix products: 0.44 us -> 1.31 us  [dot(): return lax.dot_general(a, b, dims, preferred_element_type=jnp.float32)]
    convert_element_type x0 -> x1, other arithmetic: none -> 0.76 us  [on_device(): gq = (gq + swap(gq_other, 'ctx', 1)).astype(jnp.bfloat16)]
    pallas_call x1 -> x2, Pallas kernels: 5.29 us -> 4.69 us  [the longest x1 2.93 us: attention(): pl.pallas_call(functools.partial(scores_kernel, half, local, lengths.shap...]
  transfers between devices with their start and end apart: 24 -> 23, of which waited for: 18 -> 13; matrix products, arithmetic and copies ran while one was open for 3% -> 5% of each run, Pallas kernels for 9% -> 8%
where the time goes in v3:
time: 56.4 us; the launch traced here: 56.2 us
  starting transfers between devices  27.7 us (49%)
  waiting for transfers between devices  18.1 us (32%)
  Pallas kernels  4.69 us (8%)
  local copies, waits for them, and re-layouts  1.91 us (3%)
  other arithmetic  1.73 us (3%)
  matrix products  1.31 us (2%)
  between operations  0.82 us (1%)
    ppermute x23, starting transfers between devices, swap(): return lax.ppermute(x, axis, [(i, i ^ mask) for i in range(size)])  27.7 us
    ppermute x23, waiting for transfers between devices, swap(): return lax.ppermute(x, axis, [(i, i ^ mask) for i in range(size)])  18.1 us
    pallas_call x1, Pallas kernels, attention(): pl.pallas_call(functools.partial(scores_kernel, half, local, lengths.shap...  2.93 us
    pallas_call x1, Pallas kernels, attention(): pl.pallas_call(functools.partial(gradients_kernel, half, local), out_shap...  1.76 us
    unnamed x11, local copies, waits for them, and re-layouts  1.73 us
    dot_general x1, matrix products, dot(): return lax.dot_general(a, b, dims, preferred_element_type=jnp.float32)  1.31 us
  transfers between devices with their start and end apart: 23, of which 13 were waited for; matrix products, arithmetic and copies ran while one was open for 5% of the time, Pallas kernels for 8%

profile of v3, /device:TPU:0, one launch (start us, length us, event | category | flops | bytes accessed | tf_op | source)
XLA Modules:
  0.0 56.2 jit_solution(6917231655652377495)
XLA Ops:
  0.6 0.5 collective-permute-start
  1.1 0.1 collective-permute-start.1
  1.2 3.0 %collective-permute-start.4 = (bf16[128,256]{1,0:T(8,128)(2,1)}, bf16[128,256]{1,0:T(8,128)(2,1)S(1)}, u32[]{:S(2)}, u32[]{:S(2)}) collective-permute-start(bf16[128,256]{1,0:T(8,128)(2,1)} %bitcast.35), channel_id=1, source_target_pairs={{0,2},{1,3},{2,0},{3,1},{4,6},{5,7},{6,4},{7,5},{8,10},{9,11},{10,... | collective-permute-start | bytes 196616 | tf_op jit(solution)/shard_map/ppermute | solution.py:26
  4.2 2.6 %collective-permute-start.5 = (bf16[128,256]{1,0:T(8,128)(2,1)}, bf16[128,256]{1,0:T(8,128)(2,1)S(1)}, u32[]{:S(2)}, u32[]{:S(2)}) collective-permute-start(bf16[128,256]{1,0:T(8,128)(2,1)} %bitcast.36), channel_id=1, source_target_pairs={{0,4},{1,5},{2,6},{3,7},{4,0},{5,1},{6,2},{7,3},{8,12},{9,13},{10,... | collective-permute-start | bytes 196616 | tf_op jit(solution)/shard_map/ppermute | solution.py:26
  6.8 0.0 collective-permute-start.6
  6.8 1.7 %copy.10 = bf16[1,1,128,4096]{2,3,1,0:T(8,128)(2,1)S(1)} copy(bf16[1,1,128,4096]{3,2,1,0:T(8,128)(2,1)} %param.5) | data formatting | bytes 2097152 | tf_op args[0]
  8.6 0.0 collective-permute-done.1.refs_9_
  8.6 0.1 constant_dynamic-slice_fusion.3
  8.7 2.7 %collective-permute-start.8 = (bf16[128,1024]{0,1:T(8,128)(2,1)S(1)}, bf16[128,1024]{0,1:T(8,128)(2,1)S(1)}, u32[]{:S(2)}, u32[]{:S(2)}) collective-permute-start(bf16[128,1024]{0,1:T(8,128)(2,1)S(1)} %bitcast.51), channel_id=1, source_target_pairs={{0,24},{8,16},{16,8},{24,0},{1,25},{9,17},{17,9},{25,1},{2,26},{10... | collective-permute-start | bytes 786440 | tf_op jit(solution)/shard_map/ppermute | solution.py:26
  11.4 0.5 collective-permute-done.5.refs_4_.refs_8_
  11.9 1.3 %collective-permute-done.6.refs_5_.refs_9_ = bf16[128,256]{1,0:T(8,128)(2,1)S(1)} collective-permute-done((bf16[128,256]{1,0:T(8,128)(2,1)}, bf16[128,256]{1,0:T(8,128)(2,1)S(1)}, u32[]{:S(2)}, u32[]{:S(2)}) %collective-permute-start.6) | collective-permute-done | bytes 65568 | tf_op jit(solution)/shard_map/ppermute | solution.py:26
  13.2 2.9 %shard_map.76 = (f32[512,2048]{1,0:T(8,128)S(1)}, f32[512,2048]{1,0:T(8,128)S(1)}, f32[8,2048]{1,0:T(8,128)S(1)}, bf16[2048,128]{1,0:T(8,128)(2,1)S(1)}, bf16[2048,128]{1,0:T(8,128)(2,1)S(1)}) custom-call(s32[1,10]{1,0:T(1,128)S(1)} %copy-done.3, s32[1]{0:T(128)} %bitcast.7.refs_1_, bf16[128,256]{1,0:T(8,128)(2,1)S(1)} %bitcast.38, ...), custom_call_target="tpu_custom_call" | custom-call | flops 1000000000 | tf_op jit(solution)/shard_map/pallas_call | solution.py:158
  16.2 0.1 collective-permute-start.7
  16.2 1.2 %collective-permute-done.7.refs_3_ = f32[8,2048]{1,0:T(8,128)S(1)} collective-permute-done((f32[8,2048]{1,0:T(8,128)S(1)}, f32[8,2048]{1,0:T(8,128)S(1)}, u32[]{:S(2)}, u32[]{:S(2)}) %collective-permute-start.7) | collective-permute-done | bytes 65568 | tf_op jit(solution)/shard_map/ppermute | solution.py:26
  17.5 1.8 %shard_map.77 = (f32[128,1024]{1,0:T(8,128)S(1)}, f32[128,1024]{1,0:T(8,128)S(1)}, f32[128,256]{1,0:T(8,128)S(1)}, bf16[128,256]{1,0:T(8,128)(2,1)S(1)}, bf16[12...) custom-call(f32[512,2048]{1,0:T(8,128)S(1)} %get-tuple-element.26.refs_0_, ...), custom_call_target="tpu_custom_call" | custom-call | flops 1000000000 | tf_op jit(solution)/shard_map/pallas_call | solution.py:174
  19.2 0.0 collective-permute-done.8
  19.3 1.8 %collective-permute-start.10 = (bf16[128,256]{1,0:T(8,128)(2,1)S(1)}, bf16[128,256]{1,0:T(8,128)(2,1)S(1)}, u32[]{:S(2)}, u32[]{:S(2)}) collective-permute-start(bf16[128,256]{1,0:T(8,128)(2,1)S(1)} %get-tuple-element.37), channel_id=1, source_target_pairs={{0,4},{1,5},{2,6},{3,7},{4,0},{5,1},{6,2},{7,3},{8,12},{9,13},{10,... | collective-permute-start | bytes 196616 | tf_op jit(solution)/shard_map/ppermute | solution.py:26
  21.1 1.4 %collective-permute-start.11 = (bf16[128,256]{1,0:T(8,128)(2,1)S(1)}, bf16[128,256]{1,0:T(8,128)(2,1)S(1)}, u32[]{:S(2)}, u32[]{:S(2)}) collective-permute-start(bf16[128,256]{1,0:T(8,128)(2,1)S(1)} %get-tuple-element.38), channel_id=1, source_target_pairs={{0,6},{1,7},{2,4},{3,5},{4,2},{5,3},{6,0},{7,1},{8,14},{9,15},{10,... | collective-permute-start | bytes 196616 | tf_op jit(solution)/shard_map/ppermute | solution.py:26
  22.5 0.3 collective-permute-start.9
  22.8 1.5 %collective-permute-start.2 = (bf16[128,1024]{0,1:T(8,128)(2,1)S(1)}, bf16[128,1024]{0,1:T(8,128)(2,1)S(1)}, u32[]{:S(2)}, u32[]{:S(2)}) collective-permute-start(bf16[128,1024]{0,1:T(8,128)(2,1)S(1)} %bitcast.49), channel_id=1, source_target_pairs={{0,8},{8,0},{16,24},{24,16},{1,9},{9,1},{17,25},{25,17},{2,10},{10... | collective-permute-start | bytes 786440 | tf_op jit(solution)/shard_map/ppermute | solution.py:26
  24.3 1.5 %collective-permute-start.3 = (bf16[128,1024]{0,1:T(8,128)(2,1)S(1)}, bf16[128,1024]{0,1:T(8,128)(2,1)S(1)}, u32[]{:S(2)}, u32[]{:S(2)}) collective-permute-start(bf16[128,1024]{0,1:T(8,128)(2,1)S(1)} %bitcast.48), channel_id=1, source_target_pairs={{0,16},{8,24},{16,0},{24,8},{1,17},{9,25},{17,1},{25,9},{2,18},{10... | collective-permute-start | bytes 786440 | tf_op jit(solution)/shard_map/ppermute | solution.py:26
  25.8 1.7 %collective-permute-done.10 = bf16[128,256]{1,0:T(8,128)(2,1)S(1)} collective-permute-done((bf16[128,256]{1,0:T(8,128)(2,1)S(1)}, bf16[128,256]{1,0:T(8,128)(2,1)S(1)}, u32[]{:S(2)}, u32[]{:S(2)}) %collective-permute-start.10) | collective-permute-done | bytes 65568 | tf_op jit(solution)/shard_map/ppermute | solution.py:26
  27.5 0.0 collective-permute-done.11
  27.5 1.0 %collective-permute-done.9 = bf16[128,256]{1,0:T(8,128)(2,1)S(1)} collective-permute-done((bf16[128,256]{1,0:T(8,128)(2,1)S(1)}, bf16[128,256]{1,0:T(8,128)(2,1)S(1)}, u32[]{:S(2)}, u32[]{:S(2)}) %collective-permute-start.9) | collective-permute-done | bytes 65568 | tf_op jit(solution)/shard_map/ppermute | solution.py:26
  28.6 0.0 copy-start.4
  28.6 1.6 %collective-permute-start.12 = (bf16[128,256]{1,0:T(8,128)(2,1)S(1)}, bf16[128,256]{1,0:T(8,128)(2,1)S(1)}, u32[]{:S(2)}, u32[]{:S(2)}) collective-permute-start(bf16[128,256]{1,0:T(8,128)(2,1)S(1)} %add_convert_fusion.1), channel_id=1, source_target_pairs={{0,8},{8,0},{16,24},{24,16},{1,9},{9,1},{17,25},{25,17},{2,10},{10... | collective-permute-start | bytes 196616 | tf_op jit(solution)/shard_map/ppermute | solution.py:26
  30.2 1.5 %collective-permute-start.13 = (bf16[128,256]{1,0:T(8,128)(2,1)S(1)}, bf16[128,256]{1,0:T(8,128)(2,1)}, u32[]{:S(2)}, u32[]{:S(2)}) collective-permute-start(bf16[128,256]{1,0:T(8,128)(2,1)S(1)} %add_convert_fusion.1), channel_id=1, source_target_pairs={{0,16},{8,24},{16,0},{24,8},{1,17},{9,25},{17,1},{25,9},{2,18},{10... | collective-permute-start | bytes 196616 | tf_op jit(solution)/shard_map/ppermute | solution.py:26
  31.7 0.5 collective-permute-start.14
  32.1 0.8 %collective-permute-done.12 = bf16[128,256]{1,0:T(8,128)(2,1)S(1)} collective-permute-done((bf16[128,256]{1,0:T(8,128)(2,1)S(1)}, bf16[128,256]{1,0:T(8,128)(2,1)S(1)}, u32[]{:S(2)}, u32[]{:S(2)}) %collective-permute-start.12) | collective-permute-done | bytes 65568 | tf_op jit(solution)/shard_map/ppermute | solution.py:26
  32.9 1.6 %collective-permute-done.13 = bf16[128,256]{1,0:T(8,128)(2,1)} collective-permute-done((bf16[128,256]{1,0:T(8,128)(2,1)S(1)}, bf16[128,256]{1,0:T(8,128)(2,1)}, u32[]{:S(2)}, u32[]{:S(2)}) %collective-permute-start.13) | collective-permute-done | bytes 65568 | tf_op jit(solution)/shard_map/ppermute | solution.py:26
  34.5 2.4 %collective-permute-done.14 = bf16[128,256]{1,0:T(8,128)(2,1)} collective-permute-done((bf16[128,256]{1,0:T(8,128)(2,1)S(1)}, bf16[128,256]{1,0:T(8,128)(2,1)}, u32[]{:S(2)}, u32[]{:S(2)}) %collective-permute-start.14) | collective-permute-done | bytes 65568 | tf_op jit(solution)/shard_map/ppermute | solution.py:26
  36.9 1.3 %convolution_multiply_fusion = f32[1024,256]{1,0:T(8,128)S(1)} fusion(bf16[128,1024]{0,1:T(8,128)(2,1)S(1)} %collective-permute-done.8, bf16[128,1024]{0,1:T(8,128)(2,1)S(1)} %collective-permute-done.3, bf16[128,1024]{0,1:T(8,128)(2,1)S(1)} %collective-permute-done.2, bf16[128,1024]{0,1:T(8,128)(2,1)S(1)} %bitcast.47, ...), kind=kOutput, calls=%fused_computation | convolution fusion | flops 273940480 | bytes 2359296 | tf_op jit(solution)/shard_map/dot_general | solution.py:21
  38.3 0.1 collective-permute-start.15
  38.4 0.5 collective-permute-start.19
  38.9 1.0 %collective-permute-done.15 = bf16[4,128,256]{2,1,0:T(8,128)(2,1)S(1)} collective-permute-done((bf16[4,128,256]{2,1,0:T(8,128)(2,1)S(1)}, bf16[4,128,256]{2,1,0:T(8,128)(2,1)S(1)}, u32[]{:S(2)}, u32[]{:S(2)}) %collective-permute-start.15) | collective-permute-done | bytes 262176 | tf_op jit(solution)/shard_map/ppermute | solution.py:26
  39.9 0.1 bitcast_add_fusion
  40.0 0.7 %collective-permute-start.16 = (bf16[128,256]{1,0:T(8,128)(2,1)S(1)}, bf16[128,256]{1,0:T(8,128)(2,1)S(1)}, u32[]{:S(2)}, u32[]{:S(2)}) collective-permute-start(bf16[128,256]{1,0:T(8,128)(2,1)S(1)} %get-tuple-element.47), channel_id=1, source_target_pairs={{0,2},{1,3},{2,0},{3,1},{4,6},{5,7},{6,4},{7,5},{8,10},{9,11},{10,... | collective-permute-start | bytes 196616 | tf_op jit(solution)/shard_map/ppermute | solution.py:26
  40.7 1.8 %collective-permute-start.17 = (bf16[128,256]{1,0:T(8,128)(2,1)S(1)}, bf16[128,256]{1,0:T(8,128)(2,1)S(1)}, u32[]{:S(2)}, u32[]{:S(2)}) collective-permute-start(bf16[128,256]{1,0:T(8,128)(2,1)S(1)} %get-tuple-element.49), channel_id=1, source_target_pairs={{0,4},{1,5},{2,6},{3,7},{4,0},{5,1},{6,2},{7,3},{8,12},{9,13},{10,... | collective-permute-start | bytes 196616 | tf_op jit(solution)/shard_map/ppermute | solution.py:26
  42.5 2.0 %collective-permute-start.18 = (bf16[128,256]{1,0:T(8,128)(2,1)S(1)}, bf16[128,256]{1,0:T(8,128)(2,1)S(1)}, u32[]{:S(2)}, u32[]{:S(2)}) collective-permute-start(bf16[128,256]{1,0:T(8,128)(2,1)S(1)} %get-tuple-element.48), channel_id=1, source_target_pairs={{0,6},{1,7},{2,4},{3,5},{4,2},{5,3},{6,0},{7,1},{8,14},{9,15},{10,... | collective-permute-start | bytes 196616 | tf_op jit(solution)/shard_map/ppermute | solution.py:26
  44.5 0.8 %add_convert_fusion = bf16[128,1024]{1,0:T(8,128)(2,1)} fusion(f32[128,1024]{1,0:T(8,128)S(1)} %get-tuple-element.39, f32[128,1024]{1,0:T(8,128)S(1)} %collective-permute-done.19), kind=kLoop, calls=%fused_computation.10 | loop fusion | flops 262144 | bytes 1310720 | tf_op jit(solution)/shard_map/convert_element_type | solution.py:233
  45.2 3.8 %collective-permute-done.17 = bf16[128,256]{1,0:T(8,128)(2,1)S(1)} collective-permute-done((bf16[128,256]{1,0:T(8,128)(2,1)S(1)}, bf16[128,256]{1,0:T(8,128)(2,1)S(1)}, u32[]{:S(2)}, u32[]{:S(2)}) %collective-permute-start.17) | collective-permute-done | bytes 65568 | tf_op jit(solution)/shard_map/ppermute | solution.py:26
  49.1 0.6 %collective-permute-start.20 = (bf16[128,256]{1,0:T(8,128)(2,1)S(1)}, bf16[128,256]{1,0:T(8,128)(2,1)S(1)}, u32[]{:S(2)}, u32[]{:S(2)}) collective-permute-start(bf16[128,256]{1,0:T(8,128)(2,1)S(1)} %fusion.17), channel_id=1, source_target_pairs={{0,24},{8,16},{16,8},{24,0},{1,25},{9,17},{17,9},{25,1},{2,26},{10... | collective-permute-start | bytes 196616 | tf_op jit(solution)/shard_map/ppermute | solution.py:26
  49.7 1.4 %collective-permute-start.21 = (bf16[128,256]{1,0:T(8,128)(2,1)S(1)}, bf16[128,256]{1,0:T(8,128)(2,1)S(1)}, u32[]{:S(2)}, u32[]{:S(2)}) collective-permute-start(bf16[128,256]{1,0:T(8,128)(2,1)S(1)} %fusion.17), channel_id=1, source_target_pairs={{0,16},{8,24},{16,0},{24,8},{1,17},{9,25},{17,1},{25,9},{2,18},{10... | collective-permute-start | bytes 196616 | tf_op jit(solution)/shard_map/ppermute | solution.py:26
  51.1 1.5 %collective-permute-start.22 = (bf16[128,256]{1,0:T(8,128)(2,1)S(1)}, bf16[128,256]{1,0:T(8,128)(2,1)S(1)}, u32[]{:S(2)}, u32[]{:S(2)}) collective-permute-start(bf16[128,256]{1,0:T(8,128)(2,1)S(1)} %fusion.17), channel_id=1, source_target_pairs={{0,8},{8,0},{16,24},{24,16},{1,9},{9,1},{17,25},{25,17},{2,10},{10... | collective-permute-start | bytes 196616 | tf_op jit(solution)/shard_map/ppermute | solution.py:26
  52.6 1.8 %collective-permute-done.20 = bf16[128,256]{1,0:T(8,128)(2,1)S(1)} collective-permute-done((bf16[128,256]{1,0:T(8,128)(2,1)S(1)}, bf16[128,256]{1,0:T(8,128)(2,1)S(1)}, u32[]{:S(2)}, u32[]{:S(2)}) %collective-permute-start.20) | collective-permute-done | bytes 65568 | tf_op jit(solution)/shard_map/ppermute | solution.py:26
  54.4 0.2 collective-permute-done.21
  54.6 0.7 %collective-permute-done.22 = bf16[128,256]{1,0:T(8,128)(2,1)S(1)} collective-permute-done((bf16[128,256]{1,0:T(8,128)(2,1)S(1)}, bf16[128,256]{1,0:T(8,128)(2,1)S(1)}, u32[]{:S(2)}, u32[]{:S(2)}) %collective-permute-start.22) | collective-permute-done | bytes 65568 | tf_op jit(solution)/shard_map/ppermute | solution.py:26
  55.4 0.8 %maximum_convert_fusion = f32[512,256]{1,0:T(8,128)} fusion(bf16[128,256]{1,0:T(8,128)(2,1)S(1)} %get-tuple-element.53, bf16[128,256]{1,0:T(8,128)(2,1)S(1)} %get-tuple-element.52, bf16[128,256]{1,0:T(8,128)(2,1)S(1)} %get-tuple-element.51, bf16[128,256]{1,0:T(8,128)(2,1)S(1)} %get-tuple-element.50), kind=kLoop, calls=%fused_computation.19 | loop fusion | flops 1048576 | bytes 786432 | tf_op jit(solution)/shard_map/concatenate | solution.py:258
  (21 shorter events, 0.2 us)
Async XLA Ops:
  0.6 7.9 %collective-permute-start = (bf16[128,1024]{1,0:T(8,128)(2,1)}, bf16[128,1024]{1,0:T(8,128)(2,1)S(1)}, u32[]{:S(2)}, u32[]{:S(2)}) collective-permute-start(bf16[128,1024]{1,0:T(8,128)(2,1)} %bitcast.40), channel_id=1, source_target_pairs={{0,1},{1,0},{2,3},{3,2},{4,5},{5,4},{6,7},{7,6},{8,9},{9,8},{10,11... | collective-permute-start | bytes 786440 | tf_op jit(solution)/shard_map/ppermute | solution.py:26
  1.1 7.4 %collective-permute-start.1 = (bf16[128,1024]{1,0:T(8,128)(2,1)}, bf16[128,1024]{1,0:T(8,128)(2,1)S(1)}, u32[]{:S(2)}, u32[]{:S(2)}) collective-permute-start(bf16[128,1024]{1,0:T(8,128)(2,1)} %bitcast.42), channel_id=1, source_target_pairs={{0,1},{1,0},{2,3},{3,2},{4,5},{5,4},{6,7},{7,6},{8,9},{9,8},{10,11... | collective-permute-start | bytes 786440 | tf_op jit(solution)/shard_map/ppermute | solution.py:26
  1.2 10.2 %collective-permute-start.4 = (bf16[128,256]{1,0:T(8,128)(2,1)}, bf16[128,256]{1,0:T(8,128)(2,1)S(1)}, u32[]{:S(2)}, u32[]{:S(2)}) collective-permute-start(bf16[128,256]{1,0:T(8,128)(2,1)} %bitcast.35), channel_id=1, source_target_pairs={{0,2},{1,3},{2,0},{3,1},{4,6},{5,7},{6,4},{7,5},{8,10},{9,11},{10,... | collective-permute-start | bytes 196616 | tf_op jit(solution)/shard_map/ppermute | solution.py:26
  4.2 7.7 %collective-permute-start.5 = (bf16[128,256]{1,0:T(8,128)(2,1)}, bf16[128,256]{1,0:T(8,128)(2,1)S(1)}, u32[]{:S(2)}, u32[]{:S(2)}) collective-permute-start(bf16[128,256]{1,0:T(8,128)(2,1)} %bitcast.36), channel_id=1, source_target_pairs={{0,4},{1,5},{2,6},{3,7},{4,0},{5,1},{6,2},{7,3},{8,12},{9,13},{10,... | collective-permute-start | bytes 196616 | tf_op jit(solution)/shard_map/ppermute | solution.py:26
  6.8 6.4 %collective-permute-start.6 = (bf16[128,256]{1,0:T(8,128)(2,1)}, bf16[128,256]{1,0:T(8,128)(2,1)S(1)}, u32[]{:S(2)}, u32[]{:S(2)}) collective-permute-start(bf16[128,256]{1,0:T(8,128)(2,1)} %bitcast.37), channel_id=1, source_target_pairs={{0,6},{1,7},{2,4},{3,5},{4,2},{5,3},{6,0},{7,1},{8,14},{9,15},{10,... | collective-permute-start | bytes 196616 | tf_op jit(solution)/shard_map/ppermute | solution.py:26
  6.8 6.4 %copy-start = (bf16[1,1,128,256]{3,2,1,0:T(8,128)(2,1)S(1)}, bf16[1,1,128,256]{3,2,1,0:T(8,128)(2,1)}, u32[]{:S(2)}) copy-start(bf16[1,1,128,256]{3,2,1,0:T(8,128)(2,1)} %param.7) | copy-start | bytes 196612
  6.8 6.4 %copy-start.1 = (bf16[1,1,128,1024]{3,2,1,0:T(8,128)(2,1)S(1)}, bf16[1,1,128,1024]{3,2,1,0:T(8,128)(2,1)}, u32[]{:S(2)}) copy-start(bf16[1,1,128,1024]{3,2,1,0:T(8,128)(2,1)} %param.6) | copy-start | bytes 786436
  6.8 6.4 %copy-start.2 = (bf16[1,1,128,1024]{3,2,1,0:T(8,128)(2,1)S(1)}, bf16[1,1,128,1024]{3,2,1,0:T(8,128)(2,1)}, u32[]{:S(2)}) copy-start(bf16[1,1,128,1024]{3,2,1,0:T(8,128)(2,1)} %param.8) | copy-start | bytes 786436
  6.8 6.4 %copy-start.3 = (s32[1,10]{1,0:T(1,128)S(1)}, s32[1,10]{1,0:T(1,128)}, u32[]{:S(2)}) copy-start(s32[1,10]{1,0:T(1,128)} %refs_0_.1) | copy-start | bytes 124
  8.7 10.5 %collective-permute-start.8 = (bf16[128,1024]{0,1:T(8,128)(2,1)S(1)}, bf16[128,1024]{0,1:T(8,128)(2,1)S(1)}, u32[]{:S(2)}, u32[]{:S(2)}) collective-permute-start(bf16[128,1024]{0,1:T(8,128)(2,1)S(1)} %bitcast.51), channel_id=1, source_target_pairs={{0,24},{8,16},{16,8},{24,0},{1,25},{9,17},{17,9},{25,1},{2,26},{10... | collective-permute-start | bytes 786440 | tf_op jit(solution)/shard_map/ppermute | solution.py:26
  16.2 1.3 %collective-permute-start.7 = (f32[8,2048]{1,0:T(8,128)S(1)}, f32[8,2048]{1,0:T(8,128)S(1)}, u32[]{:S(2)}, u32[]{:S(2)}) collective-permute-start(f32[8,2048]{1,0:T(8,128)S(1)} %get-tuple-element.28.refs_2_), channel_id=1, source_target_pairs={{0,1},{1,0},{2,3},{3,2},{4,5},{5,4},{6,7},{7,6},{8,9},{9,8},{10,11... | collective-permute-start | bytes 196616 | tf_op jit(solution)/shard_map/ppermute | solution.py:26
  19.3 8.3 %collective-permute-start.10 = (bf16[128,256]{1,0:T(8,128)(2,1)S(1)}, bf16[128,256]{1,0:T(8,128)(2,1)S(1)}, u32[]{:S(2)}, u32[]{:S(2)}) collective-permute-start(bf16[128,256]{1,0:T(8,128)(2,1)S(1)} %get-tuple-element.37), channel_id=1, source_target_pairs={{0,4},{1,5},{2,6},{3,7},{4,0},{5,1},{6,2},{7,3},{8,12},{9,13},{10,... | collective-permute-start | bytes 196616 | tf_op jit(solution)/shard_map/ppermute | solution.py:26
  21.1 6.5 %collective-permute-start.11 = (bf16[128,256]{1,0:T(8,128)(2,1)S(1)}, bf16[128,256]{1,0:T(8,128)(2,1)S(1)}, u32[]{:S(2)}, u32[]{:S(2)}) collective-permute-start(bf16[128,256]{1,0:T(8,128)(2,1)S(1)} %get-tuple-element.38), channel_id=1, source_target_pairs={{0,6},{1,7},{2,4},{3,5},{4,2},{5,3},{6,0},{7,1},{8,14},{9,15},{10,... | collective-permute-start | bytes 196616 | tf_op jit(solution)/shard_map/ppermute | solution.py:26
  22.5 6.1 %collective-permute-start.9 = (bf16[128,256]{1,0:T(8,128)(2,1)S(1)}, bf16[128,256]{1,0:T(8,128)(2,1)S(1)}, u32[]{:S(2)}, u32[]{:S(2)}) collective-permute-start(bf16[128,256]{1,0:T(8,128)(2,1)S(1)} %get-tuple-element.36), channel_id=1, source_target_pairs={{0,2},{1,3},{2,0},{3,1},{4,6},{5,7},{6,4},{7,5},{8,10},{9,11},{10,... | collective-permute-start | bytes 196616 | tf_op jit(solution)/shard_map/ppermute | solution.py:26
  22.8 9.3 %collective-permute-start.2 = (bf16[128,1024]{0,1:T(8,128)(2,1)S(1)}, bf16[128,1024]{0,1:T(8,128)(2,1)S(1)}, u32[]{:S(2)}, u32[]{:S(2)}) collective-permute-start(bf16[128,1024]{0,1:T(8,128)(2,1)S(1)} %bitcast.49), channel_id=1, source_target_pairs={{0,8},{8,0},{16,24},{24,16},{1,9},{9,1},{17,25},{25,17},{2,10},{10... | collective-permute-start | bytes 786440 | tf_op jit(solution)/shard_map/ppermute | solution.py:26
  24.3 7.8 %collective-permute-start.3 = (bf16[128,1024]{0,1:T(8,128)(2,1)S(1)}, bf16[128,1024]{0,1:T(8,128)(2,1)S(1)}, u32[]{:S(2)}, u32[]{:S(2)}) collective-permute-start(bf16[128,1024]{0,1:T(8,128)(2,1)S(1)} %bitcast.48), channel_id=1, source_target_pairs={{0,16},{8,24},{16,0},{24,8},{1,17},{9,25},{17,1},{25,9},{2,18},{10... | collective-permute-start | bytes 786440 | tf_op jit(solution)/shard_map/ppermute | solution.py:26
  28.6 9.7 %copy-start.4 = (bf16[128,256]{1,0:T(8,128)(2,1)}, bf16[128,256]{1,0:T(8,128)(2,1)S(1)}, u32[]{:S(2)}) copy-start(bf16[128,256]{1,0:T(8,128)(2,1)S(1)} %add_convert_fusion.1) | copy-start | bytes 196612
  28.6 4.3 %collective-permute-start.12 = (bf16[128,256]{1,0:T(8,128)(2,1)S(1)}, bf16[128,256]{1,0:T(8,128)(2,1)S(1)}, u32[]{:S(2)}, u32[]{:S(2)}) collective-permute-start(bf16[128,256]{1,0:T(8,128)(2,1)S(1)} %add_convert_fusion.1), channel_id=1, source_target_pairs={{0,8},{8,0},{16,24},{24,16},{1,9},{9,1},{17,25},{25,17},{2,10},{10... | collective-permute-start | bytes 196616 | tf_op jit(solution)/shard_map/ppermute | solution.py:26
  30.2 4.4 %collective-permute-start.13 = (bf16[128,256]{1,0:T(8,128)(2,1)S(1)}, bf16[128,256]{1,0:T(8,128)(2,1)}, u32[]{:S(2)}, u32[]{:S(2)}) collective-permute-start(bf16[128,256]{1,0:T(8,128)(2,1)S(1)} %add_convert_fusion.1), channel_id=1, source_target_pairs={{0,16},{8,24},{16,0},{24,8},{1,17},{9,25},{17,1},{25,9},{2,18},{10... | collective-permute-start | bytes 196616 | tf_op jit(solution)/shard_map/ppermute | solution.py:26
  31.7 5.3 %collective-permute-start.14 = (bf16[128,256]{1,0:T(8,128)(2,1)S(1)}, bf16[128,256]{1,0:T(8,128)(2,1)}, u32[]{:S(2)}, u32[]{:S(2)}) collective-permute-start(bf16[128,256]{1,0:T(8,128)(2,1)S(1)} %add_convert_fusion.1), channel_id=1, source_target_pairs={{0,24},{8,16},{16,8},{24,0},{1,25},{9,17},{17,9},{25,1},{2,26},{10... | collective-permute-start | bytes 196616 | tf_op jit(solution)/shard_map/ppermute | solution.py:26
  38.3 1.6 %collective-permute-start.15 = (bf16[4,128,256]{2,1,0:T(8,128)(2,1)S(1)}, bf16[4,128,256]{2,1,0:T(8,128)(2,1)S(1)}, u32[]{:S(2)}, u32[]{:S(2)}) collective-permute-start(bf16[4,128,256]{2,1,0:T(8,128)(2,1)S(1)} %fusion.7), channel_id=1, source_target_pairs={{0,1},{1,0},{2,3},{3,2},{4,5},{5,4},{6,7},{7,6},{8,9},{9,8},{10,11... | collective-permute-start | bytes 786440 | tf_op jit(solution)/shard_map/ppermute | solution.py:26
  38.4 6.1 %collective-permute-start.19 = (f32[128,1024]{1,0:T(8,128)S(1)}, f32[128,1024]{1,0:T(8,128)S(1)}, u32[]{:S(2)}, u32[]{:S(2)}) collective-permute-start(f32[128,1024]{1,0:T(8,128)S(1)} %get-tuple-element.40), channel_id=1, source_target_pairs={{0,1},{1,0},{2,3},{3,2},{4,5},{5,4},{6,7},{7,6},{8,9},{9,8},{10,11... | collective-permute-start | bytes 1572872 | tf_op jit(solution)/shard_map/ppermute | solution.py:26
  40.0 5.2 %collective-permute-start.16 = (bf16[128,256]{1,0:T(8,128)(2,1)S(1)}, bf16[128,256]{1,0:T(8,128)(2,1)S(1)}, u32[]{:S(2)}, u32[]{:S(2)}) collective-permute-start(bf16[128,256]{1,0:T(8,128)(2,1)S(1)} %get-tuple-element.47), channel_id=1, source_target_pairs={{0,2},{1,3},{2,0},{3,1},{4,6},{5,7},{6,4},{7,5},{8,10},{9,11},{10,... | collective-permute-start | bytes 196616 | tf_op jit(solution)/shard_map/ppermute | solution.py:26
  40.7 8.3 %collective-permute-start.17 = (bf16[128,256]{1,0:T(8,128)(2,1)S(1)}, bf16[128,256]{1,0:T(8,128)(2,1)S(1)}, u32[]{:S(2)}, u32[]{:S(2)}) collective-permute-start(bf16[128,256]{1,0:T(8,128)(2,1)S(1)} %get-tuple-element.49), channel_id=1, source_target_pairs={{0,4},{1,5},{2,6},{3,7},{4,0},{5,1},{6,2},{7,3},{8,12},{9,13},{10,... | collective-permute-start | bytes 196616 | tf_op jit(solution)/shard_map/ppermute | solution.py:26
  42.5 6.5 %collective-permute-start.18 = (bf16[128,256]{1,0:T(8,128)(2,1)S(1)}, bf16[128,256]{1,0:T(8,128)(2,1)S(1)}, u32[]{:S(2)}, u32[]{:S(2)}) collective-permute-start(bf16[128,256]{1,0:T(8,128)(2,1)S(1)} %get-tuple-element.48), channel_id=1, source_target_pairs={{0,6},{1,7},{2,4},{3,5},{4,2},{5,3},{6,0},{7,1},{8,14},{9,15},{10,... | collective-permute-start | bytes 196616 | tf_op jit(solution)/shard_map/ppermute | solution.py:26
  49.1 5.3 %collective-permute-start.20 = (bf16[128,256]{1,0:T(8,128)(2,1)S(1)}, bf16[128,256]{1,0:T(8,128)(2,1)S(1)}, u32[]{:S(2)}, u32[]{:S(2)}) collective-permute-start(bf16[128,256]{1,0:T(8,128)(2,1)S(1)} %fusion.17), channel_id=1, source_target_pairs={{0,24},{8,16},{16,8},{24,0},{1,25},{9,17},{17,9},{25,1},{2,26},{10... | collective-permute-start | bytes 196616 | tf_op jit(solution)/shard_map/ppermute | solution.py:26
  49.7 5.0 %collective-permute-start.21 = (bf16[128,256]{1,0:T(8,128)(2,1)S(1)}, bf16[128,256]{1,0:T(8,128)(2,1)S(1)}, u32[]{:S(2)}, u32[]{:S(2)}) collective-permute-start(bf16[128,256]{1,0:T(8,128)(2,1)S(1)} %fusion.17), channel_id=1, source_target_pairs={{0,16},{8,24},{16,0},{24,8},{1,17},{9,25},{17,1},{25,9},{2,18},{10... | collective-permute-start | bytes 196616 | tf_op jit(solution)/shard_map/ppermute | solution.py:26
  51.1 4.3 %collective-permute-start.22 = (bf16[128,256]{1,0:T(8,128)(2,1)S(1)}, bf16[128,256]{1,0:T(8,128)(2,1)S(1)}, u32[]{:S(2)}, u32[]{:S(2)}) collective-permute-start(bf16[128,256]{1,0:T(8,128)(2,1)S(1)} %fusion.17), channel_id=1, source_target_pairs={{0,8},{8,0},{16,24},{24,16},{1,9},{9,1},{17,25},{25,17},{2,10},{10... | collective-permute-start | bytes 196616 | tf_op jit(solution)/shard_map/ppermute | solution.py:26

commit v4 on v3

--- a/solution.py
+++ b/solution.py
@@ -30,16 +30,19 @@
     return x.reshape(x.shape[0] // 8, 8, x.shape[1])
 
 
-def scores_kernel(half, local, pieces, *refs):
-    (len_ref, me_ref), kv_refs = refs[:2], refs[2 : 2 + half]
-    q_refs, do_refs = refs[2 + half : 4 + half], refs[4 + half : 6 + half]
-    e_ref, d_ref, stat_ref, q_rows, do_rows, bias = refs[6 + half :]
+def mask_kernel(half, local, pieces, *refs):
+    len_ref, me_ref, *ins = refs[:6]
+    q_refs, do_refs = ins[:2], ins[2:]
+    bias, q_rows, do_rows = refs[6:]
     stripes = 2 * half
     me = me_ref[0]
     heads = q_refs[0].shape[1] // HD
     per_group = RESPONSES + 1
-    coef = SCALE * LOG2E
-    width = 2 * local
+    for b in range(2):
+        for h in range(heads):
+            rows = slice((b * heads + h) * local, (b * heads + h + 1) * local)
+            q_rows[rows, :] = q_refs[b][:, h * HD : (h + 1) * HD]
+            do_rows[rows, :] = do_refs[b][:, h * HD : (h + 1) * HD]
 
     row_pos = lax.broadcasted_iota(jnp.int32, (local, local), 0) * stripes
     for b in range(2):
@@ -64,18 +67,18 @@
             )
             bias[b, k * local : (k + 1) * local, :] = jnp.where(ok, 0.0, NEG)
 
+
+def scores_kernel(half, local, *refs):
+    kv_refs = refs[:half]
+    bias, q_rows, do_rows, e_ref, d_ref, stat_ref = refs[half:]
+    heads = q_rows.shape[0] // (2 * local)
+    coef = SCALE * LOG2E
+    width = 2 * local
     for b in range(2):
         for pair in range(heads // 2):
-            c = pair * 2 * HD
             cols = slice((b * heads + 2 * pair) * local, (b * heads + 2 * pair + 2) * local)
-            q2 = jnp.concatenate(
-                [q_refs[b][:, c : c + HD], q_refs[b][:, c + HD : c + 2 * HD]], axis=0
-            )
-            do2 = jnp.concatenate(
-                [do_refs[b][:, c : c + HD], do_refs[b][:, c + HD : c + 2 * HD]], axis=0
-            )
-            q_rows[cols, :] = q2
-            do_rows[cols, :] = do2
+            q2 = q_rows[cols, :]
+            do2 = do_rows[cols, :]
             top = jnp.full((8, width), NEG, jnp.float32)
             for k in range(half):
                 rows = slice(k * local, (k + 1) * local)
@@ -155,21 +158,30 @@
     vm = pl.BlockSpec(memory_space=pltpu.VMEM)
     sm = pl.BlockSpec(memory_space=pltpu.SMEM)
     bf16, f32 = jnp.bfloat16, jnp.float32
-    e, d, stat, q_rows, do_rows = pl.pallas_call(
-        functools.partial(scores_kernel, half, local, lengths.shape[1]),
+    bias, q_rows, do_rows = pl.pallas_call(
+        functools.partial(mask_kernel, half, local, lengths.shape[1]),
+        out_shape=(
+            jax.ShapeDtypeStruct((2, keys, local), f32),
+            jax.ShapeDtypeStruct((columns, HD), bf16),
+            jax.ShapeDtypeStruct((columns, HD), bf16),
+        ),
+        in_specs=[sm, sm] + [vm] * 4,
+        out_specs=(vm,) * 3,
+        cost_estimate=pl.CostEstimate(flops=COST0, bytes_accessed=0, transcendentals=0),
+        compiler_params=pltpu.CompilerParams(vmem_limit_bytes=keys * 20 * 1024),
+    )(lengths, me, q, q_other, do, do_other)
+    e, d, stat = pl.pallas_call(
+        functools.partial(scores_kernel, half, local),
         out_shape=(
             jax.ShapeDtypeStruct((keys, columns), f32),
             jax.ShapeDtypeStruct((keys, columns), f32),
             jax.ShapeDtypeStruct((8, columns), f32),
-            jax.ShapeDtypeStruct((columns, HD), bf16),
-            jax.ShapeDtypeStruct((columns, HD), bf16),
         ),
-        in_specs=[sm, sm] + [vm] * (half + 4),
-        out_specs=(vm,) * 5,
-        scratch_shapes=[pltpu.VMEM((2, keys, local), f32)],
+        in_specs=[vm] * (half + 3),
+        out_specs=(vm,) * 3,
         cost_estimate=pl.CostEstimate(flops=COST1, bytes_accessed=0, transcendentals=0),
         compiler_params=pltpu.CompilerParams(vmem_limit_bytes=keys * 44 * 1024),
-    )(lengths, me, *kv, q, q_other, do, do_other)
+    )(*kv, bias, q_rows, do_rows)
     stat_other = swap(stat, "ctx", 1)
     return pl.pallas_call(
         functools.partial(gradients_kernel, half, local),
@@ -191,8 +203,9 @@
     )(e, d, stat, stat_other, q_rows, do_rows, *kv)
 
 
-COST1 = 1_000_000_000
-COST2 = 1_000_000_000
+COST0 = 1_000_000_000
+COST1 = 2_000_000_000
+COST2 = 2_000_000_000
 
 
 def on_device(inputs, queries, keys_values, out_grad, lengths):

time: 56.4 us -> 54.6 us (0.968)
  waiting for transfers between devices: 18.1 us -> 17 us
  matrix products: 1.31 us -> 0.43 us
    ppermute x23, waiting for transfers between devices: 18.1 us -> 17 us  [swap(): return lax.ppermute(x, axis, [(i, i ^ mask) for i in range(size)])]
    dot_general x1, matrix products: 1.31 us -> 0.43 us  [dot(): return lax.dot_general(a, b, dims, preferred_element_type=jnp.float32)]
    pallas_call x1 -> x2, Pallas kernels: 2.93 us -> 3.06 us  [the longest x1 2.13 us: attention(): pl.pallas_call(functools.partial(scores_kernel, half, local), out_shape=(...]
  transfers between devices with their start and end apart: 23 -> 23, of which waited for: 13 -> 12; matrix products, arithmetic and copies ran while one was open for 5% -> 5% of each run, Pallas kernels for 8% -> 9%
where the time goes in v4:
time: 54.6 us; the launch traced here: 54.4 us
  starting transfers between devices  27.7 us (51%)
  waiting for transfers between devices  17 us (31%)
  Pallas kernels  4.82 us (9%)
  local copies, waits for them, and re-layouts  1.9 us (3%)
  other arithmetic  1.73 us (3%)
  between operations  0.83 us (2%)
    ppermute x23, starting transfers between devices, swap(): return lax.ppermute(x, axis, [(i, i ^ mask) for i in range(size)])  27.7 us
    ppermute x23, waiting for transfers between devices, swap(): return lax.ppermute(x, axis, [(i, i ^ mask) for i in range(size)])  17 us
    pallas_call x1, Pallas kernels, attention(): pl.pallas_call(functools.partial(scores_kernel, half, local), out_shape=(...  2.13 us
    pallas_call x1, Pallas kernels, attention(): pl.pallas_call(functools.partial(gradients_kernel, half, local), out_shap...  1.76 us
    unnamed x11, local copies, waits for them, and re-layouts  1.73 us
  transfers between devices with their start and end apart: 23, of which 12 were waited for; matrix products, arithmetic and copies ran while one was open for 5% of the time, Pallas kernels for 9%

profile of v4, /device:TPU:0, one launch (start us, length us, event | category | flops | bytes accessed | tf_op | source)
XLA Modules:
  0.0 54.4 jit_solution(7860941699345015885)
XLA Ops:
  0.6 0.5 collective-permute-start
  1.1 0.1 collective-permute-start.1
  1.2 3.0 %collective-permute-start.4 = (bf16[128,256]{1,0:T(8,128)(2,1)}, bf16[128,256]{1,0:T(8,128)(2,1)S(1)}, u32[]{:S(2)}, u32[]{:S(2)}) collective-permute-start(bf16[128,256]{1,0:T(8,128)(2,1)} %bitcast.35), channel_id=1, source_target_pairs={{0,2},{1,3},{2,0},{3,1},{4,6},{5,7},{6,4},{7,5},{8,10},{9,11},{10,... | collective-permute-start | bytes 196616 | tf_op jit(solution)/shard_map/ppermute | solution.py:26
  4.2 2.6 %collective-permute-start.5 = (bf16[128,256]{1,0:T(8,128)(2,1)}, bf16[128,256]{1,0:T(8,128)(2,1)S(1)}, u32[]{:S(2)}, u32[]{:S(2)}) collective-permute-start(bf16[128,256]{1,0:T(8,128)(2,1)} %bitcast.36), channel_id=1, source_target_pairs={{0,4},{1,5},{2,6},{3,7},{4,0},{5,1},{6,2},{7,3},{8,12},{9,13},{10,... | collective-permute-start | bytes 196616 | tf_op jit(solution)/shard_map/ppermute | solution.py:26
  6.8 0.0 collective-permute-start.6
  6.8 1.7 %copy.10 = bf16[1,1,128,4096]{2,3,1,0:T(8,128)(2,1)S(1)} copy(bf16[1,1,128,4096]{3,2,1,0:T(8,128)(2,1)} %param.5) | data formatting | bytes 2097152 | tf_op args[0]
  8.6 0.0 collective-permute-done.refs_3_
  8.6 0.1 constant_dynamic-slice_fusion.3
  8.7 0.0 copy-start
  8.7 2.7 %collective-permute-start.8 = (bf16[128,1024]{0,1:T(8,128)(2,1)S(1)}, bf16[128,1024]{0,1:T(8,128)(2,1)S(1)}, u32[]{:S(2)}, u32[]{:S(2)}) collective-permute-start(bf16[128,1024]{0,1:T(8,128)(2,1)S(1)} %bitcast.51), channel_id=1, source_target_pairs={{0,24},{8,16},{16,8},{24,0},{1,25},{9,17},{17,9},{25,1},{2,26},{10... | collective-permute-start | bytes 786440 | tf_op jit(solution)/shard_map/ppermute | solution.py:26
  11.4 0.9 %shard_map.76 = (f32[2,512,128]{2,1,0:T(8,128)S(1)}, bf16[2048,128]{1,0:T(8,128)(2,1)S(1)}, bf16[2048,128]{1,0:T(8,128)(2,1)S(1)}) custom-call(s32[1,10]{1,0:T(1,128)S(1)} %copy-done.3, s32[1]{0:T(128)} %bitcast.8.refs_1_, bf16[128,1024]{1,0:T(8,128)(2,1)S(1)} %bitcast.41, bf16[128,1024]{1,0:T(8,128)(2,1)S(1)} %collective-permute-done.refs_3_, ...), custom_call_target="tpu_custom_call" | custom-call | flops 1000000000 | tf_op jit(solution)/shard_map/pallas_call | solution.py:161
  12.4 0.0 collective-permute-done.5.refs_2_.refs_8_
  12.4 0.8 %collective-permute-done.6.refs_3_.refs_9_ = bf16[128,256]{1,0:T(8,128)(2,1)S(1)} collective-permute-done((bf16[128,256]{1,0:T(8,128)(2,1)}, bf16[128,256]{1,0:T(8,128)(2,1)S(1)}, u32[]{:S(2)}, u32[]{:S(2)}) %collective-permute-start.6) | collective-permute-done | bytes 65568 | tf_op jit(solution)/shard_map/ppermute | solution.py:26
  13.2 2.1 %shard_map.77 = (f32[512,2048]{1,0:T(8,128)S(1)}, f32[512,2048]{1,0:T(8,128)S(1)}, f32[8,2048]{1,0:T(8,128)S(1)}) custom-call(bf16[128,256]{1,0:T(8,128)(2,1)S(1)} %bitcast.38, bf16[128,256]{1,0:T(8,128)(2,1)S(1)} %collective-permute-done.4.refs_1_.refs_7_, bf16[128,256]{1,0:T(8,128)(2,1)S(1)} %collective-permute-done.5.refs_2_.refs_8_, ...), custom_call_target="tpu_custom_call" | custom-call | flops 2000000000 | tf_op jit(solution)/shard_map/pallas_call | solution.py:173
  15.3 0.1 collective-permute-start.7
  15.4 1.2 %collective-permute-done.7.refs_3_ = f32[8,2048]{1,0:T(8,128)S(1)} collective-permute-done((f32[8,2048]{1,0:T(8,128)S(1)}, f32[8,2048]{1,0:T(8,128)S(1)}, u32[]{:S(2)}, u32[]{:S(2)}) %collective-permute-start.7) | collective-permute-done | bytes 65568 | tf_op jit(solution)/shard_map/ppermute | solution.py:26
  16.7 1.8 %shard_map.78 = (f32[128,1024]{1,0:T(8,128)S(1)}, f32[128,1024]{1,0:T(8,128)S(1)}, f32[128,256]{1,0:T(8,128)S(1)}, bf16[128,256]{1,0:T(8,128)(2,1)S(1)}, bf16[12...) custom-call(f32[512,2048]{1,0:T(8,128)S(1)} %get-tuple-element.30.refs_0_, ...), custom_call_target="tpu_custom_call" | custom-call | flops 2000000000 | tf_op jit(solution)/shard_map/pallas_call | solution.py:186
  18.4 1.8 %collective-permute-start.10 = (bf16[128,256]{1,0:T(8,128)(2,1)S(1)}, bf16[128,256]{1,0:T(8,128)(2,1)S(1)}, u32[]{:S(2)}, u32[]{:S(2)}) collective-permute-start(bf16[128,256]{1,0:T(8,128)(2,1)S(1)} %get-tuple-element.39), channel_id=1, source_target_pairs={{0,4},{1,5},{2,6},{3,7},{4,0},{5,1},{6,2},{7,3},{8,12},{9,13},{10,... | collective-permute-start | bytes 196616 | tf_op jit(solution)/shard_map/ppermute | solution.py:26
  20.2 1.4 %collective-permute-start.11 = (bf16[128,256]{1,0:T(8,128)(2,1)S(1)}, bf16[128,256]{1,0:T(8,128)(2,1)S(1)}, u32[]{:S(2)}, u32[]{:S(2)}) collective-permute-start(bf16[128,256]{1,0:T(8,128)(2,1)S(1)} %get-tuple-element.40), channel_id=1, source_target_pairs={{0,6},{1,7},{2,4},{3,5},{4,2},{5,3},{6,0},{7,1},{8,14},{9,15},{10,... | collective-permute-start | bytes 196616 | tf_op jit(solution)/shard_map/ppermute | solution.py:26
  21.6 0.4 collective-permute-start.9
  22.0 1.5 %collective-permute-start.2 = (bf16[128,1024]{0,1:T(8,128)(2,1)S(1)}, bf16[128,1024]{0,1:T(8,128)(2,1)S(1)}, u32[]{:S(2)}, u32[]{:S(2)}) collective-permute-start(bf16[128,1024]{0,1:T(8,128)(2,1)S(1)} %bitcast.49), channel_id=1, source_target_pairs={{0,8},{8,0},{16,24},{24,16},{1,9},{9,1},{17,25},{25,17},{2,10},{10... | collective-permute-start | bytes 786440 | tf_op jit(solution)/shard_map/ppermute | solution.py:26
  23.5 1.5 %collective-permute-start.3 = (bf16[128,1024]{0,1:T(8,128)(2,1)S(1)}, bf16[128,1024]{0,1:T(8,128)(2,1)S(1)}, u32[]{:S(2)}, u32[]{:S(2)}) collective-permute-start(bf16[128,1024]{0,1:T(8,128)(2,1)S(1)} %bitcast.48), channel_id=1, source_target_pairs={{0,16},{8,24},{16,0},{24,8},{1,17},{9,25},{17,1},{25,9},{2,18},{10... | collective-permute-start | bytes 786440 | tf_op jit(solution)/shard_map/ppermute | solution.py:26
  25.0 1.7 %collective-permute-done.10 = bf16[128,256]{1,0:T(8,128)(2,1)S(1)} collective-permute-done((bf16[128,256]{1,0:T(8,128)(2,1)S(1)}, bf16[128,256]{1,0:T(8,128)(2,1)S(1)}, u32[]{:S(2)}, u32[]{:S(2)}) %collective-permute-start.10) | collective-permute-done | bytes 65568 | tf_op jit(solution)/shard_map/ppermute | solution.py:26
  26.7 1.1 %collective-permute-done.9 = bf16[128,256]{1,0:T(8,128)(2,1)S(1)} collective-permute-done((bf16[128,256]{1,0:T(8,128)(2,1)S(1)}, bf16[128,256]{1,0:T(8,128)(2,1)S(1)}, u32[]{:S(2)}, u32[]{:S(2)}) %collective-permute-start.9) | collective-permute-done | bytes 65568 | tf_op jit(solution)/shard_map/ppermute | solution.py:26
  27.8 0.0 copy-start.4
  27.8 1.5 %collective-permute-start.12 = (bf16[128,256]{1,0:T(8,128)(2,1)S(1)}, bf16[128,256]{1,0:T(8,128)(2,1)S(1)}, u32[]{:S(2)}, u32[]{:S(2)}) collective-permute-start(bf16[128,256]{1,0:T(8,128)(2,1)S(1)} %add_convert_fusion.1), channel_id=1, source_target_pairs={{0,8},{8,0},{16,24},{24,16},{1,9},{9,1},{17,25},{25,17},{2,10},{10... | collective-permute-start | bytes 196616 | tf_op jit(solution)/shard_map/ppermute | solution.py:26
  29.3 1.5 %collective-permute-start.13 = (bf16[128,256]{1,0:T(8,128)(2,1)S(1)}, bf16[128,256]{1,0:T(8,128)(2,1)S(1)}, u32[]{:S(2)}, u32[]{:S(2)}) collective-permute-start(bf16[128,256]{1,0:T(8,128)(2,1)S(1)} %add_convert_fusion.1), channel_id=1, source_target_pairs={{0,16},{8,24},{16,0},{24,8},{1,17},{9,25},{17,1},{25,9},{2,18},{10... | collective-permute-start | bytes 196616 | tf_op jit(solution)/shard_map/ppermute | solution.py:26
  30.8 0.5 collective-permute-start.14
  31.4 0.8 %collective-permute-done.12 = bf16[128,256]{1,0:T(8,128)(2,1)S(1)} collective-permute-done((bf16[128,256]{1,0:T(8,128)(2,1)S(1)}, bf16[128,256]{1,0:T(8,128)(2,1)S(1)}, u32[]{:S(2)}, u32[]{:S(2)}) %collective-permute-start.12) | collective-permute-done | bytes 65568 | tf_op jit(solution)/shard_map/ppermute | solution.py:26
  32.1 1.4 %collective-permute-done.13 = bf16[128,256]{1,0:T(8,128)(2,1)S(1)} collective-permute-done((bf16[128,256]{1,0:T(8,128)(2,1)S(1)}, bf16[128,256]{1,0:T(8,128)(2,1)S(1)}, u32[]{:S(2)}, u32[]{:S(2)}) %collective-permute-start.13) | collective-permute-done | bytes 65568 | tf_op jit(solution)/shard_map/ppermute | solution.py:26
  33.6 2.4 %collective-permute-done.14 = bf16[128,256]{1,0:T(8,128)(2,1)S(1)} collective-permute-done((bf16[128,256]{1,0:T(8,128)(2,1)S(1)}, bf16[128,256]{1,0:T(8,128)(2,1)S(1)}, u32[]{:S(2)}, u32[]{:S(2)}) %collective-permute-start.14) | collective-permute-done | bytes 65568 | tf_op jit(solution)/shard_map/ppermute | solution.py:26
  36.0 0.4 convolution_multiply_fusion
  36.5 0.1 collective-permute-start.15
  36.6 0.5 collective-permute-start.19
  37.1 1.0 %collective-permute-done.15 = bf16[4,128,256]{2,1,0:T(8,128)(2,1)S(1)} collective-permute-done((bf16[4,128,256]{2,1,0:T(8,128)(2,1)S(1)}, bf16[4,128,256]{2,1,0:T(8,128)(2,1)S(1)}, u32[]{:S(2)}, u32[]{:S(2)}) %collective-permute-start.15) | collective-permute-done | bytes 262176 | tf_op jit(solution)/shard_map/ppermute | solution.py:26
  38.1 0.1 bitcast_add_fusion
  38.2 0.7 %collective-permute-start.16 = (bf16[128,256]{1,0:T(8,128)(2,1)S(1)}, bf16[128,256]{1,0:T(8,128)(2,1)S(1)}, u32[]{:S(2)}, u32[]{:S(2)}) collective-permute-start(bf16[128,256]{1,0:T(8,128)(2,1)S(1)} %get-tuple-element.49), channel_id=1, source_target_pairs={{0,2},{1,3},{2,0},{3,1},{4,6},{5,7},{6,4},{7,5},{8,10},{9,11},{10,... | collective-permute-start | bytes 196616 | tf_op jit(solution)/shard_map/ppermute | solution.py:26
  38.9 1.7 %collective-permute-start.17 = (bf16[128,256]{1,0:T(8,128)(2,1)S(1)}, bf16[128,256]{1,0:T(8,128)(2,1)S(1)}, u32[]{:S(2)}, u32[]{:S(2)}) collective-permute-start(bf16[128,256]{1,0:T(8,128)(2,1)S(1)} %get-tuple-element.51), channel_id=1, source_target_pairs={{0,4},{1,5},{2,6},{3,7},{4,0},{5,1},{6,2},{7,3},{8,12},{9,13},{10,... | collective-permute-start | bytes 196616 | tf_op jit(solution)/shard_map/ppermute | solution.py:26
  40.7 2.0 %collective-permute-start.18 = (bf16[128,256]{1,0:T(8,128)(2,1)S(1)}, bf16[128,256]{1,0:T(8,128)(2,1)S(1)}, u32[]{:S(2)}, u32[]{:S(2)}) collective-permute-start(bf16[128,256]{1,0:T(8,128)(2,1)S(1)} %get-tuple-element.50), channel_id=1, source_target_pairs={{0,6},{1,7},{2,4},{3,5},{4,2},{5,3},{6,0},{7,1},{8,14},{9,15},{10,... | collective-permute-start | bytes 196616 | tf_op jit(solution)/shard_map/ppermute | solution.py:26
  42.7 0.8 %add_convert_fusion = bf16[128,1024]{1,0:T(8,128)(2,1)} fusion(f32[128,1024]{1,0:T(8,128)S(1)} %get-tuple-element.41, f32[128,1024]{1,0:T(8,128)S(1)} %collective-permute-done.19), kind=kLoop, calls=%fused_computation.10 | loop fusion | flops 262144 | bytes 1310720 | tf_op jit(solution)/shard_map/convert_element_type | solution.py:246
  43.4 3.8 %collective-permute-done.17 = bf16[128,256]{1,0:T(8,128)(2,1)S(1)} collective-permute-done((bf16[128,256]{1,0:T(8,128)(2,1)S(1)}, bf16[128,256]{1,0:T(8,128)(2,1)S(1)}, u32[]{:S(2)}, u32[]{:S(2)}) %collective-permute-start.17) | collective-permute-done | bytes 65568 | tf_op jit(solution)/shard_map/ppermute | solution.py:26
  47.2 0.8 %collective-permute-start.20 = (bf16[128,256]{1,0:T(8,128)(2,1)S(1)}, bf16[128,256]{1,0:T(8,128)(2,1)S(1)}, u32[]{:S(2)}, u32[]{:S(2)}) collective-permute-start(bf16[128,256]{1,0:T(8,128)(2,1)S(1)} %fusion.17), channel_id=1, source_target_pairs={{0,24},{8,16},{16,8},{24,0},{1,25},{9,17},{17,9},{25,1},{2,26},{10... | collective-permute-start | bytes 196616 | tf_op jit(solution)/shard_map/ppermute | solution.py:26
  48.0 1.3 %collective-permute-start.21 = (bf16[128,256]{1,0:T(8,128)(2,1)S(1)}, bf16[128,256]{1,0:T(8,128)(2,1)S(1)}, u32[]{:S(2)}, u32[]{:S(2)}) collective-permute-start(bf16[128,256]{1,0:T(8,128)(2,1)S(1)} %fusion.17), channel_id=1, source_target_pairs={{0,16},{8,24},{16,0},{24,8},{1,17},{9,25},{17,1},{25,9},{2,18},{10... | collective-permute-start | bytes 196616 | tf_op jit(solution)/shard_map/ppermute | solution.py:26
  49.3 1.5 %collective-permute-start.22 = (bf16[128,256]{1,0:T(8,128)(2,1)S(1)}, bf16[128,256]{1,0:T(8,128)(2,1)S(1)}, u32[]{:S(2)}, u32[]{:S(2)}) collective-permute-start(bf16[128,256]{1,0:T(8,128)(2,1)S(1)} %fusion.17), channel_id=1, source_target_pairs={{0,8},{8,0},{16,24},{24,16},{1,9},{9,1},{17,25},{25,17},{2,10},{10... | collective-permute-start | bytes 196616 | tf_op jit(solution)/shard_map/ppermute | solution.py:26
  50.8 1.8 %collective-permute-done.20 = bf16[128,256]{1,0:T(8,128)(2,1)S(1)} collective-permute-done((bf16[128,256]{1,0:T(8,128)(2,1)S(1)}, bf16[128,256]{1,0:T(8,128)(2,1)S(1)}, u32[]{:S(2)}, u32[]{:S(2)}) %collective-permute-start.20) | collective-permute-done | bytes 65568 | tf_op jit(solution)/shard_map/ppermute | solution.py:26
  52.6 0.4 collective-permute-done.21
  53.0 0.6 %collective-permute-done.22 = bf16[128,256]{1,0:T(8,128)(2,1)S(1)} collective-permute-done((bf16[128,256]{1,0:T(8,128)(2,1)S(1)}, bf16[128,256]{1,0:T(8,128)(2,1)S(1)}, u32[]{:S(2)}, u32[]{:S(2)}) %collective-permute-start.22) | collective-permute-done | bytes 65568 | tf_op jit(solution)/shard_map/ppermute | solution.py:26
  53.6 0.8 %maximum_convert_fusion = f32[512,256]{1,0:T(8,128)} fusion(bf16[128,256]{1,0:T(8,128)(2,1)S(1)} %get-tuple-element.55, bf16[128,256]{1,0:T(8,128)(2,1)S(1)} %get-tuple-element.54, bf16[128,256]{1,0:T(8,128)(2,1)S(1)} %get-tuple-element.53, bf16[128,256]{1,0:T(8,128)(2,1)S(1)} %get-tuple-element.52), kind=kLoop, calls=%fused_computation.19 | loop fusion | flops 1048576 | bytes 786432 | tf_op jit(solution)/shard_map/concatenate | solution.py:271
  (22 shorter events, 0.2 us)
Async XLA Ops:
  0.6 7.9 %collective-permute-start = (bf16[128,1024]{1,0:T(8,128)(2,1)}, bf16[128,1024]{1,0:T(8,128)(2,1)S(1)}, u32[]{:S(2)}, u32[]{:S(2)}) collective-permute-start(bf16[128,1024]{1,0:T(8,128)(2,1)} %bitcast.40), channel_id=1, source_target_pairs={{0,1},{1,0},{2,3},{3,2},{4,5},{5,4},{6,7},{7,6},{8,9},{9,8},{10,11... | collective-permute-start | bytes 786440 | tf_op jit(solution)/shard_map/ppermute | solution.py:26
  1.1 7.4 %collective-permute-start.1 = (bf16[128,1024]{1,0:T(8,128)(2,1)}, bf16[128,1024]{1,0:T(8,128)(2,1)S(1)}, u32[]{:S(2)}, u32[]{:S(2)}) collective-permute-start(bf16[128,1024]{1,0:T(8,128)(2,1)} %bitcast.42), channel_id=1, source_target_pairs={{0,1},{1,0},{2,3},{3,2},{4,5},{5,4},{6,7},{7,6},{8,9},{9,8},{10,11... | collective-permute-start | bytes 786440 | tf_op jit(solution)/shard_map/ppermute | solution.py:26
  1.2 11.2 %collective-permute-start.4 = (bf16[128,256]{1,0:T(8,128)(2,1)}, bf16[128,256]{1,0:T(8,128)(2,1)S(1)}, u32[]{:S(2)}, u32[]{:S(2)}) collective-permute-start(bf16[128,256]{1,0:T(8,128)(2,1)} %bitcast.35), channel_id=1, source_target_pairs={{0,2},{1,3},{2,0},{3,1},{4,6},{5,7},{6,4},{7,5},{8,10},{9,11},{10,... | collective-permute-start | bytes 196616 | tf_op jit(solution)/shard_map/ppermute | solution.py:26
  4.2 8.2 %collective-permute-start.5 = (bf16[128,256]{1,0:T(8,128)(2,1)}, bf16[128,256]{1,0:T(8,128)(2,1)S(1)}, u32[]{:S(2)}, u32[]{:S(2)}) collective-permute-start(bf16[128,256]{1,0:T(8,128)(2,1)} %bitcast.36), channel_id=1, source_target_pairs={{0,4},{1,5},{2,6},{3,7},{4,0},{5,1},{6,2},{7,3},{8,12},{9,13},{10,... | collective-permute-start | bytes 196616 | tf_op jit(solution)/shard_map/ppermute | solution.py:26
  6.8 6.4 %collective-permute-start.6 = (bf16[128,256]{1,0:T(8,128)(2,1)}, bf16[128,256]{1,0:T(8,128)(2,1)S(1)}, u32[]{:S(2)}, u32[]{:S(2)}) collective-permute-start(bf16[128,256]{1,0:T(8,128)(2,1)} %bitcast.37), channel_id=1, source_target_pairs={{0,6},{1,7},{2,4},{3,5},{4,2},{5,3},{6,0},{7,1},{8,14},{9,15},{10,... | collective-permute-start | bytes 196616 | tf_op jit(solution)/shard_map/ppermute | solution.py:26
  6.8 4.6 %copy-start.1 = (bf16[1,1,128,1024]{3,2,1,0:T(8,128)(2,1)S(1)}, bf16[1,1,128,1024]{3,2,1,0:T(8,128)(2,1)}, u32[]{:S(2)}) copy-start(bf16[1,1,128,1024]{3,2,1,0:T(8,128)(2,1)} %param.6) | copy-start | bytes 786436
  6.8 4.6 %copy-start.2 = (bf16[1,1,128,1024]{3,2,1,0:T(8,128)(2,1)S(1)}, bf16[1,1,128,1024]{3,2,1,0:T(8,128)(2,1)}, u32[]{:S(2)}) copy-start(bf16[1,1,128,1024]{3,2,1,0:T(8,128)(2,1)} %param.8) | copy-start | bytes 786436
  6.8 4.6 %copy-start.3 = (s32[1,10]{1,0:T(1,128)S(1)}, s32[1,10]{1,0:T(1,128)}, u32[]{:S(2)}) copy-start(s32[1,10]{1,0:T(1,128)} %refs_0_.1) | copy-start | bytes 124
  8.7 4.5 %copy-start = (bf16[1,1,128,256]{3,2,1,0:T(8,128)(2,1)S(1)}, bf16[1,1,128,256]{3,2,1,0:T(8,128)(2,1)}, u32[]{:S(2)}) copy-start(bf16[1,1,128,256]{3,2,1,0:T(8,128)(2,1)} %param.7) | copy-start | bytes 196612
  8.7 9.7 %collective-permute-start.8 = (bf16[128,1024]{0,1:T(8,128)(2,1)S(1)}, bf16[128,1024]{0,1:T(8,128)(2,1)S(1)}, u32[]{:S(2)}, u32[]{:S(2)}) collective-permute-start(bf16[128,1024]{0,1:T(8,128)(2,1)S(1)} %bitcast.51), channel_id=1, source_target_pairs={{0,24},{8,16},{16,8},{24,0},{1,25},{9,17},{17,9},{25,1},{2,26},{10... | collective-permute-start | bytes 786440 | tf_op jit(solution)/shard_map/ppermute | solution.py:26
  15.3 1.3 %collective-permute-start.7 = (f32[8,2048]{1,0:T(8,128)S(1)}, f32[8,2048]{1,0:T(8,128)S(1)}, u32[]{:S(2)}, u32[]{:S(2)}) collective-permute-start(f32[8,2048]{1,0:T(8,128)S(1)} %get-tuple-element.32.refs_2_), channel_id=1, source_target_pairs={{0,1},{1,0},{2,3},{3,2},{4,5},{5,4},{6,7},{7,6},{8,9},{9,8},{10,11... | collective-permute-start | bytes 196616 | tf_op jit(solution)/shard_map/ppermute | solution.py:26
  18.4 8.3 %collective-permute-start.10 = (bf16[128,256]{1,0:T(8,128)(2,1)S(1)}, bf16[128,256]{1,0:T(8,128)(2,1)S(1)}, u32[]{:S(2)}, u32[]{:S(2)}) collective-permute-start(bf16[128,256]{1,0:T(8,128)(2,1)S(1)} %get-tuple-element.39), channel_id=1, source_target_pairs={{0,4},{1,5},{2,6},{3,7},{4,0},{5,1},{6,2},{7,3},{8,12},{9,13},{10,... | collective-permute-start | bytes 196616 | tf_op jit(solution)/shard_map/ppermute | solution.py:26
  20.2 6.5 %collective-permute-start.11 = (bf16[128,256]{1,0:T(8,128)(2,1)S(1)}, bf16[128,256]{1,0:T(8,128)(2,1)S(1)}, u32[]{:S(2)}, u32[]{:S(2)}) collective-permute-start(bf16[128,256]{1,0:T(8,128)(2,1)S(1)} %get-tuple-element.40), channel_id=1, source_target_pairs={{0,6},{1,7},{2,4},{3,5},{4,2},{5,3},{6,0},{7,1},{8,14},{9,15},{10,... | collective-permute-start | bytes 196616 | tf_op jit(solution)/shard_map/ppermute | solution.py:26
  21.6 6.1 %collective-permute-start.9 = (bf16[128,256]{1,0:T(8,128)(2,1)S(1)}, bf16[128,256]{1,0:T(8,128)(2,1)S(1)}, u32[]{:S(2)}, u32[]{:S(2)}) collective-permute-start(bf16[128,256]{1,0:T(8,128)(2,1)S(1)} %get-tuple-element.38), channel_id=1, source_target_pairs={{0,2},{1,3},{2,0},{3,1},{4,6},{5,7},{6,4},{7,5},{8,10},{9,11},{10,... | collective-permute-start | bytes 196616 | tf_op jit(solution)/shard_map/ppermute | solution.py:26
  22.0 9.4 %collective-permute-start.2 = (bf16[128,1024]{0,1:T(8,128)(2,1)S(1)}, bf16[128,1024]{0,1:T(8,128)(2,1)S(1)}, u32[]{:S(2)}, u32[]{:S(2)}) collective-permute-start(bf16[128,1024]{0,1:T(8,128)(2,1)S(1)} %bitcast.49), channel_id=1, source_target_pairs={{0,8},{8,0},{16,24},{24,16},{1,9},{9,1},{17,25},{25,17},{2,10},{10... | collective-permute-start | bytes 786440 | tf_op jit(solution)/shard_map/ppermute | solution.py:26
  23.5 7.9 %collective-permute-start.3 = (bf16[128,1024]{0,1:T(8,128)(2,1)S(1)}, bf16[128,1024]{0,1:T(8,128)(2,1)S(1)}, u32[]{:S(2)}, u32[]{:S(2)}) collective-permute-start(bf16[128,1024]{0,1:T(8,128)(2,1)S(1)} %bitcast.48), channel_id=1, source_target_pairs={{0,16},{8,24},{16,0},{24,8},{1,17},{9,25},{17,1},{25,9},{2,18},{10... | collective-permute-start | bytes 786440 | tf_op jit(solution)/shard_map/ppermute | solution.py:26
  27.8 8.6 %copy-start.4 = (bf16[128,256]{1,0:T(8,128)(2,1)}, bf16[128,256]{1,0:T(8,128)(2,1)S(1)}, u32[]{:S(2)}) copy-start(bf16[128,256]{1,0:T(8,128)(2,1)S(1)} %add_convert_fusion.1) | copy-start | bytes 196612
  27.8 4.3 %collective-permute-start.12 = (bf16[128,256]{1,0:T(8,128)(2,1)S(1)}, bf16[128,256]{1,0:T(8,128)(2,1)S(1)}, u32[]{:S(2)}, u32[]{:S(2)}) collective-permute-start(bf16[128,256]{1,0:T(8,128)(2,1)S(1)} %add_convert_fusion.1), channel_id=1, source_target_pairs={{0,8},{8,0},{16,24},{24,16},{1,9},{9,1},{17,25},{25,17},{2,10},{10... | collective-permute-start | bytes 196616 | tf_op jit(solution)/shard_map/ppermute | solution.py:26
  29.3 4.3 %collective-permute-start.13 = (bf16[128,256]{1,0:T(8,128)(2,1)S(1)}, bf16[128,256]{1,0:T(8,128)(2,1)S(1)}, u32[]{:S(2)}, u32[]{:S(2)}) collective-permute-start(bf16[128,256]{1,0:T(8,128)(2,1)S(1)} %add_convert_fusion.1), channel_id=1, source_target_pairs={{0,16},{8,24},{16,0},{24,8},{1,17},{9,25},{17,1},{25,9},{2,18},{10... | collective-permute-start | bytes 196616 | tf_op jit(solution)/shard_map/ppermute | solution.py:26
  30.8 5.2 %collective-permute-start.14 = (bf16[128,256]{1,0:T(8,128)(2,1)S(1)}, bf16[128,256]{1,0:T(8,128)(2,1)S(1)}, u32[]{:S(2)}, u32[]{:S(2)}) collective-permute-start(bf16[128,256]{1,0:T(8,128)(2,1)S(1)} %add_convert_fusion.1), channel_id=1, source_target_pairs={{0,24},{8,16},{16,8},{24,0},{1,25},{9,17},{17,9},{25,1},{2,26},{10... | collective-permute-start | bytes 196616 | tf_op jit(solution)/shard_map/ppermute | solution.py:26
  36.5 1.6 %collective-permute-start.15 = (bf16[4,128,256]{2,1,0:T(8,128)(2,1)S(1)}, bf16[4,128,256]{2,1,0:T(8,128)(2,1)S(1)}, u32[]{:S(2)}, u32[]{:S(2)}) collective-permute-start(bf16[4,128,256]{2,1,0:T(8,128)(2,1)S(1)} %fusion.7), channel_id=1, source_target_pairs={{0,1},{1,0},{2,3},{3,2},{4,5},{5,4},{6,7},{7,6},{8,9},{9,8},{10,11... | collective-permute-start | bytes 786440 | tf_op jit(solution)/shard_map/ppermute | solution.py:26
  36.6 6.1 %collective-permute-start.19 = (f32[128,1024]{1,0:T(8,128)S(1)}, f32[128,1024]{1,0:T(8,128)S(1)}, u32[]{:S(2)}, u32[]{:S(2)}) collective-permute-start(f32[128,1024]{1,0:T(8,128)S(1)} %get-tuple-element.42), channel_id=1, source_target_pairs={{0,1},{1,0},{2,3},{3,2},{4,5},{5,4},{6,7},{7,6},{8,9},{9,8},{10,11... | collective-permute-start | bytes 1572872 | tf_op jit(solution)/shard_map/ppermute | solution.py:26
  38.2 5.2 %collective-permute-start.16 = (bf16[128,256]{1,0:T(8,128)(2,1)S(1)}, bf16[128,256]{1,0:T(8,128)(2,1)S(1)}, u32[]{:S(2)}, u32[]{:S(2)}) collective-permute-start(bf16[128,256]{1,0:T(8,128)(2,1)S(1)} %get-tuple-element.49), channel_id=1, source_target_pairs={{0,2},{1,3},{2,0},{3,1},{4,6},{5,7},{6,4},{7,5},{8,10},{9,11},{10,... | collective-permute-start | bytes 196616 | tf_op jit(solution)/shard_map/ppermute | solution.py:26
  38.9 8.3 %collective-permute-start.17 = (bf16[128,256]{1,0:T(8,128)(2,1)S(1)}, bf16[128,256]{1,0:T(8,128)(2,1)S(1)}, u32[]{:S(2)}, u32[]{:S(2)}) collective-permute-start(bf16[128,256]{1,0:T(8,128)(2,1)S(1)} %get-tuple-element.51), channel_id=1, source_target_pairs={{0,4},{1,5},{2,6},{3,7},{4,0},{5,1},{6,2},{7,3},{8,12},{9,13},{10,... | collective-permute-start | bytes 196616 | tf_op jit(solution)/shard_map/ppermute | solution.py:26
  40.7 6.5 %collective-permute-start.18 = (bf16[128,256]{1,0:T(8,128)(2,1)S(1)}, bf16[128,256]{1,0:T(8,128)(2,1)S(1)}, u32[]{:S(2)}, u32[]{:S(2)}) collective-permute-start(bf16[128,256]{1,0:T(8,128)(2,1)S(1)} %get-tuple-element.50), channel_id=1, source_target_pairs={{0,6},{1,7},{2,4},{3,5},{4,2},{5,3},{6,0},{7,1},{8,14},{9,15},{10,... | collective-permute-start | bytes 196616 | tf_op jit(solution)/shard_map/ppermute | solution.py:26
  47.2 5.3 %collective-permute-start.20 = (bf16[128,256]{1,0:T(8,128)(2,1)S(1)}, bf16[128,256]{1,0:T(8,128)(2,1)S(1)}, u32[]{:S(2)}, u32[]{:S(2)}) collective-permute-start(bf16[128,256]{1,0:T(8,128)(2,1)S(1)} %fusion.17), channel_id=1, source_target_pairs={{0,24},{8,16},{16,8},{24,0},{1,25},{9,17},{17,9},{25,1},{2,26},{10... | collective-permute-start | bytes 196616 | tf_op jit(solution)/shard_map/ppermute | solution.py:26
  48.0 5.0 %collective-permute-start.21 = (bf16[128,256]{1,0:T(8,128)(2,1)S(1)}, bf16[128,256]{1,0:T(8,128)(2,1)S(1)}, u32[]{:S(2)}, u32[]{:S(2)}) collective-permute-start(bf16[128,256]{1,0:T(8,128)(2,1)S(1)} %fusion.17), channel_id=1, source_target_pairs={{0,16},{8,24},{16,0},{24,8},{1,17},{9,25},{17,1},{25,9},{2,18},{10... | collective-permute-start | bytes 196616 | tf_op jit(solution)/shard_map/ppermute | solution.py:26
  49.3 4.3 %collective-permute-start.22 = (bf16[128,256]{1,0:T(8,128)(2,1)S(1)}, bf16[128,256]{1,0:T(8,128)(2,1)S(1)}, u32[]{:S(2)}, u32[]{:S(2)}) collective-permute-start(bf16[128,256]{1,0:T(8,128)(2,1)S(1)} %fusion.17), channel_id=1, source_target_pairs={{0,8},{8,0},{16,24},{24,16},{1,9},{9,1},{17,25},{25,17},{2,10},{10... | collective-permute-start | bytes 196616 | tf_op jit(solution)/shard_map/ppermute | solution.py:26

commit v5 on v4

--- a/solution.py
+++ b/solution.py
@@ -73,17 +73,18 @@
     bias, q_rows, do_rows, e_ref, d_ref, stat_ref = refs[half:]
     heads = q_rows.shape[0] // (2 * local)
     coef = SCALE * LOG2E
-    width = 2 * local
+    width = 4 * local
     for b in range(2):
-        for pair in range(heads // 2):
-            cols = slice((b * heads + 2 * pair) * local, (b * heads + 2 * pair + 2) * local)
+        for group in range(heads // 4):
+            first = b * heads + 4 * group
+            cols = slice(first * local, (first + 4) * local)
             q2 = q_rows[cols, :]
             do2 = do_rows[cols, :]
             top = jnp.full((8, width), NEG, jnp.float32)
             for k in range(half):
                 rows = slice(k * local, (k + 1) * local)
                 add = bias[b, rows, :]
-                x = dot(kv_refs[k][:, :HD], q2, NT) + jnp.concatenate([add, add], axis=1)
+                x = dot(kv_refs[k][:, :HD], q2, NT) + jnp.concatenate([add] * 4, axis=1)
                 e_ref[rows, cols] = x
                 top = jnp.maximum(top, jnp.max(fold(x), axis=0))
             top = jnp.max(top, axis=0, keepdims=True) * coef
@@ -240,7 +241,7 @@
     for k, slab in zip((3,), early):
         x_slabs[k] = slab
 
-    terms = [swap(parts[k - 1], "ctx", 2 * k) for k in range(1, half)]
+    terms = [swap(parts[k - 1], "ctx", 2 * k) for k in reversed(range(1, half))]
     gkv = own + sum(t.astype(jnp.float32) for t in terms)
     gkv = gkv.astype(jnp.bfloat16)
     gq = (gq + swap(gq_other, "ctx", 1)).astype(jnp.bfloat16)
@@ -256,7 +257,7 @@
     w_chip = w_own + swap(w_sib.astype(jnp.bfloat16), "ctx", 1).astype(jnp.float32)
     z = me // 2
     w_mine = lax.dynamic_index_in_dim(w_chip, z, 0, keepdims=False)
-    for k in range(1, half):
+    for k in reversed(range(1, half)):
         block = lax.dynamic_index_in_dim(w_chip, z ^ k, 0, keepdims=False)
         w_mine = w_mine + swap(block.astype(jnp.bfloat16), "ctx", 2 * k).astype(jnp.float32)
 

time: 54.6 us -> 54.2 us (level)
  starting transfers between devices: 27.7 us -> 28.6 us
  waiting for transfers between devices: 17 us -> 16.1 us
    ppermute x23, waiting for transfers between devices: 17 us -> 16.1 us  [swap(): return lax.ppermute(x, axis, [(i, i ^ mask) for i in range(size)])]
    ppermute x23, starting transfers between devices: 27.7 us -> 28.6 us  [swap(): return lax.ppermute(x, axis, [(i, i ^ mask) for i in range(size)])]
  transfers between devices with their start and end apart: 23 -> 23, of which waited for: 12 -> 12; matrix products, arithmetic and copies ran while one was open for 5% -> 5% of each run, Pallas kernels for 9% -> 8%
where the time goes in v5:
time: 54.2 us; the launch traced here: 54 us
  starting transfers between devices  28.6 us (53%)
  waiting for transfers between devices  16.1 us (30%)
  Pallas kernels  4.47 us (8%)
  local copies, waits for them, and re-layouts  1.9 us (4%)
  other arithmetic  1.73 us (3%)
  between operations  0.83 us (2%)
    ppermute x23, starting transfers between devices, swap(): return lax.ppermute(x, axis, [(i, i ^ mask) for i in range(size)])  28.6 us
    ppermute x23, waiting for transfers between devices, swap(): return lax.ppermute(x, axis, [(i, i ^ mask) for i in range(size)])  16.1 us
    pallas_call x1, Pallas kernels, attention(): pl.pallas_call(functools.partial(scores_kernel, half, local), out_shape=(...  1.78 us
    pallas_call x1, Pallas kernels, attention(): pl.pallas_call(functools.partial(gradients_kernel, half, local), out_shap...  1.76 us
    unnamed x11, local copies, waits for them, and re-layouts  1.73 us
  transfers between devices with their start and end apart: 23, of which 12 were waited for; matrix products, arithmetic and copies ran while one was open for 5% of the time, Pallas kernels for 8%

profile of v5, /device:TPU:0, one launch (start us, length us, event | category | flops | bytes accessed | tf_op | source)
XLA Modules:
  0.0 54.0 jit_solution(16414160046947150425)
XLA Ops:
  0.6 0.5 collective-permute-start
  1.1 0.1 collective-permute-start.1
  1.2 3.0 %collective-permute-start.4 = (bf16[128,256]{1,0:T(8,128)(2,1)}, bf16[128,256]{1,0:T(8,128)(2,1)S(1)}, u32[]{:S(2)}, u32[]{:S(2)}) collective-permute-start(bf16[128,256]{1,0:T(8,128)(2,1)} %bitcast.35), channel_id=1, source_target_pairs={{0,2},{1,3},{2,0},{3,1},{4,6},{5,7},{6,4},{7,5},{8,10},{9,11},{10,... | collective-permute-start | bytes 196616 | tf_op jit(solution)/shard_map/ppermute | solution.py:26
  4.2 2.6 %collective-permute-start.5 = (bf16[128,256]{1,0:T(8,128)(2,1)}, bf16[128,256]{1,0:T(8,128)(2,1)S(1)}, u32[]{:S(2)}, u32[]{:S(2)}) collective-permute-start(bf16[128,256]{1,0:T(8,128)(2,1)} %bitcast.36), channel_id=1, source_target_pairs={{0,4},{1,5},{2,6},{3,7},{4,0},{5,1},{6,2},{7,3},{8,12},{9,13},{10,... | collective-permute-start | bytes 196616 | tf_op jit(solution)/shard_map/ppermute | solution.py:26
  6.8 0.0 collective-permute-start.6
  6.8 1.7 %copy.10 = bf16[1,1,128,4096]{2,3,1,0:T(8,128)(2,1)S(1)} copy(bf16[1,1,128,4096]{3,2,1,0:T(8,128)(2,1)} %param.5) | data formatting | bytes 2097152 | tf_op args[0]
  8.6 0.0 collective-permute-done.refs_3_
  8.6 0.1 constant_dynamic-slice_fusion.3
  8.7 0.0 copy-start
  8.7 2.7 %collective-permute-start.8 = (bf16[128,1024]{0,1:T(8,128)(2,1)S(1)}, bf16[128,1024]{0,1:T(8,128)(2,1)S(1)}, u32[]{:S(2)}, u32[]{:S(2)}) collective-permute-start(bf16[128,1024]{0,1:T(8,128)(2,1)S(1)} %bitcast.51), channel_id=1, source_target_pairs={{0,24},{8,16},{16,8},{24,0},{1,25},{9,17},{17,9},{25,1},{2,26},{10... | collective-permute-start | bytes 786440 | tf_op jit(solution)/shard_map/ppermute | solution.py:26
  11.4 0.9 %shard_map.76 = (f32[2,512,128]{2,1,0:T(8,128)S(1)}, bf16[2048,128]{1,0:T(8,128)(2,1)S(1)}, bf16[2048,128]{1,0:T(8,128)(2,1)S(1)}) custom-call(s32[1,10]{1,0:T(1,128)S(1)} %copy-done.3, s32[1]{0:T(128)} %bitcast.8.refs_1_, bf16[128,1024]{1,0:T(8,128)(2,1)S(1)} %bitcast.41, bf16[128,1024]{1,0:T(8,128)(2,1)S(1)} %collective-permute-done.refs_3_, ...), custom_call_target="tpu_custom_call" | custom-call | flops 1000000000 | tf_op jit(solution)/shard_map/pallas_call | solution.py:162
  12.4 0.0 collective-permute-done.5.refs_2_.refs_8_
  12.4 0.8 %collective-permute-done.6.refs_3_.refs_9_ = bf16[128,256]{1,0:T(8,128)(2,1)S(1)} collective-permute-done((bf16[128,256]{1,0:T(8,128)(2,1)}, bf16[128,256]{1,0:T(8,128)(2,1)S(1)}, u32[]{:S(2)}, u32[]{:S(2)}) %collective-permute-start.6) | collective-permute-done | bytes 65568 | tf_op jit(solution)/shard_map/ppermute | solution.py:26
  13.2 1.8 %shard_map.77 = (f32[512,2048]{1,0:T(8,128)S(1)}, f32[512,2048]{1,0:T(8,128)S(1)}, f32[8,2048]{1,0:T(8,128)S(1)}) custom-call(bf16[128,256]{1,0:T(8,128)(2,1)S(1)} %bitcast.38, bf16[128,256]{1,0:T(8,128)(2,1)S(1)} %collective-permute-done.4.refs_1_.refs_7_, bf16[128,256]{1,0:T(8,128)(2,1)S(1)} %collective-permute-done.5.refs_2_.refs_8_, ...), custom_call_target="tpu_custom_call" | custom-call | flops 2000000000 | tf_op jit(solution)/shard_map/pallas_call | solution.py:174
  15.0 0.1 collective-permute-start.7
  15.1 1.2 %collective-permute-done.7.refs_3_ = f32[8,2048]{1,0:T(8,128)S(1)} collective-permute-done((f32[8,2048]{1,0:T(8,128)S(1)}, f32[8,2048]{1,0:T(8,128)S(1)}, u32[]{:S(2)}, u32[]{:S(2)}) %collective-permute-start.7) | collective-permute-done | bytes 65568 | tf_op jit(solution)/shard_map/ppermute | solution.py:26
  16.3 1.8 %shard_map.78 = (f32[128,1024]{1,0:T(8,128)S(1)}, f32[128,1024]{1,0:T(8,128)S(1)}, f32[128,256]{1,0:T(8,128)S(1)}, bf16[128,256]{1,0:T(8,128)(2,1)S(1)}, bf16[12...) custom-call(f32[512,2048]{1,0:T(8,128)S(1)} %get-tuple-element.30.refs_0_, ...), custom_call_target="tpu_custom_call" | custom-call | flops 2000000000 | tf_op jit(solution)/shard_map/pallas_call | solution.py:187
  18.1 1.8 %collective-permute-start.10 = (bf16[128,256]{1,0:T(8,128)(2,1)S(1)}, bf16[128,256]{1,0:T(8,128)(2,1)S(1)}, u32[]{:S(2)}, u32[]{:S(2)}) collective-permute-start(bf16[128,256]{1,0:T(8,128)(2,1)S(1)} %get-tuple-element.39), channel_id=1, source_target_pairs={{0,4},{1,5},{2,6},{3,7},{4,0},{5,1},{6,2},{7,3},{8,12},{9,13},{10,... | collective-permute-start | bytes 196616 | tf_op jit(solution)/shard_map/ppermute | solution.py:26
  19.9 1.7 %collective-permute-start.11 = (bf16[128,256]{1,0:T(8,128)(2,1)S(1)}, bf16[128,256]{1,0:T(8,128)(2,1)S(1)}, u32[]{:S(2)}, u32[]{:S(2)}) collective-permute-start(bf16[128,256]{1,0:T(8,128)(2,1)S(1)} %get-tuple-element.40), channel_id=1, source_target_pairs={{0,2},{1,3},{2,0},{3,1},{4,6},{5,7},{6,4},{7,5},{8,10},{9,11},{10,... | collective-permute-start | bytes 196616 | tf_op jit(solution)/shard_map/ppermute | solution.py:26
  21.5 1.0 %collective-permute-start.9 = (bf16[128,256]{1,0:T(8,128)(2,1)S(1)}, bf16[128,256]{1,0:T(8,128)(2,1)S(1)}, u32[]{:S(2)}, u32[]{:S(2)}) collective-permute-start(bf16[128,256]{1,0:T(8,128)(2,1)S(1)} %get-tuple-element.38), channel_id=1, source_target_pairs={{0,6},{1,7},{2,4},{3,5},{4,2},{5,3},{6,0},{7,1},{8,14},{9,15},{10,... | collective-permute-start | bytes 196616 | tf_op jit(solution)/shard_map/ppermute | solution.py:26
  22.5 1.5 %collective-permute-start.2 = (bf16[128,1024]{0,1:T(8,128)(2,1)S(1)}, bf16[128,1024]{0,1:T(8,128)(2,1)S(1)}, u32[]{:S(2)}, u32[]{:S(2)}) collective-permute-start(bf16[128,1024]{0,1:T(8,128)(2,1)S(1)} %bitcast.49), channel_id=1, source_target_pairs={{0,8},{8,0},{16,24},{24,16},{1,9},{9,1},{17,25},{25,17},{2,10},{10... | collective-permute-start | bytes 786440 | tf_op jit(solution)/shard_map/ppermute | solution.py:26
  24.0 1.5 %collective-permute-start.3 = (bf16[128,1024]{0,1:T(8,128)(2,1)S(1)}, bf16[128,1024]{0,1:T(8,128)(2,1)S(1)}, u32[]{:S(2)}, u32[]{:S(2)}) collective-permute-start(bf16[128,1024]{0,1:T(8,128)(2,1)S(1)} %bitcast.48), channel_id=1, source_target_pairs={{0,16},{8,24},{16,0},{24,8},{1,17},{9,25},{17,1},{25,9},{2,18},{10... | collective-permute-start | bytes 786440 | tf_op jit(solution)/shard_map/ppermute | solution.py:26
  25.6 2.0 %collective-permute-done.9 = bf16[128,256]{1,0:T(8,128)(2,1)S(1)} collective-permute-done((bf16[128,256]{1,0:T(8,128)(2,1)S(1)}, bf16[128,256]{1,0:T(8,128)(2,1)S(1)}, u32[]{:S(2)}, u32[]{:S(2)}) %collective-permute-start.9) | collective-permute-done | bytes 65568 | tf_op jit(solution)/shard_map/ppermute | solution.py:26
  27.6 0.0 copy-start.4
  27.7 1.5 %collective-permute-start.12 = (bf16[128,256]{1,0:T(8,128)(2,1)S(1)}, bf16[128,256]{1,0:T(8,128)(2,1)S(1)}, u32[]{:S(2)}, u32[]{:S(2)}) collective-permute-start(bf16[128,256]{1,0:T(8,128)(2,1)S(1)} %add_convert_fusion.1), channel_id=1, source_target_pairs={{0,8},{8,0},{16,24},{24,16},{1,9},{9,1},{17,25},{25,17},{2,10},{10... | collective-permute-start | bytes 196616 | tf_op jit(solution)/shard_map/ppermute | solution.py:26
  29.2 1.5 %collective-permute-start.13 = (bf16[128,256]{1,0:T(8,128)(2,1)S(1)}, bf16[128,256]{1,0:T(8,128)(2,1)S(1)}, u32[]{:S(2)}, u32[]{:S(2)}) collective-permute-start(bf16[128,256]{1,0:T(8,128)(2,1)S(1)} %add_convert_fusion.1), channel_id=1, source_target_pairs={{0,16},{8,24},{16,0},{24,8},{1,17},{9,25},{17,1},{25,9},{2,18},{10... | collective-permute-start | bytes 196616 | tf_op jit(solution)/shard_map/ppermute | solution.py:26
  30.7 0.5 collective-permute-start.14
  31.2 1.4 %collective-permute-done.3 = bf16[128,1024]{0,1:T(8,128)(2,1)S(1)} collective-permute-done((bf16[128,1024]{0,1:T(8,128)(2,1)S(1)}, bf16[128,1024]{0,1:T(8,128)(2,1)S(1)}, u32[]{:S(2)}, u32[]{:S(2)}) %collective-permute-start.3) | collective-permute-done | bytes 262176 | tf_op jit(solution)/shard_map/ppermute | solution.py:26
  32.7 0.8 %collective-permute-done.13 = bf16[128,256]{1,0:T(8,128)(2,1)S(1)} collective-permute-done((bf16[128,256]{1,0:T(8,128)(2,1)S(1)}, bf16[128,256]{1,0:T(8,128)(2,1)S(1)}, u32[]{:S(2)}, u32[]{:S(2)}) %collective-permute-start.13) | collective-permute-done | bytes 65568 | tf_op jit(solution)/shard_map/ppermute | solution.py:26
  33.4 2.4 %collective-permute-done.14 = bf16[128,256]{1,0:T(8,128)(2,1)S(1)} collective-permute-done((bf16[128,256]{1,0:T(8,128)(2,1)S(1)}, bf16[128,256]{1,0:T(8,128)(2,1)S(1)}, u32[]{:S(2)}, u32[]{:S(2)}) %collective-permute-start.14) | collective-permute-done | bytes 65568 | tf_op jit(solution)/shard_map/ppermute | solution.py:26
  35.9 0.4 convolution_multiply_fusion
  36.3 0.1 collective-permute-start.15
  36.4 0.5 collective-permute-start.19
  36.9 1.0 %collective-permute-done.15 = bf16[4,128,256]{2,1,0:T(8,128)(2,1)S(1)} collective-permute-done((bf16[4,128,256]{2,1,0:T(8,128)(2,1)S(1)}, bf16[4,128,256]{2,1,0:T(8,128)(2,1)S(1)}, u32[]{:S(2)}, u32[]{:S(2)}) %collective-permute-start.15) | collective-permute-done | bytes 262176 | tf_op jit(solution)/shard_map/ppermute | solution.py:26
  37.9 0.1 bitcast_add_fusion
  38.0 1.2 %collective-permute-start.16 = (bf16[128,256]{1,0:T(8,128)(2,1)S(1)}, bf16[128,256]{1,0:T(8,128)(2,1)S(1)}, u32[]{:S(2)}, u32[]{:S(2)}) collective-permute-start(bf16[128,256]{1,0:T(8,128)(2,1)S(1)} %get-tuple-element.49), channel_id=1, source_target_pairs={{0,6},{1,7},{2,4},{3,5},{4,2},{5,3},{6,0},{7,1},{8,14},{9,15},{10,... | collective-permute-start | bytes 196616 | tf_op jit(solution)/shard_map/ppermute | solution.py:26
  39.3 0.0 collective-permute-start.17
  39.3 3.2 %collective-permute-start.18 = (bf16[128,256]{1,0:T(8,128)(2,1)S(1)}, bf16[128,256]{1,0:T(8,128)(2,1)S(1)}, u32[]{:S(2)}, u32[]{:S(2)}) collective-permute-start(bf16[128,256]{1,0:T(8,128)(2,1)S(1)} %get-tuple-element.50), channel_id=1, source_target_pairs={{0,2},{1,3},{2,0},{3,1},{4,6},{5,7},{6,4},{7,5},{8,10},{9,11},{10,... | collective-permute-start | bytes 196616 | tf_op jit(solution)/shard_map/ppermute | solution.py:26
  42.5 0.8 %add_convert_fusion = bf16[128,1024]{1,0:T(8,128)(2,1)} fusion(f32[128,1024]{1,0:T(8,128)S(1)} %get-tuple-element.41, f32[128,1024]{1,0:T(8,128)S(1)} %collective-permute-done.19), kind=kLoop, calls=%fused_computation.10 | loop fusion | flops 262144 | bytes 1310720 | tf_op jit(solution)/shard_map/convert_element_type | solution.py:247
  43.3 1.6 %collective-permute-done.16 = bf16[128,256]{1,0:T(8,128)(2,1)S(1)} collective-permute-done((bf16[128,256]{1,0:T(8,128)(2,1)S(1)}, bf16[128,256]{1,0:T(8,128)(2,1)S(1)}, u32[]{:S(2)}, u32[]{:S(2)}) %collective-permute-start.16) | collective-permute-done | bytes 65568 | tf_op jit(solution)/shard_map/ppermute | solution.py:26
  44.9 1.9 %collective-permute-done.17 = bf16[128,256]{1,0:T(8,128)(2,1)S(1)} collective-permute-done((bf16[128,256]{1,0:T(8,128)(2,1)S(1)}, bf16[128,256]{1,0:T(8,128)(2,1)S(1)}, u32[]{:S(2)}, u32[]{:S(2)}) %collective-permute-start.17) | collective-permute-done | bytes 65568 | tf_op jit(solution)/shard_map/ppermute | solution.py:26
  46.9 0.6 %collective-permute-start.20 = (bf16[128,256]{1,0:T(8,128)(2,1)S(1)}, bf16[128,256]{1,0:T(8,128)(2,1)S(1)}, u32[]{:S(2)}, u32[]{:S(2)}) collective-permute-start(bf16[128,256]{1,0:T(8,128)(2,1)S(1)} %fusion.17), channel_id=1, source_target_pairs={{0,24},{8,16},{16,8},{24,0},{1,25},{9,17},{17,9},{25,1},{2,26},{10... | collective-permute-start | bytes 196616 | tf_op jit(solution)/shard_map/ppermute | solution.py:26
  47.5 1.4 %collective-permute-start.21 = (bf16[128,256]{1,0:T(8,128)(2,1)S(1)}, bf16[128,256]{1,0:T(8,128)(2,1)S(1)}, u32[]{:S(2)}, u32[]{:S(2)}) collective-permute-start(bf16[128,256]{1,0:T(8,128)(2,1)S(1)} %fusion.17), channel_id=1, source_target_pairs={{0,16},{8,24},{16,0},{24,8},{1,17},{9,25},{17,1},{25,9},{2,18},{10... | collective-permute-start | bytes 196616 | tf_op jit(solution)/shard_map/ppermute | solution.py:26
  48.9 1.5 %collective-permute-start.22 = (bf16[128,256]{1,0:T(8,128)(2,1)S(1)}, bf16[128,256]{1,0:T(8,128)(2,1)S(1)}, u32[]{:S(2)}, u32[]{:S(2)}) collective-permute-start(bf16[128,256]{1,0:T(8,128)(2,1)S(1)} %fusion.17), channel_id=1, source_target_pairs={{0,8},{8,0},{16,24},{24,16},{1,9},{9,1},{17,25},{25,17},{2,10},{10... | collective-permute-start | bytes 196616 | tf_op jit(solution)/shard_map/ppermute | solution.py:26
  50.4 2.1 %collective-permute-done.20 = bf16[128,256]{1,0:T(8,128)(2,1)S(1)} collective-permute-done((bf16[128,256]{1,0:T(8,128)(2,1)S(1)}, bf16[128,256]{1,0:T(8,128)(2,1)S(1)}, u32[]{:S(2)}, u32[]{:S(2)}) %collective-permute-start.20) | collective-permute-done | bytes 65568 | tf_op jit(solution)/shard_map/ppermute | solution.py:26
  52.5 0.1 collective-permute-done.21
  52.6 0.6 %collective-permute-done.22 = bf16[128,256]{1,0:T(8,128)(2,1)S(1)} collective-permute-done((bf16[128,256]{1,0:T(8,128)(2,1)S(1)}, bf16[128,256]{1,0:T(8,128)(2,1)S(1)}, u32[]{:S(2)}, u32[]{:S(2)}) %collective-permute-start.22) | collective-permute-done | bytes 65568 | tf_op jit(solution)/shard_map/ppermute | solution.py:26
  53.2 0.8 %maximum_convert_fusion = f32[512,256]{1,0:T(8,128)} fusion(bf16[128,256]{1,0:T(8,128)(2,1)S(1)} %get-tuple-element.55, bf16[128,256]{1,0:T(8,128)(2,1)S(1)} %get-tuple-element.54, bf16[128,256]{1,0:T(8,128)(2,1)S(1)} %get-tuple-element.53, bf16[128,256]{1,0:T(8,128)(2,1)S(1)} %get-tuple-element.52), kind=kLoop, calls=%fused_computation.19 | loop fusion | flops 1048576 | bytes 786432 | tf_op jit(solution)/shard_map/concatenate | solution.py:272
  (22 shorter events, 0.2 us)
Async XLA Ops:
  0.6 7.9 %collective-permute-start = (bf16[128,1024]{1,0:T(8,128)(2,1)}, bf16[128,1024]{1,0:T(8,128)(2,1)S(1)}, u32[]{:S(2)}, u32[]{:S(2)}) collective-permute-start(bf16[128,1024]{1,0:T(8,128)(2,1)} %bitcast.40), channel_id=1, source_target_pairs={{0,1},{1,0},{2,3},{3,2},{4,5},{5,4},{6,7},{7,6},{8,9},{9,8},{10,11... | collective-permute-start | bytes 786440 | tf_op jit(solution)/shard_map/ppermute | solution.py:26
  1.1 7.4 %collective-permute-start.1 = (bf16[128,1024]{1,0:T(8,128)(2,1)}, bf16[128,1024]{1,0:T(8,128)(2,1)S(1)}, u32[]{:S(2)}, u32[]{:S(2)}) collective-permute-start(bf16[128,1024]{1,0:T(8,128)(2,1)} %bitcast.42), channel_id=1, source_target_pairs={{0,1},{1,0},{2,3},{3,2},{4,5},{5,4},{6,7},{7,6},{8,9},{9,8},{10,11... | collective-permute-start | bytes 786440 | tf_op jit(solution)/shard_map/ppermute | solution.py:26
  1.2 11.2 %collective-permute-start.4 = (bf16[128,256]{1,0:T(8,128)(2,1)}, bf16[128,256]{1,0:T(8,128)(2,1)S(1)}, u32[]{:S(2)}, u32[]{:S(2)}) collective-permute-start(bf16[128,256]{1,0:T(8,128)(2,1)} %bitcast.35), channel_id=1, source_target_pairs={{0,2},{1,3},{2,0},{3,1},{4,6},{5,7},{6,4},{7,5},{8,10},{9,11},{10,... | collective-permute-start | bytes 196616 | tf_op jit(solution)/shard_map/ppermute | solution.py:26
  4.2 8.2 %collective-permute-start.5 = (bf16[128,256]{1,0:T(8,128)(2,1)}, bf16[128,256]{1,0:T(8,128)(2,1)S(1)}, u32[]{:S(2)}, u32[]{:S(2)}) collective-permute-start(bf16[128,256]{1,0:T(8,128)(2,1)} %bitcast.36), channel_id=1, source_target_pairs={{0,4},{1,5},{2,6},{3,7},{4,0},{5,1},{6,2},{7,3},{8,12},{9,13},{10,... | collective-permute-start | bytes 196616 | tf_op jit(solution)/shard_map/ppermute | solution.py:26
  6.8 6.4 %collective-permute-start.6 = (bf16[128,256]{1,0:T(8,128)(2,1)}, bf16[128,256]{1,0:T(8,128)(2,1)S(1)}, u32[]{:S(2)}, u32[]{:S(2)}) collective-permute-start(bf16[128,256]{1,0:T(8,128)(2,1)} %bitcast.37), channel_id=1, source_target_pairs={{0,6},{1,7},{2,4},{3,5},{4,2},{5,3},{6,0},{7,1},{8,14},{9,15},{10,... | collective-permute-start | bytes 196616 | tf_op jit(solution)/shard_map/ppermute | solution.py:26
  6.8 4.6 %copy-start.1 = (bf16[1,1,128,1024]{3,2,1,0:T(8,128)(2,1)S(1)}, bf16[1,1,128,1024]{3,2,1,0:T(8,128)(2,1)}, u32[]{:S(2)}) copy-start(bf16[1,1,128,1024]{3,2,1,0:T(8,128)(2,1)} %param.6) | copy-start | bytes 786436
  6.8 4.6 %copy-start.2 = (bf16[1,1,128,1024]{3,2,1,0:T(8,128)(2,1)S(1)}, bf16[1,1,128,1024]{3,2,1,0:T(8,128)(2,1)}, u32[]{:S(2)}) copy-start(bf16[1,1,128,1024]{3,2,1,0:T(8,128)(2,1)} %param.8) | copy-start | bytes 786436
  6.8 4.6 %copy-start.3 = (s32[1,10]{1,0:T(1,128)S(1)}, s32[1,10]{1,0:T(1,128)}, u32[]{:S(2)}) copy-start(s32[1,10]{1,0:T(1,128)} %refs_0_.1) | copy-start | bytes 124
  8.7 4.5 %copy-start = (bf16[1,1,128,256]{3,2,1,0:T(8,128)(2,1)S(1)}, bf16[1,1,128,256]{3,2,1,0:T(8,128)(2,1)}, u32[]{:S(2)}) copy-start(bf16[1,1,128,256]{3,2,1,0:T(8,128)(2,1)} %param.7) | copy-start | bytes 196612
  8.7 9.4 %collective-permute-start.8 = (bf16[128,1024]{0,1:T(8,128)(2,1)S(1)}, bf16[128,1024]{0,1:T(8,128)(2,1)S(1)}, u32[]{:S(2)}, u32[]{:S(2)}) collective-permute-start(bf16[128,1024]{0,1:T(8,128)(2,1)S(1)} %bitcast.51), channel_id=1, source_target_pairs={{0,24},{8,16},{16,8},{24,0},{1,25},{9,17},{17,9},{25,1},{2,26},{10... | collective-permute-start | bytes 786440 | tf_op jit(solution)/shard_map/ppermute | solution.py:26
  15.0 1.3 %collective-permute-start.7 = (f32[8,2048]{1,0:T(8,128)S(1)}, f32[8,2048]{1,0:T(8,128)S(1)}, u32[]{:S(2)}, u32[]{:S(2)}) collective-permute-start(f32[8,2048]{1,0:T(8,128)S(1)} %get-tuple-element.32.refs_2_), channel_id=1, source_target_pairs={{0,1},{1,0},{2,3},{3,2},{4,5},{5,4},{6,7},{7,6},{8,9},{9,8},{10,11... | collective-permute-start | bytes 196616 | tf_op jit(solution)/shard_map/ppermute | solution.py:26
  18.1 7.5 %collective-permute-start.10 = (bf16[128,256]{1,0:T(8,128)(2,1)S(1)}, bf16[128,256]{1,0:T(8,128)(2,1)S(1)}, u32[]{:S(2)}, u32[]{:S(2)}) collective-permute-start(bf16[128,256]{1,0:T(8,128)(2,1)S(1)} %get-tuple-element.39), channel_id=1, source_target_pairs={{0,4},{1,5},{2,6},{3,7},{4,0},{5,1},{6,2},{7,3},{8,12},{9,13},{10,... | collective-permute-start | bytes 196616 | tf_op jit(solution)/shard_map/ppermute | solution.py:26
  19.9 5.7 %collective-permute-start.11 = (bf16[128,256]{1,0:T(8,128)(2,1)S(1)}, bf16[128,256]{1,0:T(8,128)(2,1)S(1)}, u32[]{:S(2)}, u32[]{:S(2)}) collective-permute-start(bf16[128,256]{1,0:T(8,128)(2,1)S(1)} %get-tuple-element.40), channel_id=1, source_target_pairs={{0,2},{1,3},{2,0},{3,1},{4,6},{5,7},{6,4},{7,5},{8,10},{9,11},{10,... | collective-permute-start | bytes 196616 | tf_op jit(solution)/shard_map/ppermute | solution.py:26
  21.5 6.1 %collective-permute-start.9 = (bf16[128,256]{1,0:T(8,128)(2,1)S(1)}, bf16[128,256]{1,0:T(8,128)(2,1)S(1)}, u32[]{:S(2)}, u32[]{:S(2)}) collective-permute-start(bf16[128,256]{1,0:T(8,128)(2,1)S(1)} %get-tuple-element.38), channel_id=1, source_target_pairs={{0,6},{1,7},{2,4},{3,5},{4,2},{5,3},{6,0},{7,1},{8,14},{9,15},{10,... | collective-permute-start | bytes 196616 | tf_op jit(solution)/shard_map/ppermute | solution.py:26
  22.5 8.7 %collective-permute-start.2 = (bf16[128,1024]{0,1:T(8,128)(2,1)S(1)}, bf16[128,1024]{0,1:T(8,128)(2,1)S(1)}, u32[]{:S(2)}, u32[]{:S(2)}) collective-permute-start(bf16[128,1024]{0,1:T(8,128)(2,1)S(1)} %bitcast.49), channel_id=1, source_target_pairs={{0,8},{8,0},{16,24},{24,16},{1,9},{9,1},{17,25},{25,17},{2,10},{10... | collective-permute-start | bytes 786440 | tf_op jit(solution)/shard_map/ppermute | solution.py:26
  24.0 8.6 %collective-permute-start.3 = (bf16[128,1024]{0,1:T(8,128)(2,1)S(1)}, bf16[128,1024]{0,1:T(8,128)(2,1)S(1)}, u32[]{:S(2)}, u32[]{:S(2)}) collective-permute-start(bf16[128,1024]{0,1:T(8,128)(2,1)S(1)} %bitcast.48), channel_id=1, source_target_pairs={{0,16},{8,24},{16,0},{24,8},{1,17},{9,25},{17,1},{25,9},{2,18},{10... | collective-permute-start | bytes 786440 | tf_op jit(solution)/shard_map/ppermute | solution.py:26
  27.6 8.6 %copy-start.4 = (bf16[128,256]{1,0:T(8,128)(2,1)}, bf16[128,256]{1,0:T(8,128)(2,1)S(1)}, u32[]{:S(2)}) copy-start(bf16[128,256]{1,0:T(8,128)(2,1)S(1)} %add_convert_fusion.1) | copy-start | bytes 196612
  27.7 5.0 %collective-permute-start.12 = (bf16[128,256]{1,0:T(8,128)(2,1)S(1)}, bf16[128,256]{1,0:T(8,128)(2,1)S(1)}, u32[]{:S(2)}, u32[]{:S(2)}) collective-permute-start(bf16[128,256]{1,0:T(8,128)(2,1)S(1)} %add_convert_fusion.1), channel_id=1, source_target_pairs={{0,8},{8,0},{16,24},{24,16},{1,9},{9,1},{17,25},{25,17},{2,10},{10... | collective-permute-start | bytes 196616 | tf_op jit(solution)/shard_map/ppermute | solution.py:26
  29.2 4.3 %collective-permute-start.13 = (bf16[128,256]{1,0:T(8,128)(2,1)S(1)}, bf16[128,256]{1,0:T(8,128)(2,1)S(1)}, u32[]{:S(2)}, u32[]{:S(2)}) collective-permute-start(bf16[128,256]{1,0:T(8,128)(2,1)S(1)} %add_convert_fusion.1), channel_id=1, source_target_pairs={{0,16},{8,24},{16,0},{24,8},{1,17},{9,25},{17,1},{25,9},{2,18},{10... | collective-permute-start | bytes 196616 | tf_op jit(solution)/shard_map/ppermute | solution.py:26
  30.7 5.2 %collective-permute-start.14 = (bf16[128,256]{1,0:T(8,128)(2,1)S(1)}, bf16[128,256]{1,0:T(8,128)(2,1)S(1)}, u32[]{:S(2)}, u32[]{:S(2)}) collective-permute-start(bf16[128,256]{1,0:T(8,128)(2,1)S(1)} %add_convert_fusion.1), channel_id=1, source_target_pairs={{0,24},{8,16},{16,8},{24,0},{1,25},{9,17},{17,9},{25,1},{2,26},{10... | collective-permute-start | bytes 196616 | tf_op jit(solution)/shard_map/ppermute | solution.py:26
  36.3 1.6 %collective-permute-start.15 = (bf16[4,128,256]{2,1,0:T(8,128)(2,1)S(1)}, bf16[4,128,256]{2,1,0:T(8,128)(2,1)S(1)}, u32[]{:S(2)}, u32[]{:S(2)}) collective-permute-start(bf16[4,128,256]{2,1,0:T(8,128)(2,1)S(1)} %fusion.7), channel_id=1, source_target_pairs={{0,1},{1,0},{2,3},{3,2},{4,5},{5,4},{6,7},{7,6},{8,9},{9,8},{10,11... | collective-permute-start | bytes 786440 | tf_op jit(solution)/shard_map/ppermute | solution.py:26
  36.4 6.1 %collective-permute-start.19 = (f32[128,1024]{1,0:T(8,128)S(1)}, f32[128,1024]{1,0:T(8,128)S(1)}, u32[]{:S(2)}, u32[]{:S(2)}) collective-permute-start(f32[128,1024]{1,0:T(8,128)S(1)} %get-tuple-element.42), channel_id=1, source_target_pairs={{0,1},{1,0},{2,3},{3,2},{4,5},{5,4},{6,7},{7,6},{8,9},{9,8},{10,11... | collective-permute-start | bytes 1572872 | tf_op jit(solution)/shard_map/ppermute | solution.py:26
  38.0 6.9 %collective-permute-start.16 = (bf16[128,256]{1,0:T(8,128)(2,1)S(1)}, bf16[128,256]{1,0:T(8,128)(2,1)S(1)}, u32[]{:S(2)}, u32[]{:S(2)}) collective-permute-start(bf16[128,256]{1,0:T(8,128)(2,1)S(1)} %get-tuple-element.49), channel_id=1, source_target_pairs={{0,6},{1,7},{2,4},{3,5},{4,2},{5,3},{6,0},{7,1},{8,14},{9,15},{10,... | collective-permute-start | bytes 196616 | tf_op jit(solution)/shard_map/ppermute | solution.py:26
  39.3 7.6 %collective-permute-start.17 = (bf16[128,256]{1,0:T(8,128)(2,1)S(1)}, bf16[128,256]{1,0:T(8,128)(2,1)S(1)}, u32[]{:S(2)}, u32[]{:S(2)}) collective-permute-start(bf16[128,256]{1,0:T(8,128)(2,1)S(1)} %get-tuple-element.51), channel_id=1, source_target_pairs={{0,4},{1,5},{2,6},{3,7},{4,0},{5,1},{6,2},{7,3},{8,12},{9,13},{10,... | collective-permute-start | bytes 196616 | tf_op jit(solution)/shard_map/ppermute | solution.py:26
  39.3 7.5 %collective-permute-start.18 = (bf16[128,256]{1,0:T(8,128)(2,1)S(1)}, bf16[128,256]{1,0:T(8,128)(2,1)S(1)}, u32[]{:S(2)}, u32[]{:S(2)}) collective-permute-start(bf16[128,256]{1,0:T(8,128)(2,1)S(1)} %get-tuple-element.50), channel_id=1, source_target_pairs={{0,2},{1,3},{2,0},{3,1},{4,6},{5,7},{6,4},{7,5},{8,10},{9,11},{10,... | collective-permute-start | bytes 196616 | tf_op jit(solution)/shard_map/ppermute | solution.py:26
  46.9 5.7 %collective-permute-start.20 = (bf16[128,256]{1,0:T(8,128)(2,1)S(1)}, bf16[128,256]{1,0:T(8,128)(2,1)S(1)}, u32[]{:S(2)}, u32[]{:S(2)}) collective-permute-start(bf16[128,256]{1,0:T(8,128)(2,1)S(1)} %fusion.17), channel_id=1, source_target_pairs={{0,24},{8,16},{16,8},{24,0},{1,25},{9,17},{17,9},{25,1},{2,26},{10... | collective-permute-start | bytes 196616 | tf_op jit(solution)/shard_map/ppermute | solution.py:26
  47.5 5.1 %collective-permute-start.21 = (bf16[128,256]{1,0:T(8,128)(2,1)S(1)}, bf16[128,256]{1,0:T(8,128)(2,1)S(1)}, u32[]{:S(2)}, u32[]{:S(2)}) collective-permute-start(bf16[128,256]{1,0:T(8,128)(2,1)S(1)} %fusion.17), channel_id=1, source_target_pairs={{0,16},{8,24},{16,0},{24,8},{1,17},{9,25},{17,1},{25,9},{2,18},{10... | collective-permute-start | bytes 196616 | tf_op jit(solution)/shard_map/ppermute | solution.py:26
  48.9 4.3 %collective-permute-start.22 = (bf16[128,256]{1,0:T(8,128)(2,1)S(1)}, bf16[128,256]{1,0:T(8,128)(2,1)S(1)}, u32[]{:S(2)}, u32[]{:S(2)}) collective-permute-start(bf16[128,256]{1,0:T(8,128)(2,1)S(1)} %fusion.17), channel_id=1, source_target_pairs={{0,8},{8,0},{16,24},{24,16},{1,9},{9,1},{17,25},{25,17},{2,10},{10... | collective-permute-start | bytes 196616 | tf_op jit(solution)/shard_map/ppermute | solution.py:26

commit v6 on v5

--- a/solution.py
+++ b/solution.py
@@ -73,18 +73,18 @@
     bias, q_rows, do_rows, e_ref, d_ref, stat_ref = refs[half:]
     heads = q_rows.shape[0] // (2 * local)
     coef = SCALE * LOG2E
-    width = 4 * local
+    width = 8 * local
     for b in range(2):
-        for group in range(heads // 4):
-            first = b * heads + 4 * group
-            cols = slice(first * local, (first + 4) * local)
+        for group in range(heads // 8):
+            first = b * heads + 8 * group
+            cols = slice(first * local, (first + 8) * local)
             q2 = q_rows[cols, :]
             do2 = do_rows[cols, :]
             top = jnp.full((8, width), NEG, jnp.float32)
             for k in range(half):
                 rows = slice(k * local, (k + 1) * local)
                 add = bias[b, rows, :]
-                x = dot(kv_refs[k][:, :HD], q2, NT) + jnp.concatenate([add] * 4, axis=1)
+                x = dot(kv_refs[k][:, :HD], q2, NT) + jnp.concatenate([add] * 8, axis=1)
                 e_ref[rows, cols] = x
                 top = jnp.maximum(top, jnp.max(fold(x), axis=0))
             top = jnp.max(top, axis=0, keepdims=True) * coef
@@ -113,7 +113,7 @@
     columns = e_ref.shape[1]
     heads = columns // (2 * local)
     side = columns // 2
-    width = 2 * local
+    width = 4 * local
 
     for k in range(half):
         k_t[:, k * local : (k + 1) * local] = kv_refs[k][:, :HD].T

time: 54.2 us -> 54.1 us (level)
  no operation moved by 1% of the time
where the time goes in v6:
time: 54.1 us; the launch traced here: 54 us
  starting transfers between devices  28.6 us (53%)
  waiting for transfers between devices  16.1 us (30%)
  Pallas kernels  4.39 us (8%)
  local copies, waits for them, and re-layouts  1.9 us (4%)
  other arithmetic  1.73 us (3%)
  between operations  0.83 us (2%)
    ppermute x23, starting transfers between devices, swap(): return lax.ppermute(x, axis, [(i, i ^ mask) for i in range(size)])  28.6 us
    ppermute x23, waiting for transfers between devices, swap(): return lax.ppermute(x, axis, [(i, i ^ mask) for i in range(size)])  16.1 us
    pallas_call x1, Pallas kernels, attention(): pl.pallas_call(functools.partial(gradients_kernel, half, local), out_shap...  1.75 us
    unnamed x11, local copies, waits for them, and re-layouts  1.73 us
    pallas_call x1, Pallas kernels, attention(): pl.pallas_call(functools.partial(scores_kernel, half, local), out_shape=(...  1.7 us
  transfers between devices with their start and end apart: 23, of which 12 were waited for; matrix products, arithmetic and copies ran while one was open for 5% of the time, Pallas kernels for 8%

profile of v6, /device:TPU:0, one launch (start us, length us, event | category | flops | bytes accessed | tf_op | source)
XLA Modules:
  0.0 54.0 jit_solution(3295642592416378169)
XLA Ops:
  0.6 0.5 collective-permute-start
  1.1 0.1 collective-permute-start.1
  1.2 3.0 %collective-permute-start.4 = (bf16[128,256]{1,0:T(8,128)(2,1)}, bf16[128,256]{1,0:T(8,128)(2,1)S(1)}, u32[]{:S(2)}, u32[]{:S(2)}) collective-permute-start(bf16[128,256]{1,0:T(8,128)(2,1)} %bitcast.35), channel_id=1, source_target_pairs={{0,2},{1,3},{2,0},{3,1},{4,6},{5,7},{6,4},{7,5},{8,10},{9,11},{10,... | collective-permute-start | bytes 196616 | tf_op jit(solution)/shard_map/ppermute | solution.py:26
  4.2 2.6 %collective-permute-start.5 = (bf16[128,256]{1,0:T(8,128)(2,1)}, bf16[128,256]{1,0:T(8,128)(2,1)S(1)}, u32[]{:S(2)}, u32[]{:S(2)}) collective-permute-start(bf16[128,256]{1,0:T(8,128)(2,1)} %bitcast.36), channel_id=1, source_target_pairs={{0,4},{1,5},{2,6},{3,7},{4,0},{5,1},{6,2},{7,3},{8,12},{9,13},{10,... | collective-permute-start | bytes 196616 | tf_op jit(solution)/shard_map/ppermute | solution.py:26
  6.8 0.0 collective-permute-start.6
  6.8 1.7 %copy.10 = bf16[1,1,128,4096]{2,3,1,0:T(8,128)(2,1)S(1)} copy(bf16[1,1,128,4096]{3,2,1,0:T(8,128)(2,1)} %param.5) | data formatting | bytes 2097152 | tf_op args[0]
  8.6 0.0 collective-permute-done.refs_3_
  8.6 0.1 constant_dynamic-slice_fusion.3
  8.7 0.0 copy-start
  8.7 2.7 %collective-permute-start.8 = (bf16[128,1024]{0,1:T(8,128)(2,1)S(1)}, bf16[128,1024]{0,1:T(8,128)(2,1)S(1)}, u32[]{:S(2)}, u32[]{:S(2)}) collective-permute-start(bf16[128,1024]{0,1:T(8,128)(2,1)S(1)} %bitcast.51), channel_id=1, source_target_pairs={{0,24},{8,16},{16,8},{24,0},{1,25},{9,17},{17,9},{25,1},{2,26},{10... | collective-permute-start | bytes 786440 | tf_op jit(solution)/shard_map/ppermute | solution.py:26
  11.4 0.9 %shard_map.76 = (f32[2,512,128]{2,1,0:T(8,128)S(1)}, bf16[2048,128]{1,0:T(8,128)(2,1)S(1)}, bf16[2048,128]{1,0:T(8,128)(2,1)S(1)}) custom-call(s32[1,10]{1,0:T(1,128)S(1)} %copy-done.3, s32[1]{0:T(128)} %bitcast.8.refs_1_, bf16[128,1024]{1,0:T(8,128)(2,1)S(1)} %bitcast.41, bf16[128,1024]{1,0:T(8,128)(2,1)S(1)} %collective-permute-done.refs_3_, ...), custom_call_target="tpu_custom_call" | custom-call | flops 1000000000 | tf_op jit(solution)/shard_map/pallas_call | solution.py:162
  12.4 0.0 collective-permute-done.5.refs_2_.refs_8_
  12.4 0.8 %collective-permute-done.6.refs_3_.refs_9_ = bf16[128,256]{1,0:T(8,128)(2,1)S(1)} collective-permute-done((bf16[128,256]{1,0:T(8,128)(2,1)}, bf16[128,256]{1,0:T(8,128)(2,1)S(1)}, u32[]{:S(2)}, u32[]{:S(2)}) %collective-permute-start.6) | collective-permute-done | bytes 65568 | tf_op jit(solution)/shard_map/ppermute | solution.py:26
  13.2 1.7 %shard_map.77 = (f32[512,2048]{1,0:T(8,128)S(1)}, f32[512,2048]{1,0:T(8,128)S(1)}, f32[8,2048]{1,0:T(8,128)S(1)}) custom-call(bf16[128,256]{1,0:T(8,128)(2,1)S(1)} %bitcast.38, bf16[128,256]{1,0:T(8,128)(2,1)S(1)} %collective-permute-done.4.refs_1_.refs_7_, bf16[128,256]{1,0:T(8,128)(2,1)S(1)} %collective-permute-done.5.refs_2_.refs_8_, ...), custom_call_target="tpu_custom_call" | custom-call | flops 2000000000 | tf_op jit(solution)/shard_map/pallas_call | solution.py:174
  14.9 0.1 collective-permute-start.7
  15.0 1.2 %collective-permute-done.7.refs_3_ = f32[8,2048]{1,0:T(8,128)S(1)} collective-permute-done((f32[8,2048]{1,0:T(8,128)S(1)}, f32[8,2048]{1,0:T(8,128)S(1)}, u32[]{:S(2)}, u32[]{:S(2)}) %collective-permute-start.7) | collective-permute-done | bytes 65568 | tf_op jit(solution)/shard_map/ppermute | solution.py:26
  16.2 1.8 %shard_map.78 = (f32[128,1024]{1,0:T(8,128)S(1)}, f32[128,1024]{1,0:T(8,128)S(1)}, f32[128,256]{1,0:T(8,128)S(1)}, bf16[128,256]{1,0:T(8,128)(2,1)S(1)}, bf16[12...) custom-call(f32[512,2048]{1,0:T(8,128)S(1)} %get-tuple-element.30.refs_0_, ...), custom_call_target="tpu_custom_call" | custom-call | flops 2000000000 | tf_op jit(solution)/shard_map/pallas_call | solution.py:187
  18.0 1.8 %collective-permute-start.10 = (bf16[128,256]{1,0:T(8,128)(2,1)S(1)}, bf16[128,256]{1,0:T(8,128)(2,1)S(1)}, u32[]{:S(2)}, u32[]{:S(2)}) collective-permute-start(bf16[128,256]{1,0:T(8,128)(2,1)S(1)} %get-tuple-element.39), channel_id=1, source_target_pairs={{0,4},{1,5},{2,6},{3,7},{4,0},{5,1},{6,2},{7,3},{8,12},{9,13},{10,... | collective-permute-start | bytes 196616 | tf_op jit(solution)/shard_map/ppermute | solution.py:26
  19.8 1.7 %collective-permute-start.11 = (bf16[128,256]{1,0:T(8,128)(2,1)S(1)}, bf16[128,256]{1,0:T(8,128)(2,1)S(1)}, u32[]{:S(2)}, u32[]{:S(2)}) collective-permute-start(bf16[128,256]{1,0:T(8,128)(2,1)S(1)} %get-tuple-element.40), channel_id=1, source_target_pairs={{0,2},{1,3},{2,0},{3,1},{4,6},{5,7},{6,4},{7,5},{8,10},{9,11},{10,... | collective-permute-start | bytes 196616 | tf_op jit(solution)/shard_map/ppermute | solution.py:26
  21.5 1.0 %collective-permute-start.9 = (bf16[128,256]{1,0:T(8,128)(2,1)S(1)}, bf16[128,256]{1,0:T(8,128)(2,1)S(1)}, u32[]{:S(2)}, u32[]{:S(2)}) collective-permute-start(bf16[128,256]{1,0:T(8,128)(2,1)S(1)} %get-tuple-element.38), channel_id=1, source_target_pairs={{0,6},{1,7},{2,4},{3,5},{4,2},{5,3},{6,0},{7,1},{8,14},{9,15},{10,... | collective-permute-start | bytes 196616 | tf_op jit(solution)/shard_map/ppermute | solution.py:26
  22.5 1.5 %collective-permute-start.2 = (bf16[128,1024]{0,1:T(8,128)(2,1)S(1)}, bf16[128,1024]{0,1:T(8,128)(2,1)S(1)}, u32[]{:S(2)}, u32[]{:S(2)}) collective-permute-start(bf16[128,1024]{0,1:T(8,128)(2,1)S(1)} %bitcast.49), channel_id=1, source_target_pairs={{0,8},{8,0},{16,24},{24,16},{1,9},{9,1},{17,25},{25,17},{2,10},{10... | collective-permute-start | bytes 786440 | tf_op jit(solution)/shard_map/ppermute | solution.py:26
  23.9 1.5 %collective-permute-start.3 = (bf16[128,1024]{0,1:T(8,128)(2,1)S(1)}, bf16[128,1024]{0,1:T(8,128)(2,1)S(1)}, u32[]{:S(2)}, u32[]{:S(2)}) collective-permute-start(bf16[128,1024]{0,1:T(8,128)(2,1)S(1)} %bitcast.48), channel_id=1, source_target_pairs={{0,16},{8,24},{16,0},{24,8},{1,17},{9,25},{17,1},{25,9},{2,18},{10... | collective-permute-start | bytes 786440 | tf_op jit(solution)/shard_map/ppermute | solution.py:26
  25.5 2.1 %collective-permute-done.9 = bf16[128,256]{1,0:T(8,128)(2,1)S(1)} collective-permute-done((bf16[128,256]{1,0:T(8,128)(2,1)S(1)}, bf16[128,256]{1,0:T(8,128)(2,1)S(1)}, u32[]{:S(2)}, u32[]{:S(2)}) %collective-permute-start.9) | collective-permute-done | bytes 65568 | tf_op jit(solution)/shard_map/ppermute | solution.py:26
  27.6 0.0 copy-start.4
  27.6 1.6 %collective-permute-start.12 = (bf16[128,256]{1,0:T(8,128)(2,1)S(1)}, bf16[128,256]{1,0:T(8,128)(2,1)S(1)}, u32[]{:S(2)}, u32[]{:S(2)}) collective-permute-start(bf16[128,256]{1,0:T(8,128)(2,1)S(1)} %add_convert_fusion.1), channel_id=1, source_target_pairs={{0,8},{8,0},{16,24},{24,16},{1,9},{9,1},{17,25},{25,17},{2,10},{10... | collective-permute-start | bytes 196616 | tf_op jit(solution)/shard_map/ppermute | solution.py:26
  29.2 1.5 %collective-permute-start.13 = (bf16[128,256]{1,0:T(8,128)(2,1)S(1)}, bf16[128,256]{1,0:T(8,128)(2,1)S(1)}, u32[]{:S(2)}, u32[]{:S(2)}) collective-permute-start(bf16[128,256]{1,0:T(8,128)(2,1)S(1)} %add_convert_fusion.1), channel_id=1, source_target_pairs={{0,16},{8,24},{16,0},{24,8},{1,17},{9,25},{17,1},{25,9},{2,18},{10... | collective-permute-start | bytes 196616 | tf_op jit(solution)/shard_map/ppermute | solution.py:26
  30.7 0.5 collective-permute-start.14
  31.2 1.4 %collective-permute-done.3 = bf16[128,1024]{0,1:T(8,128)(2,1)S(1)} collective-permute-done((bf16[128,1024]{0,1:T(8,128)(2,1)S(1)}, bf16[128,1024]{0,1:T(8,128)(2,1)S(1)}, u32[]{:S(2)}, u32[]{:S(2)}) %collective-permute-start.3) | collective-permute-done | bytes 262176 | tf_op jit(solution)/shard_map/ppermute | solution.py:26
  32.6 0.8 %collective-permute-done.13 = bf16[128,256]{1,0:T(8,128)(2,1)S(1)} collective-permute-done((bf16[128,256]{1,0:T(8,128)(2,1)S(1)}, bf16[128,256]{1,0:T(8,128)(2,1)S(1)}, u32[]{:S(2)}, u32[]{:S(2)}) %collective-permute-start.13) | collective-permute-done | bytes 65568 | tf_op jit(solution)/shard_map/ppermute | solution.py:26
  33.4 2.4 %collective-permute-done.14 = bf16[128,256]{1,0:T(8,128)(2,1)S(1)} collective-permute-done((bf16[128,256]{1,0:T(8,128)(2,1)S(1)}, bf16[128,256]{1,0:T(8,128)(2,1)S(1)}, u32[]{:S(2)}, u32[]{:S(2)}) %collective-permute-start.14) | collective-permute-done | bytes 65568 | tf_op jit(solution)/shard_map/ppermute | solution.py:26
  35.9 0.4 convolution_multiply_fusion
  36.3 0.1 collective-permute-start.15
  36.4 0.5 collective-permute-start.19
  36.9 1.0 %collective-permute-done.15 = bf16[4,128,256]{2,1,0:T(8,128)(2,1)S(1)} collective-permute-done((bf16[4,128,256]{2,1,0:T(8,128)(2,1)S(1)}, bf16[4,128,256]{2,1,0:T(8,128)(2,1)S(1)}, u32[]{:S(2)}, u32[]{:S(2)}) %collective-permute-start.15) | collective-permute-done | bytes 262176 | tf_op jit(solution)/shard_map/ppermute | solution.py:26
  37.9 0.1 bitcast_add_fusion
  38.0 1.1 %collective-permute-start.16 = (bf16[128,256]{1,0:T(8,128)(2,1)S(1)}, bf16[128,256]{1,0:T(8,128)(2,1)S(1)}, u32[]{:S(2)}, u32[]{:S(2)}) collective-permute-start(bf16[128,256]{1,0:T(8,128)(2,1)S(1)} %get-tuple-element.49), channel_id=1, source_target_pairs={{0,6},{1,7},{2,4},{3,5},{4,2},{5,3},{6,0},{7,1},{8,14},{9,15},{10,... | collective-permute-start | bytes 196616 | tf_op jit(solution)/shard_map/ppermute | solution.py:26
  39.2 0.1 collective-permute-start.17
  39.2 3.3 %collective-permute-start.18 = (bf16[128,256]{1,0:T(8,128)(2,1)S(1)}, bf16[128,256]{1,0:T(8,128)(2,1)S(1)}, u32[]{:S(2)}, u32[]{:S(2)}) collective-permute-start(bf16[128,256]{1,0:T(8,128)(2,1)S(1)} %get-tuple-element.50), channel_id=1, source_target_pairs={{0,2},{1,3},{2,0},{3,1},{4,6},{5,7},{6,4},{7,5},{8,10},{9,11},{10,... | collective-permute-start | bytes 196616 | tf_op jit(solution)/shard_map/ppermute | solution.py:26
  42.5 0.8 %add_convert_fusion = bf16[128,1024]{1,0:T(8,128)(2,1)} fusion(f32[128,1024]{1,0:T(8,128)S(1)} %get-tuple-element.41, f32[128,1024]{1,0:T(8,128)S(1)} %collective-permute-done.19), kind=kLoop, calls=%fused_computation.10 | loop fusion | flops 262144 | bytes 1310720 | tf_op jit(solution)/shard_map/convert_element_type | solution.py:247
  43.3 1.6 %collective-permute-done.16 = bf16[128,256]{1,0:T(8,128)(2,1)S(1)} collective-permute-done((bf16[128,256]{1,0:T(8,128)(2,1)S(1)}, bf16[128,256]{1,0:T(8,128)(2,1)S(1)}, u32[]{:S(2)}, u32[]{:S(2)}) %collective-permute-start.16) | collective-permute-done | bytes 65568 | tf_op jit(solution)/shard_map/ppermute | solution.py:26
  44.9 1.8 %collective-permute-done.17 = bf16[128,256]{1,0:T(8,128)(2,1)S(1)} collective-permute-done((bf16[128,256]{1,0:T(8,128)(2,1)S(1)}, bf16[128,256]{1,0:T(8,128)(2,1)S(1)}, u32[]{:S(2)}, u32[]{:S(2)}) %collective-permute-start.17) | collective-permute-done | bytes 65568 | tf_op jit(solution)/shard_map/ppermute | solution.py:26
  46.8 0.7 %collective-permute-start.20 = (bf16[128,256]{1,0:T(8,128)(2,1)S(1)}, bf16[128,256]{1,0:T(8,128)(2,1)S(1)}, u32[]{:S(2)}, u32[]{:S(2)}) collective-permute-start(bf16[128,256]{1,0:T(8,128)(2,1)S(1)} %fusion.17), channel_id=1, source_target_pairs={{0,24},{8,16},{16,8},{24,0},{1,25},{9,17},{17,9},{25,1},{2,26},{10... | collective-permute-start | bytes 196616 | tf_op jit(solution)/shard_map/ppermute | solution.py:26
  47.4 1.4 %collective-permute-start.21 = (bf16[128,256]{1,0:T(8,128)(2,1)S(1)}, bf16[128,256]{1,0:T(8,128)(2,1)S(1)}, u32[]{:S(2)}, u32[]{:S(2)}) collective-permute-start(bf16[128,256]{1,0:T(8,128)(2,1)S(1)} %fusion.17), channel_id=1, source_target_pairs={{0,16},{8,24},{16,0},{24,8},{1,17},{9,25},{17,1},{25,9},{2,18},{10... | collective-permute-start | bytes 196616 | tf_op jit(solution)/shard_map/ppermute | solution.py:26
  48.8 1.5 %collective-permute-start.22 = (bf16[128,256]{1,0:T(8,128)(2,1)S(1)}, bf16[128,256]{1,0:T(8,128)(2,1)S(1)}, u32[]{:S(2)}, u32[]{:S(2)}) collective-permute-start(bf16[128,256]{1,0:T(8,128)(2,1)S(1)} %fusion.17), channel_id=1, source_target_pairs={{0,8},{8,0},{16,24},{24,16},{1,9},{9,1},{17,25},{25,17},{2,10},{10... | collective-permute-start | bytes 196616 | tf_op jit(solution)/shard_map/ppermute | solution.py:26
  50.3 2.0 %collective-permute-done.20 = bf16[128,256]{1,0:T(8,128)(2,1)S(1)} collective-permute-done((bf16[128,256]{1,0:T(8,128)(2,1)S(1)}, bf16[128,256]{1,0:T(8,128)(2,1)S(1)}, u32[]{:S(2)}, u32[]{:S(2)}) %collective-permute-start.20) | collective-permute-done | bytes 65568 | tf_op jit(solution)/shard_map/ppermute | solution.py:26
  52.3 0.2 collective-permute-done.21
  52.5 0.6 %collective-permute-done.22 = bf16[128,256]{1,0:T(8,128)(2,1)S(1)} collective-permute-done((bf16[128,256]{1,0:T(8,128)(2,1)S(1)}, bf16[128,256]{1,0:T(8,128)(2,1)S(1)}, u32[]{:S(2)}, u32[]{:S(2)}) %collective-permute-start.22) | collective-permute-done | bytes 65568 | tf_op jit(solution)/shard_map/ppermute | solution.py:26
  53.1 0.8 %maximum_convert_fusion = f32[512,256]{1,0:T(8,128)} fusion(bf16[128,256]{1,0:T(8,128)(2,1)S(1)} %get-tuple-element.55, bf16[128,256]{1,0:T(8,128)(2,1)S(1)} %get-tuple-element.54, bf16[128,256]{1,0:T(8,128)(2,1)S(1)} %get-tuple-element.53, bf16[128,256]{1,0:T(8,128)(2,1)S(1)} %get-tuple-element.52), kind=kLoop, calls=%fused_computation.19 | loop fusion | flops 1048576 | bytes 786432 | tf_op jit(solution)/shard_map/concatenate | solution.py:272
  (22 shorter events, 0.2 us)
Async XLA Ops:
  0.6 7.9 %collective-permute-start = (bf16[128,1024]{1,0:T(8,128)(2,1)}, bf16[128,1024]{1,0:T(8,128)(2,1)S(1)}, u32[]{:S(2)}, u32[]{:S(2)}) collective-permute-start(bf16[128,1024]{1,0:T(8,128)(2,1)} %bitcast.40), channel_id=1, source_target_pairs={{0,1},{1,0},{2,3},{3,2},{4,5},{5,4},{6,7},{7,6},{8,9},{9,8},{10,11... | collective-permute-start | bytes 786440 | tf_op jit(solution)/shard_map/ppermute | solution.py:26
  1.1 7.4 %collective-permute-start.1 = (bf16[128,1024]{1,0:T(8,128)(2,1)}, bf16[128,1024]{1,0:T(8,128)(2,1)S(1)}, u32[]{:S(2)}, u32[]{:S(2)}) collective-permute-start(bf16[128,1024]{1,0:T(8,128)(2,1)} %bitcast.42), channel_id=1, source_target_pairs={{0,1},{1,0},{2,3},{3,2},{4,5},{5,4},{6,7},{7,6},{8,9},{9,8},{10,11... | collective-permute-start | bytes 786440 | tf_op jit(solution)/shard_map/ppermute | solution.py:26
  1.2 11.2 %collective-permute-start.4 = (bf16[128,256]{1,0:T(8,128)(2,1)}, bf16[128,256]{1,0:T(8,128)(2,1)S(1)}, u32[]{:S(2)}, u32[]{:S(2)}) collective-permute-start(bf16[128,256]{1,0:T(8,128)(2,1)} %bitcast.35), channel_id=1, source_target_pairs={{0,2},{1,3},{2,0},{3,1},{4,6},{5,7},{6,4},{7,5},{8,10},{9,11},{10,... | collective-permute-start | bytes 196616 | tf_op jit(solution)/shard_map/ppermute | solution.py:26
  4.2 8.2 %collective-permute-start.5 = (bf16[128,256]{1,0:T(8,128)(2,1)}, bf16[128,256]{1,0:T(8,128)(2,1)S(1)}, u32[]{:S(2)}, u32[]{:S(2)}) collective-permute-start(bf16[128,256]{1,0:T(8,128)(2,1)} %bitcast.36), channel_id=1, source_target_pairs={{0,4},{1,5},{2,6},{3,7},{4,0},{5,1},{6,2},{7,3},{8,12},{9,13},{10,... | collective-permute-start | bytes 196616 | tf_op jit(solution)/shard_map/ppermute | solution.py:26
  6.8 6.4 %collective-permute-start.6 = (bf16[128,256]{1,0:T(8,128)(2,1)}, bf16[128,256]{1,0:T(8,128)(2,1)S(1)}, u32[]{:S(2)}, u32[]{:S(2)}) collective-permute-start(bf16[128,256]{1,0:T(8,128)(2,1)} %bitcast.37), channel_id=1, source_target_pairs={{0,6},{1,7},{2,4},{3,5},{4,2},{5,3},{6,0},{7,1},{8,14},{9,15},{10,... | collective-permute-start | bytes 196616 | tf_op jit(solution)/shard_map/ppermute | solution.py:26
  6.8 4.6 %copy-start.1 = (bf16[1,1,128,1024]{3,2,1,0:T(8,128)(2,1)S(1)}, bf16[1,1,128,1024]{3,2,1,0:T(8,128)(2,1)}, u32[]{:S(2)}) copy-start(bf16[1,1,128,1024]{3,2,1,0:T(8,128)(2,1)} %param.6) | copy-start | bytes 786436
  6.8 4.6 %copy-start.2 = (bf16[1,1,128,1024]{3,2,1,0:T(8,128)(2,1)S(1)}, bf16[1,1,128,1024]{3,2,1,0:T(8,128)(2,1)}, u32[]{:S(2)}) copy-start(bf16[1,1,128,1024]{3,2,1,0:T(8,128)(2,1)} %param.8) | copy-start | bytes 786436
  6.8 4.6 %copy-start.3 = (s32[1,10]{1,0:T(1,128)S(1)}, s32[1,10]{1,0:T(1,128)}, u32[]{:S(2)}) copy-start(s32[1,10]{1,0:T(1,128)} %refs_0_.1) | copy-start | bytes 124
  8.7 4.5 %copy-start = (bf16[1,1,128,256]{3,2,1,0:T(8,128)(2,1)S(1)}, bf16[1,1,128,256]{3,2,1,0:T(8,128)(2,1)}, u32[]{:S(2)}) copy-start(bf16[1,1,128,256]{3,2,1,0:T(8,128)(2,1)} %param.7) | copy-start | bytes 196612
  8.7 9.3 %collective-permute-start.8 = (bf16[128,1024]{0,1:T(8,128)(2,1)S(1)}, bf16[128,1024]{0,1:T(8,128)(2,1)S(1)}, u32[]{:S(2)}, u32[]{:S(2)}) collective-permute-start(bf16[128,1024]{0,1:T(8,128)(2,1)S(1)} %bitcast.51), channel_id=1, source_target_pairs={{0,24},{8,16},{16,8},{24,0},{1,25},{9,17},{17,9},{25,1},{2,26},{10... | collective-permute-start | bytes 786440 | tf_op jit(solution)/shard_map/ppermute | solution.py:26
  14.9 1.3 %collective-permute-start.7 = (f32[8,2048]{1,0:T(8,128)S(1)}, f32[8,2048]{1,0:T(8,128)S(1)}, u32[]{:S(2)}, u32[]{:S(2)}) collective-permute-start(f32[8,2048]{1,0:T(8,128)S(1)} %get-tuple-element.32.refs_2_), channel_id=1, source_target_pairs={{0,1},{1,0},{2,3},{3,2},{4,5},{5,4},{6,7},{7,6},{8,9},{9,8},{10,11... | collective-permute-start | bytes 196616 | tf_op jit(solution)/shard_map/ppermute | solution.py:26
  18.0 7.5 %collective-permute-start.10 = (bf16[128,256]{1,0:T(8,128)(2,1)S(1)}, bf16[128,256]{1,0:T(8,128)(2,1)S(1)}, u32[]{:S(2)}, u32[]{:S(2)}) collective-permute-start(bf16[128,256]{1,0:T(8,128)(2,1)S(1)} %get-tuple-element.39), channel_id=1, source_target_pairs={{0,4},{1,5},{2,6},{3,7},{4,0},{5,1},{6,2},{7,3},{8,12},{9,13},{10,... | collective-permute-start | bytes 196616 | tf_op jit(solution)/shard_map/ppermute | solution.py:26
  19.8 5.7 %collective-permute-start.11 = (bf16[128,256]{1,0:T(8,128)(2,1)S(1)}, bf16[128,256]{1,0:T(8,128)(2,1)S(1)}, u32[]{:S(2)}, u32[]{:S(2)}) collective-permute-start(bf16[128,256]{1,0:T(8,128)(2,1)S(1)} %get-tuple-element.40), channel_id=1, source_target_pairs={{0,2},{1,3},{2,0},{3,1},{4,6},{5,7},{6,4},{7,5},{8,10},{9,11},{10,... | collective-permute-start | bytes 196616 | tf_op jit(solution)/shard_map/ppermute | solution.py:26
  21.5 6.1 %collective-permute-start.9 = (bf16[128,256]{1,0:T(8,128)(2,1)S(1)}, bf16[128,256]{1,0:T(8,128)(2,1)S(1)}, u32[]{:S(2)}, u32[]{:S(2)}) collective-permute-start(bf16[128,256]{1,0:T(8,128)(2,1)S(1)} %get-tuple-element.38), channel_id=1, source_target_pairs={{0,6},{1,7},{2,4},{3,5},{4,2},{5,3},{6,0},{7,1},{8,14},{9,15},{10,... | collective-permute-start | bytes 196616 | tf_op jit(solution)/shard_map/ppermute | solution.py:26
  22.5 8.7 %collective-permute-start.2 = (bf16[128,1024]{0,1:T(8,128)(2,1)S(1)}, bf16[128,1024]{0,1:T(8,128)(2,1)S(1)}, u32[]{:S(2)}, u32[]{:S(2)}) collective-permute-start(bf16[128,1024]{0,1:T(8,128)(2,1)S(1)} %bitcast.49), channel_id=1, source_target_pairs={{0,8},{8,0},{16,24},{24,16},{1,9},{9,1},{17,25},{25,17},{2,10},{10... | collective-permute-start | bytes 786440 | tf_op jit(solution)/shard_map/ppermute | solution.py:26
  23.9 8.7 %collective-permute-start.3 = (bf16[128,1024]{0,1:T(8,128)(2,1)S(1)}, bf16[128,1024]{0,1:T(8,128)(2,1)S(1)}, u32[]{:S(2)}, u32[]{:S(2)}) collective-permute-start(bf16[128,1024]{0,1:T(8,128)(2,1)S(1)} %bitcast.48), channel_id=1, source_target_pairs={{0,16},{8,24},{16,0},{24,8},{1,17},{9,25},{17,1},{25,9},{2,18},{10... | collective-permute-start | bytes 786440 | tf_op jit(solution)/shard_map/ppermute | solution.py:26
  27.6 8.7 %copy-start.4 = (bf16[128,256]{1,0:T(8,128)(2,1)}, bf16[128,256]{1,0:T(8,128)(2,1)S(1)}, u32[]{:S(2)}) copy-start(bf16[128,256]{1,0:T(8,128)(2,1)S(1)} %add_convert_fusion.1) | copy-start | bytes 196612
  27.6 5.0 %collective-permute-start.12 = (bf16[128,256]{1,0:T(8,128)(2,1)S(1)}, bf16[128,256]{1,0:T(8,128)(2,1)S(1)}, u32[]{:S(2)}, u32[]{:S(2)}) collective-permute-start(bf16[128,256]{1,0:T(8,128)(2,1)S(1)} %add_convert_fusion.1), channel_id=1, source_target_pairs={{0,8},{8,0},{16,24},{24,16},{1,9},{9,1},{17,25},{25,17},{2,10},{10... | collective-permute-start | bytes 196616 | tf_op jit(solution)/shard_map/ppermute | solution.py:26
  29.2 4.3 %collective-permute-start.13 = (bf16[128,256]{1,0:T(8,128)(2,1)S(1)}, bf16[128,256]{1,0:T(8,128)(2,1)S(1)}, u32[]{:S(2)}, u32[]{:S(2)}) collective-permute-start(bf16[128,256]{1,0:T(8,128)(2,1)S(1)} %add_convert_fusion.1), channel_id=1, source_target_pairs={{0,16},{8,24},{16,0},{24,8},{1,17},{9,25},{17,1},{25,9},{2,18},{10... | collective-permute-start | bytes 196616 | tf_op jit(solution)/shard_map/ppermute | solution.py:26
  30.7 5.2 %collective-permute-start.14 = (bf16[128,256]{1,0:T(8,128)(2,1)S(1)}, bf16[128,256]{1,0:T(8,128)(2,1)S(1)}, u32[]{:S(2)}, u32[]{:S(2)}) collective-permute-start(bf16[128,256]{1,0:T(8,128)(2,1)S(1)} %add_convert_fusion.1), channel_id=1, source_target_pairs={{0,24},{8,16},{16,8},{24,0},{1,25},{9,17},{17,9},{25,1},{2,26},{10... | collective-permute-start | bytes 196616 | tf_op jit(solution)/shard_map/ppermute | solution.py:26
  36.3 1.6 %collective-permute-start.15 = (bf16[4,128,256]{2,1,0:T(8,128)(2,1)S(1)}, bf16[4,128,256]{2,1,0:T(8,128)(2,1)S(1)}, u32[]{:S(2)}, u32[]{:S(2)}) collective-permute-start(bf16[4,128,256]{2,1,0:T(8,128)(2,1)S(1)} %fusion.7), channel_id=1, source_target_pairs={{0,1},{1,0},{2,3},{3,2},{4,5},{5,4},{6,7},{7,6},{8,9},{9,8},{10,11... | collective-permute-start | bytes 786440 | tf_op jit(solution)/shard_map/ppermute | solution.py:26
  36.4 6.1 %collective-permute-start.19 = (f32[128,1024]{1,0:T(8,128)S(1)}, f32[128,1024]{1,0:T(8,128)S(1)}, u32[]{:S(2)}, u32[]{:S(2)}) collective-permute-start(f32[128,1024]{1,0:T(8,128)S(1)} %get-tuple-element.42), channel_id=1, source_target_pairs={{0,1},{1,0},{2,3},{3,2},{4,5},{5,4},{6,7},{7,6},{8,9},{9,8},{10,11... | collective-permute-start | bytes 1572872 | tf_op jit(solution)/shard_map/ppermute | solution.py:26
  38.0 6.9 %collective-permute-start.16 = (bf16[128,256]{1,0:T(8,128)(2,1)S(1)}, bf16[128,256]{1,0:T(8,128)(2,1)S(1)}, u32[]{:S(2)}, u32[]{:S(2)}) collective-permute-start(bf16[128,256]{1,0:T(8,128)(2,1)S(1)} %get-tuple-element.49), channel_id=1, source_target_pairs={{0,6},{1,7},{2,4},{3,5},{4,2},{5,3},{6,0},{7,1},{8,14},{9,15},{10,... | collective-permute-start | bytes 196616 | tf_op jit(solution)/shard_map/ppermute | solution.py:26
  39.2 7.6 %collective-permute-start.17 = (bf16[128,256]{1,0:T(8,128)(2,1)S(1)}, bf16[128,256]{1,0:T(8,128)(2,1)S(1)}, u32[]{:S(2)}, u32[]{:S(2)}) collective-permute-start(bf16[128,256]{1,0:T(8,128)(2,1)S(1)} %get-tuple-element.51), channel_id=1, source_target_pairs={{0,4},{1,5},{2,6},{3,7},{4,0},{5,1},{6,2},{7,3},{8,12},{9,13},{10,... | collective-permute-start | bytes 196616 | tf_op jit(solution)/shard_map/ppermute | solution.py:26
  39.2 7.5 %collective-permute-start.18 = (bf16[128,256]{1,0:T(8,128)(2,1)S(1)}, bf16[128,256]{1,0:T(8,128)(2,1)S(1)}, u32[]{:S(2)}, u32[]{:S(2)}) collective-permute-start(bf16[128,256]{1,0:T(8,128)(2,1)S(1)} %get-tuple-element.50), channel_id=1, source_target_pairs={{0,2},{1,3},{2,0},{3,1},{4,6},{5,7},{6,4},{7,5},{8,10},{9,11},{10,... | collective-permute-start | bytes 196616 | tf_op jit(solution)/shard_map/ppermute | solution.py:26
  46.8 5.6 %collective-permute-start.20 = (bf16[128,256]{1,0:T(8,128)(2,1)S(1)}, bf16[128,256]{1,0:T(8,128)(2,1)S(1)}, u32[]{:S(2)}, u32[]{:S(2)}) collective-permute-start(bf16[128,256]{1,0:T(8,128)(2,1)S(1)} %fusion.17), channel_id=1, source_target_pairs={{0,24},{8,16},{16,8},{24,0},{1,25},{9,17},{17,9},{25,1},{2,26},{10... | collective-permute-start | bytes 196616 | tf_op jit(solution)/shard_map/ppermute | solution.py:26
  47.4 5.1 %collective-permute-start.21 = (bf16[128,256]{1,0:T(8,128)(2,1)S(1)}, bf16[128,256]{1,0:T(8,128)(2,1)S(1)}, u32[]{:S(2)}, u32[]{:S(2)}) collective-permute-start(bf16[128,256]{1,0:T(8,128)(2,1)S(1)} %fusion.17), channel_id=1, source_target_pairs={{0,16},{8,24},{16,0},{24,8},{1,17},{9,25},{17,1},{25,9},{2,18},{10... | collective-permute-start | bytes 196616 | tf_op jit(solution)/shard_map/ppermute | solution.py:26
  48.8 4.3 %collective-permute-start.22 = (bf16[128,256]{1,0:T(8,128)(2,1)S(1)}, bf16[128,256]{1,0:T(8,128)(2,1)S(1)}, u32[]{:S(2)}, u32[]{:S(2)}) collective-permute-start(bf16[128,256]{1,0:T(8,128)(2,1)S(1)} %fusion.17), channel_id=1, source_target_pairs={{0,8},{8,0},{16,24},{24,16},{1,9},{9,1},{17,25},{25,17},{2,10},{10... | collective-permute-start | bytes 196616 | tf_op jit(solution)/shard_map/ppermute | solution.py:26
